TPU v7x, 32 devices: a whole 2x2x4 slice. The times are simulated.
32 devices in a mesh: img: 8 (over y, x, core), blk: 4 (over z).
Axes of the slice: x: 2, y: 2, z: 4, core: 2. Of those that a mesh axis runs over, the one named last changes fastest.
Arguments:
- images_large: bfloat16 [32, 584, 768], P('img', 'blk'), may hold values from -6 to 6
- images_small: bfloat16 [64, 200, 768], P(('img', 'blk')), may hold values from -6 to 6
- cotan_large: bfloat16 [32, 584, 768], P('img', 'blk'), may hold values from -6 to 6
- cotan_small: bfloat16 [64, 200, 768], P(('img', 'blk')), may hold values from -6 to 6
- lengths_large: int32 [32], P('img'), may hold values from 192 to 577, as said below
- lengths_small: int32 [64], P(('img', 'blk')), may hold values from 65 to 197, as said below
- index_large: int32 [584, 584], replicated, may hold values from 0 to 2211
- index_small: int32 [200, 200], replicated, may hold values from 0 to 731
- attn_gain: bfloat16 [768], replicated, may hold values from 0.5 to 1.5
- attn_shift: bfloat16 [768], replicated, may hold values from -1.796875 to 1.796875
- qkv_weight: bfloat16 [768, 2304], replicated, may hold values from -0.21875 to 0.21875
- query_bias: bfloat16 [768], replicated, may hold values from -3 to 3
- value_bias: bfloat16 [768], replicated, may hold values from -0.8984375 to 0.8984375
- table_large: bfloat16 [2212, 12], replicated, may hold values from -4 to 4
- table_small: bfloat16 [732, 12], replicated, may hold values from -4 to 4
- proj_weight: bfloat16 [768, 768], replicated, may hold values from -1.25 to 1.25
- proj_bias: bfloat16 [768], replicated, may hold values from -1.796875 to 1.796875
- attn_scale: bfloat16 [768], replicated, may hold values from 0.5 to 1.5
- mlp_gain: bfloat16 [768], replicated, may hold values from 0.5 to 1.5
- mlp_shift: bfloat16 [768], replicated, may hold values from -1.796875 to 1.796875
- inner_weight: bfloat16 [768, 3072], replicated, may hold values from -0.21875 to 0.21875
- inner_bias: bfloat16 [3072], replicated, may hold values from -1.796875 to 1.796875
- outer_weight: bfloat16 [3072, 768], replicated, may hold values from -0.109375 to 0.109375
- outer_bias: bfloat16 [768], replicated, may hold values from -1.796875 to 1.796875
- mlp_scale: bfloat16 [768], replicated, may hold values from 0.5 to 1.5
Outputs:
- result_large: bfloat16 [32, 584, 768], P('img', 'blk')
- result_small: bfloat16 [64, 200, 768], P(('img', 'blk'))
- grad_large: bfloat16 [32, 584, 768], P('img', 'blk')
- grad_small: bfloat16 [64, 200, 768], P(('img', 'blk'))
- grad_attn_gain: float32 [768], P(('img', 'blk'))
- grad_attn_shift: float32 [768], P(('img', 'blk'))
- grad_qkv_weight: float32 [768, 2304], P(('img', 'blk'))
- grad_query_bias: float32 [768], P(('img', 'blk'))
- grad_value_bias: float32 [768], P(('img', 'blk'))
- grad_table_large: float32 [2212, 12], replicated
- grad_table_small: float32 [732, 12], replicated
- grad_proj_weight: float32 [768, 768], P(('img', 'blk'))
- grad_proj_bias: float32 [768], P(('img', 'blk'))
- grad_attn_scale: float32 [768], P(('img', 'blk'))
- grad_mlp_gain: float32 [768], P(('img', 'blk'))
- grad_mlp_shift: float32 [768], P(('img', 'blk'))
- grad_inner_weight: float32 [768, 3072], P(('img', 'blk'))
- grad_inner_bias: float32 [3072], P(('img', 'blk'))
- grad_outer_weight: float32 [3072, 768], P(('img', 'blk'))
- grad_outer_bias: float32 [768], P(('img', 'blk'))
- grad_mlp_scale: float32 [768], P(('img', 'blk'))
Inputs may be any that keep to these rules, and one draw needn't show every extreme that they name: `lengths_large`: valid tokens of each 384px image; positions at or past it are padding. Among the 4 images of each index of img one has 577 and one 577 // 3. `lengths_small`: valid tokens of each 224px image; positions at or past it are padding. Among the 2 images of each device one has 197 and one 197 // 3.
All inputs are finite; a program needn't handle non-finite values.
Results may differ from a plain program's by a relative error of at most 0.024.
Values may be sent and summed in bfloat16 or wider, within the bound.
No kernel may reach another device: no remote copies, remote signals or barrier semaphores. Data moves between devices by JAX's collectives and lax.ppermute only.
A program may use at most 320 MiB of HBM per device.

v0:
```python
import jax
import jax.numpy as jnp
from jax import lax
from jax.sharding import PartitionSpec as P

HEAD = 64


NEGATIVE = -1e30
EPSILON = 1e-06
HIGHEST = lax.Precision.HIGHEST


def layer_norm(values, gain, shift):
    center = values - jnp.mean(values, -1, keepdims=True)
    spread = jnp.mean(center * center, -1, keepdims=True)
    return center * lax.rsqrt(spread + EPSILON) * gain + shift


def exact_gelu(values):
    return jax.nn.gelu(values, approximate=False)


def lookup(table, index_block):
    table_codes = jnp.arange(table.shape[0], dtype=jnp.int32)

    def lookup_one_query(index_row):
        selector = (index_row[:, None] == table_codes[None, :]).astype(jnp.bfloat16)
        return jnp.dot(selector, table, preferred_element_type=jnp.float32)

    picked = lax.map(lookup_one_query, index_block, batch_size=8)
    return jnp.transpose(picked, (2, 0, 1))


def table_gradient(grad_full, index_block, table_rows):
    table_codes = jnp.arange(table_rows, dtype=jnp.int32)

    def table_one_query(item):
        index_row, grad_row = item
        selector = (index_row[:, None] == table_codes[None, :]).astype(jnp.float32)
        return jnp.dot(selector.T, grad_row, precision=HIGHEST, preferred_element_type=jnp.float32)

    partials = lax.map(
        table_one_query, (index_block, jnp.transpose(grad_full, (1, 2, 0))), batch_size=8
    )
    return jnp.sum(partials, 0)


def key_mask(lengths, first, count):
    places = first + jnp.arange(count, dtype=jnp.int32)
    return (places[None, :] < lengths[:, None])[:, None, None, :]


def block_scores(queries, key_piece, bias_rows, lengths, first):
    count = key_piece.shape[1]
    scores = jnp.einsum(
        "iqhe,ikhe->ihqk", queries, key_piece, preferred_element_type=jnp.float32
    ) * HEAD ** (-0.5)
    scores = scores + lax.dynamic_slice_in_dim(bias_rows, first, count, 2)[None]
    return (scores, key_mask(lengths, first, count))


def merge_heads(values):
    return jnp.transpose(values, (0, 2, 1, 3)).reshape(-1, values.shape[1] * values.shape[3])


def local_fold(pieces):

    def visit(step, state):
        return step(state, pieces, 0)

    return visit


def forward_attention(queries, bias_rows, lengths, visit):
    images, rows, heads, width = queries.shape

    def absorb(state, pieces, first):
        top, total, summed = state
        key_piece, value_piece = pieces
        scores, valid = block_scores(queries, key_piece, bias_rows, lengths, first)
        scores = jnp.where(valid, scores, NEGATIVE)
        new_top = jnp.maximum(top, jnp.max(scores, -1))
        weights = jnp.where(valid, jnp.exp(scores - new_top[..., None]), 0.0)
        factor = jnp.exp(top - new_top)
        total = total * factor + jnp.sum(weights, -1)
        update = jnp.einsum(
            "ihqk,ikhe->ihqe", weights, value_piece.astype(jnp.float32), precision=HIGHEST
        )
        return (new_top, total, summed * factor[..., None] + update)

    start_state = (
        jnp.full((images, heads, rows), NEGATIVE, jnp.float32),
        jnp.zeros((images, heads, rows), jnp.float32),
        jnp.zeros((images, heads, rows, width), jnp.float32),
    )
    top, total, summed = visit(absorb, start_state)
    return (summed / total[..., None], top + jnp.log(total))


def key_pass(queries, bias_rows, lengths, grad_out, inner, log_total, visit):
    images, rows, heads, width = queries.shape
    length = bias_rows.shape[2]
    grad_wide = grad_out.astype(jnp.float32)

    def collect(state, pieces, first):
        key_piece, value_piece = pieces
        scores, valid = block_scores(queries, key_piece, bias_rows, lengths, first)
        probs = jnp.where(valid, jnp.exp(scores - log_total[..., None]), 0.0)
        grad_probs = jnp.einsum(
            "iqhe,ikhe->ihqk", grad_out, value_piece, preferred_element_type=jnp.float32
        )
        grad_scores = (probs * (grad_probs - inner[..., None])).astype(jnp.bfloat16)
        grad_query = state[0] + jnp.einsum(
            "ihqk,ikhe->ihqe", grad_scores, key_piece, preferred_element_type=jnp.float32
        ) * HEAD ** (-0.5)
        bias_full = lax.dynamic_update_slice_in_dim(
            state[1], jnp.sum(grad_scores.astype(jnp.float32), 0), first, 2
        )
        key_part = jnp.einsum(
            "ihqk,iqhe->ikhe", grad_scores, queries, preferred_element_type=jnp.float32
        ) * HEAD ** (-0.5)
        value_part = jnp.einsum("ihqk,iqhe->ikhe", probs, grad_wide, precision=HIGHEST)
        key_full = lax.dynamic_update_slice_in_dim(state[2], key_part, first, 1)
        value_full = lax.dynamic_update_slice_in_dim(state[3], value_part, first, 1)
        return (grad_query, bias_full, key_full, value_full)

    start_state = (
        jnp.zeros((images, heads, rows, width), jnp.float32),
        jnp.zeros((heads, rows, length), jnp.float32),
    )
    start_state = start_state + (
        jnp.zeros((images, length, heads, width), jnp.float32),
        jnp.zeros((images, length, heads, width), jnp.float32),
    )
    return visit(collect, start_state)


def on_device(
    images_large,
    images_small,
    cotan_large,
    cotan_small,
    lengths_large,
    lengths_small,
    index_large,
    index_small,
    attn_gain,
    attn_shift,
    qkv_weight,
    query_bias,
    value_bias,
    table_large,
    table_small,
    proj_weight,
    proj_bias,
    attn_scale,
    mlp_gain,
    mlp_shift,
    inner_weight,
    inner_bias,
    outer_weight,
    outer_bias,
    mlp_scale,
):
    wide = jnp.float32
    narrow = jnp.bfloat16
    width = attn_gain.shape[0]
    heads = table_large.shape[1]
    large_count, large_rows = (images_large.shape[0], images_large.shape[1])
    small_count, small_rows = (images_small.shape[0], images_small.shape[1])
    split_at = large_count * large_rows
    first_key = lax.axis_index("blk") * large_rows
    flat = jnp.concatenate(
        [images_large.reshape(-1, width), images_small.reshape(-1, width)], 0
    ).astype(wide)
    normed, attn_norm_back = jax.vjp(
        layer_norm, flat, attn_gain.astype(wide), attn_shift.astype(wide)
    )
    normed_low = normed.astype(narrow)
    bias_vector = jnp.concatenate(
        [query_bias.astype(wide), jnp.zeros((width,), wide), value_bias.astype(wide)]
    )
    projected = (jnp.dot(normed_low, qkv_weight, preferred_element_type=wide) + bias_vector).astype(
        narrow
    )
    large_parts = projected[:split_at].reshape(large_count, large_rows, 3, heads, -1)
    large_query, large_key, large_value = (
        large_parts[:, :, 0],
        large_parts[:, :, 1],
        large_parts[:, :, 2],
    )
    large_index = lax.dynamic_slice_in_dim(index_large, first_key, large_rows, 0)
    large_bias = lookup(table_large, large_index)

    def forward_visit(step, state):
        return step(
            state,
            (
                lax.all_gather(large_key, "blk", axis=1, tiled=True),
                lax.all_gather(large_value, "blk", axis=1, tiled=True),
            ),
            jnp.int32(0),
        )

    def backward_visit(step, state):
        return step(
            state,
            (
                lax.all_gather(large_key, "blk", axis=1, tiled=True),
                lax.all_gather(large_value, "blk", axis=1, tiled=True),
            ),
            jnp.int32(0),
        )

    large_attended, large_log = forward_attention(
        large_query, large_bias, lengths_large, forward_visit
    )
    small_parts = projected[split_at:].reshape(small_count, small_rows, 3, heads, -1)
    small_query, small_key, small_value = (
        small_parts[:, :, 0],
        small_parts[:, :, 1],
        small_parts[:, :, 2],
    )
    small_bias = lookup(table_small, index_small)
    small_visit = local_fold((small_key, small_value))
    small_attended, small_log = forward_attention(
        small_query, small_bias, lengths_small, small_visit
    )
    attended_low = jnp.concatenate(
        [merge_heads(large_attended), merge_heads(small_attended)], 0
    ).astype(narrow)
    branch = jnp.dot(attended_low, proj_weight, preferred_element_type=wide) + proj_bias.astype(
        wide
    )
    middle = flat + attn_scale.astype(wide) * branch
    normed_mlp, mlp_norm_back = jax.vjp(
        layer_norm, middle, mlp_gain.astype(wide), mlp_shift.astype(wide)
    )
    normed_mlp_low = normed_mlp.astype(narrow)
    pre_act = jnp.dot(
        normed_mlp_low, inner_weight, preferred_element_type=wide
    ) + inner_bias.astype(wide)
    activated, gelu_back = jax.vjp(exact_gelu, pre_act)
    activated_low = activated.astype(narrow)
    outer = jnp.dot(activated_low, outer_weight, preferred_element_type=wide) + outer_bias.astype(
        wide
    )
    result_low = (middle + mlp_scale.astype(wide) * outer).astype(narrow)
    cotan = jnp.concatenate(
        [cotan_large.reshape(-1, width), cotan_small.reshape(-1, width)], 0
    ).astype(wide)
    grad_mlp_scale = jnp.sum(cotan * outer, 0)
    grad_outer = (mlp_scale.astype(wide) * cotan).astype(narrow)
    grad_outer_bias = jnp.sum(grad_outer.astype(wide), 0)
    grad_outer_weight = jnp.dot(activated_low.T, grad_outer, preferred_element_type=wide)
    grad_activated = jnp.dot(grad_outer, outer_weight.T, preferred_element_type=wide)
    grad_pre = gelu_back(grad_activated)[0].astype(narrow)
    grad_inner_bias = jnp.sum(grad_pre.astype(wide), 0)
    grad_inner_weight = jnp.dot(normed_mlp_low.T, grad_pre, preferred_element_type=wide)
    grad_normed_mlp = jnp.dot(grad_pre, inner_weight.T, preferred_element_type=wide)
    grad_middle_part, grad_mlp_gain, grad_mlp_shift = mlp_norm_back(grad_normed_mlp)
    grad_middle = cotan + grad_middle_part
    grad_attn_scale = jnp.sum(grad_middle * branch, 0)
    grad_branch = (attn_scale.astype(wide) * grad_middle).astype(narrow)
    grad_proj_bias = jnp.sum(grad_branch.astype(wide), 0)
    grad_proj_weight = jnp.dot(attended_low.T, grad_branch, preferred_element_type=wide)
    grad_attended = jnp.dot(grad_branch, proj_weight.T, preferred_element_type=wide).astype(narrow)
    large_grad_out = grad_attended[:split_at].reshape(large_count, large_rows, heads, -1)
    large_inner = jnp.einsum("iqhe,ihqe->ihq", large_grad_out.astype(wide), large_attended)
    large_grad_query, large_bias_full, key_full, value_full = key_pass(
        large_query,
        large_bias,
        lengths_large,
        large_grad_out,
        large_inner,
        large_log,
        backward_visit,
    )
    large_key_grad, large_value_grad = (
        lax.psum_scatter(
            key_full.astype(jnp.bfloat16), "blk", scatter_dimension=1, tiled=True
        ).astype(jnp.float32),
        lax.psum_scatter(
            value_full.astype(jnp.bfloat16), "blk", scatter_dimension=1, tiled=True
        ).astype(jnp.float32),
    )
    large_grads = jnp.stack(
        [jnp.transpose(large_grad_query, (0, 2, 1, 3)), large_key_grad, large_value_grad], 2
    ).reshape(split_at, 3 * width)
    large_table_grad = table_gradient(large_bias_full, large_index, table_large.shape[0])
    small_grad_out = grad_attended[split_at:].reshape(small_count, small_rows, heads, -1)
    small_inner = jnp.einsum("iqhe,ihqe->ihq", small_grad_out.astype(wide), small_attended)
    small_grad_query, small_bias_full, small_key_grad, small_value_grad = key_pass(
        small_query, small_bias, lengths_small, small_grad_out, small_inner, small_log, small_visit
    )
    small_grads = jnp.stack(
        [jnp.transpose(small_grad_query, (0, 2, 1, 3)), small_key_grad, small_value_grad], 2
    ).reshape(small_count * small_rows, 3 * width)
    small_table_grad = table_gradient(small_bias_full, index_small, table_small.shape[0])
    grad_projected = jnp.concatenate([large_grads, small_grads], 0).astype(narrow)
    grad_query_bias = jnp.sum(grad_projected[:, :width].astype(wide), 0)
    grad_value_bias = jnp.sum(grad_projected[:, 2 * width :].astype(wide), 0)
    grad_qkv_weight = jnp.dot(normed_low.T, grad_projected, preferred_element_type=wide)
    grad_normed = jnp.dot(grad_projected, qkv_weight.T, preferred_element_type=wide)
    grad_flat_part, grad_attn_gain, grad_attn_shift = attn_norm_back(grad_normed)
    grad_flat = (grad_middle + grad_flat_part).astype(narrow)
    summed = (
        lax.psum_scatter(grad_attn_gain, ("img", "blk"), scatter_dimension=0, tiled=True),
        lax.psum_scatter(grad_attn_shift, ("img", "blk"), scatter_dimension=0, tiled=True),
        lax.psum_scatter(grad_qkv_weight, ("img", "blk"), scatter_dimension=0, tiled=True),
        lax.psum_scatter(grad_query_bias, ("img", "blk"), scatter_dimension=0, tiled=True),
        lax.psum_scatter(grad_value_bias, ("img", "blk"), scatter_dimension=0, tiled=True),
        lax.psum_scatter(grad_proj_weight, ("img", "blk"), scatter_dimension=0, tiled=True),
        lax.psum_scatter(grad_proj_bias, ("img", "blk"), scatter_dimension=0, tiled=True),
        lax.psum_scatter(grad_attn_scale, ("img", "blk"), scatter_dimension=0, tiled=True),
        lax.psum_scatter(grad_mlp_gain, ("img", "blk"), scatter_dimension=0, tiled=True),
        lax.psum_scatter(grad_mlp_shift, ("img", "blk"), scatter_dimension=0, tiled=True),
        lax.psum_scatter(grad_inner_weight, ("img", "blk"), scatter_dimension=0, tiled=True),
        lax.psum_scatter(grad_inner_bias, ("img", "blk"), scatter_dimension=0, tiled=True),
        lax.psum_scatter(grad_outer_weight, ("img", "blk"), scatter_dimension=0, tiled=True),
        lax.psum_scatter(grad_outer_bias, ("img", "blk"), scatter_dimension=0, tiled=True),
        lax.psum_scatter(grad_mlp_scale, ("img", "blk"), scatter_dimension=0, tiled=True),
    )
    table_sum_large, table_sum_small = lax.psum(
        (large_table_grad, small_table_grad), ("img", "blk")
    )
    return (
        result_low[:split_at].reshape(large_count, large_rows, width),
        result_low[split_at:].reshape(small_count, small_rows, width),
        grad_flat[:split_at].reshape(large_count, large_rows, width),
        grad_flat[split_at:].reshape(small_count, small_rows, width),
        summed[0],
        summed[1],
        summed[2],
        summed[3],
        summed[4],
        table_sum_large,
        table_sum_small,
        summed[5],
        summed[6],
        summed[7],
        summed[8],
        summed[9],
        summed[10],
        summed[11],
        summed[12],
        summed[13],
        summed[14],
    )


def solution(mesh):
    return jax.shard_map(
        on_device,
        mesh=mesh,
        in_specs=(
            P("img", "blk", None),
            P(("img", "blk"), None, None),
            P("img", "blk", None),
            P(("img", "blk"), None, None),
            P("img"),
            P(("img", "blk")),
            P(),
            P(),
            P(),
            P(),
            P(),
            P(),
            P(),
            P(),
            P(),
            P(),
            P(),
            P(),
            P(),
            P(),
            P(),
            P(),
            P(),
            P(),
            P(),
        ),
        out_specs=(
            P("img", "blk", None),
            P(("img", "blk"), None, None),
            P("img", "blk", None),
            P(("img", "blk"), None, None),
            P(("img", "blk")),
            P(("img", "blk")),
            P(("img", "blk"), None),
            P(("img", "blk")),
            P(("img", "blk")),
            P(),
            P(),
            P(("img", "blk"), None),
            P(("img", "blk")),
            P(("img", "blk")),
            P(("img", "blk")),
            P(("img", "blk")),
            P(("img", "blk"), None),
            P(("img", "blk")),
            P(("img", "blk"), None),
            P(("img", "blk")),
            P(("img", "blk")),
        ),
        check_vma=False,
    )
```

profile of v0, /device:TPU:0, one launch (start us, length us, event | category | flops | bytes accessed | tf_op | source)
XLA Modules:
  0.0 2054.1 jit_solution(17428444932975263402)
XLA Ops:
  59.8 78.3 %while.45 = (s32[]{:T(128)}, f32[25,8,200,12]{2,3,1,0:T(8,128)}, s32[25,8,200]{2,1,0:T(8,128)}, bf16[732,12]{0,1:T(8,128)(2,1)}, s32[]{:T(128)}) while((s32[]{:T(128)}, f32[25,8,200,12]{2,3,1,0:T(8,128)}, s32[25,8,200]{2,1,0:T(8,128)}, bf16[732,12]{0,1:T(8,128)(2,1)}, s32[]{:T(128)}) %tuple.153), condition=%wide.region_7.8_spmd.clone, body=%wide.region_6.7_spmd.clone.sunk | while | flops 29280000 | bytes 174925 | solution.py:31
  178.9 189.3 %while.44 = (s32[]{:T(128)}, f32[18,8,584,12]{2,3,1,0:T(8,128)}, s32[18,8,584]{2,1,0:T(8,128)}, bf16[2212,12]{0,1:T(8,128)(2,1)}, s32[]{:T(128)}) while((s32[]{:T(128)}, f32[18,8,584,12]{2,3,1,0:T(8,128)}, s32[18,8,584]{2,1,0:T(8,128)}, bf16[2212,12]{0,1:T(8,128)(2,1)}, s32[]{:T(128)}) %tuple.120), condition=%wide.region_3.4_spmd.clone, body=%wide.region_2.3_spmd.clone.sunk | while | flops 258361600 | bytes 457549 | solution.py:31
  445.2 23.0 %fusion.75 = (bf16[4,146,12,64]{1,3,2,0:T(8,128)(2,1)S(1)}, f32[4,12,146,64]{2,3,1,0:T(8,128)}) fusion(f32[4,146,12]{1,2,0:T(8,128)} %bitcast_add_fusion.2, f32[4,146,12]{1,2,0:T(8,128)} %get-tuple-element.343, bf16[4,584,1,12,64]{1,4,3,0,2:T(8,128)(2,1)} %copy.140, f32[4,12,146,584]{3,2,1,0:T(8,128)} %get-tuple-element.357, f32[4,12,146]{2,1,0:T(8,128)} %copy-done.30, ...), kind=kOutput, calls=%fused_computation.120 | convolution fusion | flops 3164980992 | bytes 26828960 | tf_op jit(solution)/shard_map/ihqk,ikhe->ihqe/dot_general | solution.py:87
  480.8 35.0 %multiply_convert_fusion.1 = (bf16[984,3072]{1,0:T(8,128)(2,1)}, f32[984,3072]{1,0:T(8,128)}, f32[984,3072]{1,0:T(8,128)}) fusion(f32[3072]{0:T(1024)S(1)} %copy-done.56, bf16[768,3072]{1,0:T(8,128)(2,1)} %param.53, f32[984,768]{1,0:T(8,128)S(1)} %get-tuple-element.330, f32[768]{0:T(1024)S(1)} %convert_element_type.137, f32[768]{0:T(1024)S(1)} %convert_element_type.136, ...), kind=kOutput, calls=%fused_computation.49 | convolution fusion | flops 4846381056 | bytes 37996224 | tf_op jit(solution)/shard_map/dot_general | solution.py:241
  515.8 16.7 convert_reduce_fusion.1
  604.8 21.2 %convert_bitcast_fusion = bf16[4,584,12,64]{1,3,2,0:T(8,128)(2,1)} fusion(f32[4,12,146,584]{3,2,1,0:T(8,128)} %get-tuple-element.357, f32[4,12,146]{2,1,0:T(8,128)} %get-tuple-element.344, f32[12,146,584]{2,1,0:T(8,128)} %maximum_bitcast_fusion, pred[4,584]{1,0:T(4,128)(4,1)S(1)} %copy-done.34, bf16[4,146,12,64]{1,0,3,2:T(4,128)(2,1)} %reshape.289), kind=kOutput, calls=%fused_computation.111 | convolution fusion | flops 3161336832 | bytes 24978848 | tf_op jit(solution)/shard_map/ihqk,iqhe->ikhe/dot_general | solution.py:123
  630.4 17.2 convert_reduce_fusion
  668.1 293.2 %while.46 = (s32[]{:T(128)}, f32[18,8,2212,12]{2,3,1,0:T(8,128)}, s32[18,8,584]{2,1,0:T(8,128)}, f32[18,8,584,12]{2,3,1,0:T(8,128)}, s32[]{:T(128)}) while((s32[]{:T(128)}, f32[18,8,2212,12]{2,3,1,0:T(8,128)}, s32[18,8,584]{2,1,0:T(8,128)}, f32[18,8,584,12]{2,3,1,0:T(8,128)}, s32[]{:T(128)}) %tuple.152), condition=%wide.region_29.30_spmd.clone, body=%wide.region_28.29_spmd.clone.sunk | while | flops 1498497280 | bytes 1564489 | solution.py:43
  669.2 15.5 fusion.190
  685.5 15.5 fusion.190
  701.7 15.5 fusion.190
  718.0 15.5 fusion.190
  734.2 15.5 fusion.190
  750.5 15.5 fusion.190
  766.7 15.6 fusion.190
  783.1 15.6 fusion.190
  799.4 15.5 fusion.190
  831.8 15.6 fusion.190
  848.1 15.5 fusion.190
  864.4 15.5 fusion.190
  880.6 15.5 fusion.190
  896.9 15.5 fusion.190
  929.3 15.6 fusion.190
  945.6 15.5 fusion.190
  961.4 101.1 %while.47 = (s32[]{:T(128)}, f32[25,8,732,12]{2,3,1,0:T(8,128)}, s32[25,8,200]{2,1,0:T(8,128)}, f32[25,8,200,12]{2,3,1,0:T(8,128)}, s32[]{:T(128)}) while((s32[]{:T(128)}, f32[25,8,732,12]{2,3,1,0:T(8,128)}, s32[25,8,200]{2,1,0:T(8,128)}, f32[25,8,200,12]{2,3,1,0:T(8,128)}, s32[]{:T(128)}) %tuple.154), condition=%wide.region_34.35_spmd.clone, body=%wide.region_33.34_spmd.clone.sunk | while | flops 169824000 | bytes 544585 | solution.py:43
  1086.8 151.5 %all-reduce.23.cloned.1.call-done = (bf16[4,584,12,64]{1,3,2,0:T(8,128)(2,1)}, bf16[4,584,12,64]{1,3,2,0:T(8,128)(2,1)}) async-done(((bf16[4,584,12,64]{1,3,2,0:T(8,128)(2,1)}, bf16[4,584,12,64]{1,3,2,0:T(8,128)(2,1)}), (bf16[4,584,12,64]{1,3,2,0:T(8,128)(2,1)}, bf16[4,584,12,64]{1,3,2,0:T(8,128)(2,1)})) %all-reduce.23.cloned.1.call-update) | async-done | bytes 7176208
  1337.8 62.8 %all-reduce.21.cloned.1.call-done = (f32[768]{0:T(1024)}, f32[768]{0:T(1024)}, f32[768]{0:T(1024)}, f32[768]{0:T(1024)}, f32[732,12]{0,1:T(8,128)}, /*index=5*/f...) async-done(((f32[768]{0:T(1024)}, f32[768]{0:T(1024)}, f32[768]{0:T(1024)}, ...) | async-done | bytes 78160
  1414.4 114.7 %all-reduce.19.cloned.1.call-done = f32[2212,12]{0,1:T(8,128)} async-done(((f32[2212,12]{0,1:T(8,128)}), f32[2212,12]{0,1:T(8,128)}) %all-reduce.19.cloned.1.call-update) | async-done | bytes 106192 | tf_op jit(solution)/shard_map/psum | solution.py:325
  1529.2 107.6 %reduce-scatter.9.cloned.1.call-done = f32[24,768]{1,0:T(8,128)} async-done(((f32[768,768]{1,0:T(8,128)}), f32[24,768]{1,0:T(8,128)}) %reduce-scatter.9.cloned.1.call-update) | async-done | bytes 73744 | tf_op jit(solution)/shard_map/reduce_scatter | solution.py:314
  1636.8 140.9 %reduce-scatter.11.cloned.1.call-done = f32[24,3072]{1,0:T(8,128)} async-done(((f32[768,3072]{1,0:T(8,128)}), f32[24,3072]{1,0:T(8,128)}) %reduce-scatter.11.cloned.1.call-update) | async-done | bytes 294928 | tf_op jit(solution)/shard_map/reduce_scatter | solution.py:319
  1777.7 142.3 %reduce-scatter.13.cloned.1.call-done = f32[96,768]{1,0:T(8,128)} async-done(((f32[3072,768]{1,0:T(8,128)}), f32[96,768]{1,0:T(8,128)}) %reduce-scatter.13.cloned.1.call-update) | async-done | bytes 294928 | tf_op jit(solution)/shard_map/reduce_scatter | solution.py:321
  1919.9 124.5 %reduce-scatter.7.cloned.1.call-done = f32[24,2304]{1,0:T(8,128)} async-done(((f32[768,2304]{1,0:T(8,128)}), f32[24,2304]{1,0:T(8,128)}) %reduce-scatter.7.cloned.1.call-update) | async-done | bytes 221200 | tf_op jit(solution)/shard_map/reduce_scatter | solution.py:311
  (485 shorter events, 831.6 us)
Async XLA Ops:
  7.2 9.1 copy-start
  7.2 391.7 %all-gather.5.cloned.1.call-start = ((), (), s32[]{:S(2)}) async-start(), calls=%async_computation.9 | async-start | bytes 8970240 | tf_op jit(solution)/shard_map/all_gather | solution.py:200
  12.0 9.6 copy-start.59
  12.1 9.6 copy-start.45
  50.6 384.2 %all-gather.7.cloned.1.call-start = ((), (), s32[]{:S(2)}) async-start(), calls=%async_computation.10 | async-start | bytes 8970240 | tf_op jit(solution)/shard_map/all_gather | solution.py:201
  56.4 1181.9 %all-reduce.23.cloned.1.call-start = ((), (), s32[]{:S(2)}) async-start(), calls=%async_computation.12 | async-start | bytes 15728640
  143.0 225.2 %copy-start.54 = (pred[2,200]{1,0:T(4,128)(4,1)}, pred[2,200]{1,0:T(4,128)(4,1)S(1)}, u32[]{:S(2)}) copy-start(pred[2,200]{1,0:T(4,128)(4,1)S(1)} %iota_compare_fusion.32) | copy-start | bytes 1204
  391.6 150.9 %copy-start.38 = (f32[768]{0:T(1024)}, f32[768]{0:T(1024)S(1)}, u32[]{:S(2)}) copy-start(f32[768]{0:T(1024)S(1)} %convert_element_type.136) | copy-start | bytes 9220
  392.2 88.5 %copy-start.42 = (f32[768]{0:T(1024)}, f32[768]{0:T(1024)S(1)}, u32[]{:S(2)}) copy-start(f32[768]{0:T(1024)S(1)} %convert_element_type.137) | copy-start | bytes 9220
  392.3 152.1 %copy-start.61 = (f32[768]{0:T(1024)}, f32[768]{0:T(1024)S(1)}, u32[]{:S(2)}) copy-start(f32[768]{0:T(1024)S(1)} %convert_element_type.135) | copy-start | bytes 9220
  394.3 50.9 %copy-start.33 = (pred[4,584]{1,0:T(4,128)(4,1)}, pred[4,584]{1,0:T(4,128)(4,1)S(1)}, u32[]{:S(2)}) copy-start(pred[4,584]{1,0:T(4,128)(4,1)S(1)} %iota_compare_fusion.31) | copy-start | bytes 7012
  409.3 14.7 copy-start.1
  424.0 9.4 copy-start.30
  480.2 64.1 %copy-start.5 = (f32[984,768]{1,0:T(8,128)}, f32[984,768]{1,0:T(8,128)S(1)}, u32[]{:S(2)}) copy-start(f32[984,768]{1,0:T(8,128)S(1)} %get-tuple-element.330) | copy-start | bytes 9068548
  480.2 62.3 %copy-start.25 = (f32[984]{0:T(1024)}, f32[984]{0:T(1024)S(1)}, u32[]{:S(2)}) copy-start(f32[984]{0:T(1024)S(1)} %broadcast_multiply_fusion) | copy-start | bytes 11812
  480.8 61.8 %copy-start.28 = (f32[984]{0:T(1024)}, f32[984]{0:T(1024)S(1)}, u32[]{:S(2)}) copy-start(f32[984]{0:T(1024)S(1)} %fusion.129) | copy-start | bytes 11812
  532.5 11.9 copy-start.81
  544.3 12.0 copy-start.10
  544.3 12.0 copy-start.53
  544.9 11.5 copy-start.76
  604.8 25.5 %slice-start = ((s8[4669440]{0:T(1024)(128)(4,1)}), s8[4194304]{0:T(1024)(128)(4,1)S(1)}, s32[]{:S(2)}) async-start(s8[4669440]{0:T(1024)(128)(4,1)} %bitcast.226), calls=%async_computation.13 | async-start | bytes 8388608
  604.8 21.3 %copy-start.31 = (f32[4,12,146]{2,1,0:T(8,128)S(1)}, f32[4,12,146]{2,1,0:T(8,128)}, u32[]{:S(2)}) copy-start(f32[4,12,146]{2,1,0:T(8,128)} %get-tuple-element.342) | copy-start | bytes 84100
  604.8 25.5 %slice-start.1 = ((s8[4669440]{0:T(1024)(128)(4,1)}), s8[475136]{0:T(1024)(128)(4,1)S(1)}, s32[]{:S(2)}) async-start(s8[4669440]{0:T(1024)(128)(4,1)} %bitcast.226), calls=%async_computation.14 | async-start | bytes 950272
  961.3 439.2 %all-reduce.21.cloned.1.call-start = ((), (), s32[]{:S(2)}) async-start(), calls=%async_computation.11 | async-start | bytes 204800
  1250.2 9.1 copy-start.41
  1250.2 9.1 copy-start.46
  1273.4 255.8 %all-reduce.19.cloned.1.call-start = ((), (), s32[]{:S(2)}) async-start(), calls=%async_computation.5 | async-start | bytes 294912 | tf_op jit(solution)/shard_map/psum | solution.py:325
  1278.2 358.6 %reduce-scatter.9.cloned.1.call-start = ((), (), s32[]{:S(2)}) async-start(), calls=%async_computation.6 | async-start | bytes 2433024 | tf_op jit(solution)/shard_map/reduce_scatter | solution.py:314
  1283.1 494.6 %reduce-scatter.11.cloned.1.call-start = ((), (), s32[]{:S(2)}) async-start(), calls=%async_computation.7 | async-start | bytes 9732096 | tf_op jit(solution)/shard_map/reduce_scatter | solution.py:319
  1294.5 625.5 %reduce-scatter.13.cloned.1.call-start = ((), (), s32[]{:S(2)}) async-start(), calls=%async_computation.8 | async-start | bytes 9732096 | tf_op jit(solution)/shard_map/reduce_scatter | solution.py:321
  1305.0 739.4 %reduce-scatter.7.cloned.1.call-start = ((), (), s32[]{:S(2)}) async-start(), calls=%async_computation.4 | async-start | bytes 7299072 | tf_op jit(solution)/shard_map/reduce_scatter | solution.py:311
  1316.9 9.6 copy-start.44
  (63 other events, 277.5 us)
Sparse Core Ops, SparseCore 0:
  50.8 132.5 all-gather.4
  184.9 128.0 all-gather.6
  961.5 276.8 all-reduce.22
  1273.5 126.9 all-reduce.20
  1407.5 121.6 all-reduce.18
  1535.8 100.9 reduce-scatter.8
  1643.2 134.3 reduce-scatter.10
  1785.2 134.7 reduce-scatter.12
  1926.2 118.1 reduce-scatter.6
where the time goes:
time: 2070 us; the launch traced here: 2050 us
  matrix products  858 us (41%)
  waiting for transfers between devices  844 us (41%)
  local copies, waits for them, and re-layouts  271 us (13%)
  other arithmetic  64 us (3%)
    dot_general x44, matrix products, table_one_query(): jnp.dot(selector.T, grad_row, precision=HIGHEST, preferred_element_type=j...  368 us
    dot_general x44, matrix products, lookup_one_query(): return jnp.dot(selector, table, preferred_element_type=jnp.float32)  240 us
    unnamed x11, waiting for transfers between devices  214 us
    reduce_scatter x1, waiting for transfers between devices, on_device(): lax.psum_scatter(grad_outer_weight, ('img', 'blk'), scatter_dimension=0,...  142 us
    reduce_scatter x1, waiting for transfers between devices, on_device(): lax.psum_scatter(grad_inner_weight, ('img', 'blk'), scatter_dimension=0,...  141 us
    reduce_scatter x1, waiting for transfers between devices, on_device(): lax.psum_scatter(grad_qkv_weight, ('img', 'blk'), scatter_dimension=0, ti...  124 us
    psum x1, waiting for transfers between devices, on_device(): lax.psum((large_table_grad, small_table_grad), ('img', 'blk'))  115 us
    reduce_scatter x1, waiting for transfers between devices, on_device(): lax.psum_scatter(grad_proj_weight, ('img', 'blk'), scatter_dimension=0, t...  108 us
  transfers between devices with their start and end apart: 9, of which 7 were waited for; matrix products, arithmetic and copies ran while one was open for 28% of the time, Pallas kernels for 0%

commit v1 on v0

--- a/solution.py
+++ b/solution.py
@@ -1,6 +1,10 @@
+import functools
+
 import jax
 import jax.numpy as jnp
 from jax import lax
+from jax.experimental import pallas as pl
+from jax.experimental.pallas import tpu as pltpu
 from jax.sharding import PartitionSpec as P
 
 HEAD = 64
@@ -350,9 +354,831 @@
     )
 
 
+NT = (((1,), (1,)), ((), ()))
+TN = (((0,), (0,)), ((), ()))
+WIDE = jnp.float32
+NARROW = jnp.bfloat16
+LANES = 128
+FIXED = 4096.0
+MEGA = 1 << 20
+
+
+def round_up(count, step):
+    return -(-count // step) * step
+
+
+def params(limit, *names):
+    return pltpu.CompilerParams(vmem_limit_bytes=limit * MEGA, dimension_semantics=("arbitrary",))
+
+
+def whole(shape):
+    return pl.BlockSpec(shape, lambda i: (0,) * len(shape), pipeline_mode=pl.Buffered(1))
+
+
+def row_norm(values):
+    center = values - jnp.mean(values, -1, keepdims=True)
+    spread = jnp.mean(center * center, -1, keepdims=True)
+    inverse = lax.rsqrt(spread + EPSILON)
+    return center * inverse, inverse
+
+
+def norm_backward(grad, normal, inverse, gain):
+    scaled = grad * gain
+    first = jnp.mean(scaled, -1, keepdims=True)
+    second = jnp.mean(scaled * normal, -1, keepdims=True)
+    return inverse * (scaled - first - normal * second)
+
+
+def bias_kernel(pairs, groups, table_ref, index_ref, out_ref):
+    rows, lanes = index_ref.shape
+
+    def one_tile(tile, carry):
+        column = pl.multiple_of(tile * LANES, LANES)
+        for first in range(0, rows, 16):
+            found = []
+            for half in (0, 8):
+                index = index_ref[pl.ds(first + half, 8), pl.ds(column, LANES)]
+                low = lax.bitwise_and(index, LANES - 1)
+                high = lax.shift_right_logical(index, 7)
+                picked = [None] * pairs
+                for group in range(groups):
+                    here = high == group
+                    for pair in range(pairs):
+                        source = table_ref[group * pairs + pair]
+                        value = jnp.take_along_axis(source, low, axis=1)
+                        picked[pair] = value if group == 0 else jnp.where(here, value, picked[pair])
+                found.append(picked)
+            for pair in range(pairs):
+                both = jnp.concatenate([found[0][pair], found[1][pair]], 0)
+                upper = lax.shift_right_arithmetic(both, 16)
+                lower = lax.shift_right_arithmetic(lax.shift_left(both, 16), 16)
+                place = (pl.ds(first, 16), pl.ds(column, LANES))
+                out_ref[2 * pair, place[0], place[1]] = (upper.astype(WIDE) * (1 / FIXED)).astype(NARROW)
+                out_ref[2 * pair + 1, place[0], place[1]] = (lower.astype(WIDE) * (1 / FIXED)).astype(NARROW)
+        return carry
+
+    lax.fori_loop(0, lanes // LANES, one_tile, 0)
+
+
+def bias_lookup(table, index):
+    heads = table.shape[1]
+    pairs = heads // 2
+    groups = round_up(table.shape[0], LANES) // LANES
+    fixed = jnp.round(table.astype(WIDE) * FIXED).astype(jnp.int32)
+    fixed = jnp.pad(fixed, ((0, groups * LANES - table.shape[0]), (0, 0)))
+    packed = lax.bitwise_or(
+        lax.shift_left(fixed[:, 0::2], 16), lax.bitwise_and(fixed[:, 1::2], 65535)
+    )
+    packed = jnp.transpose(packed.reshape(groups, LANES, pairs), (0, 2, 1)).reshape(-1, 1, LANES)
+    packed = jnp.broadcast_to(packed, (groups * pairs, 8, LANES))
+    rows, lanes = index.shape
+    step = next(s for s in (32, 16) if rows % s == 0)
+    return pl.pallas_call(
+        functools.partial(bias_kernel, pairs, groups),
+        grid=(rows // step,),
+        in_specs=[whole((groups * pairs, 8, LANES)), pl.BlockSpec((step, lanes), lambda i: (i, 0))],
+        out_specs=pl.BlockSpec((heads, step, lanes), lambda i: (0, i, 0)),
+        out_shape=jax.ShapeDtypeStruct((heads, rows, lanes), NARROW),
+        compiler_params=params(32),
+        cost_estimate=pl.CostEstimate(
+            flops=rows * lanes * groups * pairs * 60, bytes_accessed=rows * lanes * heads * 2, transcendentals=0
+        ),
+        name="bias_lookup",
+    )(packed, index)
+
+
+def qkv_kernel(x_ref, gain_ref, shift_ref, weight_ref, bias_ref, h_ref, p_ref):
+    @pl.when(pl.program_id(0) == 0)
+    def _():
+        normal, _ = row_norm(x_ref[...].astype(WIDE))
+        h_ref[...] = (normal * gain_ref[...] + shift_ref[...]).astype(NARROW)
+
+    product = jnp.dot(h_ref[...], weight_ref[...], preferred_element_type=WIDE)
+    p_ref[...] = (product + bias_ref[...]).astype(NARROW)
+
+
+def qkv_forward(x, gain, shift, weight, bias):
+    tokens, width = x.shape
+    total = weight.shape[1]
+    return pl.pallas_call(
+        qkv_kernel,
+        grid=(total // width,),
+        in_specs=[
+            whole((tokens, width)),
+            whole((1, width)),
+            whole((1, width)),
+            pl.BlockSpec((width, width), lambda i: (0, i)),
+            pl.BlockSpec((1, width), lambda i: (0, i)),
+        ],
+        out_specs=[whole((tokens, width)), pl.BlockSpec((tokens, width), lambda i: (0, i))],
+        out_shape=[
+            jax.ShapeDtypeStruct((tokens, width), NARROW),
+            jax.ShapeDtypeStruct((tokens, total), NARROW),
+        ],
+        compiler_params=params(48),
+        cost_estimate=pl.CostEstimate(
+            flops=2 * tokens * width * total, bytes_accessed=2 * (tokens + width) * total, transcendentals=0
+        ),
+        name="qkv_forward",
+    )(x, gain, shift, weight, bias)
+
+
+def head_parts(first_half, value, other):
+    return jnp.where(first_half, value, other), jnp.where(first_half, other, value)
+
+
+def attention_forward_kernel(
+    images, q_ref, k_ref, v_ref, mask_ref, large_bias_ref, small_bias_ref, o_ref, large_p_ref, small_p_ref
+):
+    lane = lax.broadcasted_iota(jnp.int32, (1, LANES), 1)
+    first_half = lane < HEAD
+    for number, (start, rows) in enumerate(images):
+        place = slice(start, start + rows)
+        query = q_ref[place, :] * jnp.asarray(HEAD ** (-0.5), NARROW)
+        ones = jnp.where(lane % HEAD == 0, 1.0, 0.0).astype(NARROW)
+        ones = jnp.broadcast_to(ones, query.shape)
+        queries = head_parts(first_half, query, ones)
+        keys = head_parts(first_half, k_ref[place, :], mask_ref[place, :])
+        value = v_ref[place, :]
+        outs = []
+        for head in range(2):
+            bias = large_bias_ref[head, :, :rows] if number == 0 else small_bias_ref[head, :rows, :rows]
+            scores = lax.dot_general(keys[head], queries[head], NT, preferred_element_type=WIDE)
+            scores = scores + bias.astype(WIDE)
+            weights = jnp.exp(scores - jnp.max(scores, 0, keepdims=True))
+            probs = (weights * (1.0 / jnp.sum(weights, 0, keepdims=True))).astype(NARROW)
+            if number == 0:
+                large_p_ref[head] = probs
+            else:
+                small_p_ref[head, number - 1] = probs
+            outs.append(lax.dot_general(probs, value, TN, preferred_element_type=WIDE))
+        o_ref[place, :] = jnp.where(first_half, outs[0], outs[1]).astype(NARROW)
+
+
+def attention_forward(p, mask, large_bias, small_bias, images):
+    tokens = p.shape[0]
+    heads = large_bias.shape[0]
+    pairs = heads // 2
+    large, small, smalls = images[0][1], images[1][1], len(images) - 1
+    area = large * large + smalls * small * small
+
+    def column(offset):
+        return pl.BlockSpec((tokens, LANES), lambda i: (0, offset + i))
+
+    return pl.pallas_call(
+        functools.partial(attention_forward_kernel, images),
+        grid=(pairs,),
+        in_specs=[
+            column(0),
+            column(pairs),
+            column(2 * pairs),
+            whole((tokens, LANES)),
+            pl.BlockSpec((2,) + large_bias.shape[1:], lambda i: (i, 0, 0)),
+            pl.BlockSpec((2,) + small_bias.shape[1:], lambda i: (i, 0, 0)),
+        ],
+        out_specs=[
+            column(0),
+            pl.BlockSpec((2, large, large), lambda i: (i, 0, 0)),
+            pl.BlockSpec((2, smalls, small, small), lambda i: (i, 0, 0, 0)),
+        ],
+        out_shape=[
+            jax.ShapeDtypeStruct((tokens, heads * HEAD), NARROW),
+            jax.ShapeDtypeStruct((heads, large, large), NARROW),
+            jax.ShapeDtypeStruct((heads, smalls, small, small), NARROW),
+        ],
+        compiler_params=params(48),
+        cost_estimate=pl.CostEstimate(
+            flops=16 * heads * area * HEAD, bytes_accessed=4 * heads * area, transcendentals=heads * area
+        ),
+        name="attention_forward",
+    )(p, p, p, mask, large_bias, small_bias)
+
+
+def attention_backward_kernel(
+    images, q_ref, k_ref, v_ref, do_ref, o_ref, large_p_ref, small_p_ref, dp_ref, large_ds_ref, small_ds_ref
+):
+    lane = lax.broadcasted_iota(jnp.int32, (1, LANES), 1)
+    first_half = lane < HEAD
+    small_sum = [None, None]
+    scale = HEAD ** (-0.5)
+    for number, (start, rows) in enumerate(images):
+        place = slice(start, start + rows)
+        query = q_ref[place, :] * jnp.asarray(scale, NARROW)
+        key = k_ref[place, :]
+        value = v_ref[place, :]
+        grad = do_ref[place, :]
+        product = jnp.transpose(grad.astype(WIDE) * o_ref[place, :].astype(WIDE))
+        grads = head_parts(first_half, grad, jnp.zeros_like(grad))
+        parts = []
+        for head in range(2):
+            inner = jnp.sum(product[head * HEAD : (head + 1) * HEAD], 0, keepdims=True)
+            probs = large_p_ref[head] if number == 0 else small_p_ref[head, number - 1]
+            grad_probs = lax.dot_general(value, grads[head], NT, preferred_element_type=WIDE)
+            grad_scores = (probs.astype(WIDE) * (grad_probs - inner)).astype(NARROW)
+            if number == 0:
+                large_ds_ref[head, :, :rows] = grad_scores
+            elif small_sum[head] is None:
+                small_sum[head] = grad_scores.astype(WIDE)
+            else:
+                small_sum[head] = small_sum[head] + grad_scores.astype(WIDE)
+            parts.append(
+                (
+                    lax.dot_general(grad_scores, key, TN, preferred_element_type=WIDE) * scale,
+                    jnp.dot(grad_scores, query, preferred_element_type=WIDE),
+                    jnp.dot(probs, grad, preferred_element_type=WIDE),
+                )
+            )
+        for which in range(3):
+            dp_ref[which, place, :] = jnp.where(first_half, parts[0][which], parts[1][which]).astype(NARROW)
+    large = images[0][1]
+    small = images[1][1]
+    beyond = large_ds_ref.shape[2] - large
+    if beyond:
+        large_ds_ref[:, :, large:] = jnp.zeros((2, large, beyond), NARROW)
+    small_ds_ref[...] = jnp.zeros(small_ds_ref.shape, NARROW)
+    for head in range(2):
+        small_ds_ref[head, :small, :small] = small_sum[head].astype(NARROW)
+
+
+def attention_backward(p, grad_out, out, large_p, small_p, images, large_pad, small_pad):
+    tokens = p.shape[0]
+    heads = large_p.shape[0]
+    pairs = heads // 2
+    large, small, smalls = images[0][1], images[1][1], len(images) - 1
+    area = large * large + smalls * small * small
+
+    def column(offset):
+        return pl.BlockSpec((tokens, LANES), lambda i: (0, offset + i))
+
+    return pl.pallas_call(
+        functools.partial(attention_backward_kernel, images),
+        grid=(pairs,),
+        in_specs=[
+            column(0),
+            column(pairs),
+            column(2 * pairs),
+            column(0),
+            column(0),
+            pl.BlockSpec((2, large, large), lambda i: (i, 0, 0)),
+            pl.BlockSpec((2, smalls, small, small), lambda i: (i, 0, 0, 0)),
+        ],
+        out_specs=[
+            pl.BlockSpec((3, tokens, LANES), lambda i: (0, 0, i)),
+            pl.BlockSpec((2,) + large_pad, lambda i: (i, 0, 0)),
+            pl.BlockSpec((2,) + small_pad, lambda i: (i, 0, 0)),
+        ],
+        out_shape=[
+            jax.ShapeDtypeStruct((3, tokens, heads * HEAD), NARROW),
+            jax.ShapeDtypeStruct((heads,) + large_pad, NARROW),
+            jax.ShapeDtypeStruct((heads,) + small_pad, NARROW),
+        ],
+        compiler_params=params(48),
+        cost_estimate=pl.CostEstimate(
+            flops=32 * heads * area * HEAD, bytes_accessed=4 * heads * area, transcendentals=0
+        ),
+        name="attention_backward",
+    )(p, p, p, grad_out, out, large_p, small_p)
+
+
+def gelu_parts(value):
+    size = jnp.abs(value)
+    inverse = 1.0 / (1.0 + (0.3275911 * 0.7071067811865476) * size)
+    series = inverse * (
+        0.127414796
+        + inverse
+        * (-0.142248368 + inverse * (0.7107068705 + inverse * (-0.7265760135 + inverse * 0.5307027145)))
+    )
+    bell = jnp.exp(-0.5 * value * value)
+    tail = series * bell
+    share = jnp.where(value < 0, tail, 1.0 - tail)
+    return value * share, share + value * (bell * 0.3989422804014327)
+
+
+def mlp_kernel(
+    o_ref,
+    x_ref,
+    dy_ref,
+    proj_ref,
+    vector_ref,
+    inner_ref,
+    inner_bias_ref,
+    outer_ref,
+    result_ref,
+    dm_ref,
+    do_ref,
+    dinner_ref,
+    douter_ref,
+    dproj_ref,
+    dvector_ref,
+    dbias_ref,
+    r_ref,
+    g_ref,
+    dz_ref,
+    z_ref,
+    dg_ref,
+):
+    step = pl.program_id(0)
+    proj_bias, attn_scale, gain, shift, outer_bias, mlp_scale = (vector_ref[i : i + 1, :] for i in range(6))
+    tokens = x_ref.shape[0]
+    chunk = next(c for c in (128, 64, 32, 16) if tokens % c == 0)
+
+    @pl.when(step == 0)
+    def _():
+        r_ref[...] = jnp.dot(o_ref[...], proj_ref[...], preferred_element_type=WIDE) + proj_bias
+
+        @pl.loop(0, tokens // chunk)
+        def _(i):
+            rows = pl.ds(pl.multiple_of(i * chunk, chunk), chunk)
+            middle = x_ref[rows, :].astype(WIDE) + attn_scale * r_ref[rows, :]
+            normal, _ = row_norm(middle)
+            g_ref[rows, :] = (normal * gain + shift).astype(NARROW)
+            dz_ref[rows, :] = (mlp_scale * dy_ref[rows, :].astype(WIDE)).astype(NARROW)
+
+    pre = jnp.dot(g_ref[...], inner_ref[...], preferred_element_type=WIDE) + inner_bias_ref[...]
+    active, slope = gelu_parts(pre)
+    active = active.astype(NARROW)
+    dz = dz_ref[...]
+    dactive = lax.dot_general(dz, outer_ref[...], NT, preferred_element_type=WIDE)
+    dpre = (dactive * slope).astype(NARROW)
+    douter_ref[...] = lax.dot_general(active, dz, TN, preferred_element_type=WIDE).astype(NARROW)
+    dinner_ref[...] = lax.dot_general(g_ref[...], dpre, TN, preferred_element_type=WIDE).astype(NARROW)
+    dbias_ref[...] = jnp.sum(dpre.astype(WIDE), 0, keepdims=True)
+    z = jnp.dot(active, outer_ref[...], preferred_element_type=WIDE)
+    dg = lax.dot_general(dpre, inner_ref[...], NT, preferred_element_type=WIDE)
+
+    @pl.when(step == 0)
+    def _():
+        z_ref[...] = z
+        dg_ref[...] = dg
+
+    @pl.when(step > 0)
+    def _():
+        z_ref[...] += z
+        dg_ref[...] += dg
+
+    @pl.when(step == pl.num_programs(0) - 1)
+    def _():
+        dvector_ref[...] = jnp.zeros_like(dvector_ref)
+
+        @pl.loop(0, tokens // chunk)
+        def _(i):
+            rows = pl.ds(pl.multiple_of(i * chunk, chunk), chunk)
+            branch = r_ref[rows, :]
+            middle = x_ref[rows, :].astype(WIDE) + attn_scale * branch
+            normal, inverse = row_norm(middle)
+            outer = z_ref[rows, :] + outer_bias
+            dy = dy_ref[rows, :].astype(WIDE)
+            result_ref[rows, :] = (middle + mlp_scale * outer).astype(NARROW)
+            grad = dg_ref[rows, :]
+            dm = dy + norm_backward(grad, normal, inverse, gain)
+            dm_ref[rows, :] = dm
+            dr = (attn_scale * dm).astype(NARROW)
+            g_ref[rows, :] = dr
+            sums = [
+                dy * outer,
+                dz_ref[rows, :].astype(WIDE),
+                grad * normal,
+                grad,
+                dm * branch,
+                dr.astype(WIDE),
+            ]
+            for place, term in enumerate(sums):
+                dvector_ref[place : place + 1, :] += jnp.sum(term, 0, keepdims=True)
+
+        dr = g_ref[...]
+        dproj_ref[...] = lax.dot_general(o_ref[...], dr, TN, preferred_element_type=WIDE).astype(NARROW)
+        do_ref[...] = lax.dot_general(dr, proj_ref[...], NT, preferred_element_type=WIDE).astype(NARROW)
+
+
+def mlp_pass(out, x, dy, proj, vectors, inner, inner_bias, outer):
+    tokens, width = x.shape
+    hidden = inner.shape[1]
+    block = next(b for b in (512, 256, 128) if hidden % b == 0)
+    return pl.pallas_call(
+        mlp_kernel,
+        grid=(hidden // block,),
+        in_specs=[
+            whole((tokens, width)),
+            whole((tokens, width)),
+            whole((tokens, width)),
+            whole((width, width)),
+            whole((8, width)),
+            pl.BlockSpec((width, block), lambda i: (0, i)),
+            pl.BlockSpec((1, block), lambda i: (0, i)),
+            pl.BlockSpec((block, width), lambda i: (i, 0)),
+        ],
+        out_specs=[
+            whole((tokens, width)),
+            whole((tokens, width)),
+            whole((tokens, width)),
+            pl.BlockSpec((width, block), lambda i: (0, i)),
+            pl.BlockSpec((block, width), lambda i: (i, 0)),
+            whole((width, width)),
+            whole((8, width)),
+            pl.BlockSpec((1, block), lambda i: (0, i)),
+        ],
+        out_shape=[
+            jax.ShapeDtypeStruct((tokens, width), NARROW),
+            jax.ShapeDtypeStruct((tokens, width), WIDE),
+            jax.ShapeDtypeStruct((tokens, width), NARROW),
+            jax.ShapeDtypeStruct((width, hidden), NARROW),
+            jax.ShapeDtypeStruct((hidden, width), NARROW),
+            jax.ShapeDtypeStruct((width, width), NARROW),
+            jax.ShapeDtypeStruct((8, width), WIDE),
+            jax.ShapeDtypeStruct((1, hidden), WIDE),
+        ],
+        scratch_shapes=[
+            pltpu.VMEM((tokens, width), WIDE),
+            pltpu.VMEM((tokens, width), NARROW),
+            pltpu.VMEM((tokens, width), NARROW),
+            pltpu.VMEM((tokens, width), WIDE),
+            pltpu.VMEM((tokens, width), WIDE),
+        ],
+        compiler_params=params(60),
+        cost_estimate=pl.CostEstimate(
+            flops=12 * tokens * width * hidden, bytes_accessed=8 * hidden * width, transcendentals=tokens * hidden
+        ),
+        name="mlp_pass",
+    )(out, x, dy, proj, vectors, inner, inner_bias, outer)
+
+
+def qkv_backward_kernel(dp_ref, h_ref, x_ref, dm_ref, gain_ref, weight_ref, dweight_ref, dx_ref, dvector_ref, dh_ref):
+    step = pl.program_id(0)
+    grad = dp_ref[0]
+    dweight_ref[0] = lax.dot_general(h_ref[...], grad, TN, preferred_element_type=WIDE).astype(NARROW)
+    term = lax.dot_general(grad, weight_ref[...], NT, preferred_element_type=WIDE)
+    column_sum = jnp.sum(grad.astype(WIDE), 0, keepdims=True)
+    tokens = x_ref.shape[0]
+    chunk = next(c for c in (128, 64, 32, 16) if tokens % c == 0)
+
+    @pl.when(step == 0)
+    def _():
+        dvector_ref[...] = jnp.zeros_like(dvector_ref)
+        dh_ref[...] = term
+        dvector_ref[0:1, :] = column_sum
+
+    @pl.when(step > 0)
+    def _():
+        dh_ref[...] += term
+
+    @pl.when(step == pl.num_programs(0) - 1)
+    def _():
+        dvector_ref[1:2, :] = column_sum
+
+        @pl.loop(0, tokens // chunk)
+        def _(i):
+            rows = pl.ds(pl.multiple_of(i * chunk, chunk), chunk)
+            normal, inverse = row_norm(x_ref[rows, :].astype(WIDE))
+            dh = dh_ref[rows, :]
+            dx = dm_ref[rows, :] + norm_backward(dh, normal, inverse, gain_ref[...])
+            dx_ref[rows, :] = dx.astype(NARROW)
+            dvector_ref[2:3, :] += jnp.sum(dh * normal, 0, keepdims=True)
+            dvector_ref[3:4, :] += jnp.sum(dh, 0, keepdims=True)
+
+
+def qkv_backward(dp, h, x, dm, gain, weight):
+    tokens, width = x.shape
+    return pl.pallas_call(
+        qkv_backward_kernel,
+        grid=(3,),
+        in_specs=[
+            pl.BlockSpec((1, tokens, width), lambda i: (i, 0, 0)),
+            whole((tokens, width)),
+            whole((tokens, width)),
+            whole((tokens, width)),
+            whole((1, width)),
+            pl.BlockSpec((width, width), lambda i: (0, i)),
+        ],
+        out_specs=[
+            pl.BlockSpec((1, width, width), lambda i: (i, 0, 0)),
+            whole((tokens, width)),
+            whole((8, width)),
+        ],
+        out_shape=[
+            jax.ShapeDtypeStruct((3, width, width), NARROW),
+            jax.ShapeDtypeStruct((tokens, width), NARROW),
+            jax.ShapeDtypeStruct((8, width), WIDE),
+        ],
+        scratch_shapes=[pltpu.VMEM((tokens, width), WIDE)],
+        compiler_params=params(48),
+        cost_estimate=pl.CostEstimate(
+            flops=12 * tokens * width * width, bytes_accessed=20 * tokens * width, transcendentals=0
+        ),
+        name="qkv_backward",
+    )(dp, h, x, dm, gain, weight)
+
+
+def table_kernel(heads, groups, batch, own_ref, other_ref, index_ref, out_ref, turned_ref, left_ref, right_ref):
+    @pl.when(pl.program_id(0) == 0)
+    def _():
+        out_ref[...] = jnp.zeros_like(out_ref)
+        turned_ref[...] = jnp.zeros_like(turned_ref)
+
+    rows, lanes = index_ref.shape
+    for head in range(heads):
+        turned_ref[:, head, :] = own_ref[head].astype(WIDE) + other_ref[head].astype(WIDE)
+    zero = jnp.zeros((), NARROW)
+    one = jnp.ones((), NARROW)
+    codes = lax.broadcasted_iota(jnp.int32, (LANES, LANES), 0).astype(WIDE).astype(NARROW)
+
+    def some_rows(part, carry):
+        for within in range(batch):
+            row = part * batch + within
+            index = index_ref[pl.ds(row, 1), :]
+            low = lax.bitwise_and(index, LANES - 1).astype(WIDE).astype(NARROW)
+            high = lax.shift_right_logical(index, 7).astype(WIDE).astype(NARROW)
+            for first in range(0, lanes, LANES):
+                here = slice(first, first + LANES)
+                there = slice(within * lanes + first, within * lanes + first + LANES)
+                right_ref[:, there] = jnp.where(codes == low[:, here], one, zero)
+                value = turned_ref[row, :, here].astype(NARROW)
+                wide_high = jnp.broadcast_to(high[:, here], value.shape)
+                for group in range(groups):
+                    left_ref[group * 16 : group * 16 + 16, there] = jnp.where(
+                        wide_high == jnp.asarray(group, NARROW), value, zero
+                    )
+        out_ref[...] += lax.dot_general(left_ref[...], right_ref[...], NT, preferred_element_type=WIDE)
+        return carry
+
+    lax.fori_loop(0, rows // batch, some_rows, 0)
+
+
+def table_gradient_sum(own, other, index, table_rows):
+    heads, rows, lanes = own.shape
+    groups = round_up(table_rows, LANES) // LANES
+    batch = 4
+    step = 16
+    return pl.pallas_call(
+        functools.partial(table_kernel, heads, groups, batch),
+        grid=(rows // step,),
+        in_specs=[
+            pl.BlockSpec((heads, step, lanes), lambda i: (0, i, 0)),
+            pl.BlockSpec((heads, step, lanes), lambda i: (0, i, 0)),
+            pl.BlockSpec((step, lanes), lambda i: (i, 0)),
+        ],
+        out_specs=whole((groups * 16, LANES)),
+        out_shape=jax.ShapeDtypeStruct((groups * 16, LANES), WIDE),
+        scratch_shapes=[
+            pltpu.VMEM((step, 16, lanes), WIDE),
+            pltpu.VMEM((groups * 16, batch * lanes), NARROW),
+            pltpu.VMEM((LANES, batch * lanes), NARROW),
+        ],
+        compiler_params=params(48),
+        cost_estimate=pl.CostEstimate(
+            flops=rows * lanes * 200 * 1000, bytes_accessed=4 * heads * rows * lanes, transcendentals=0
+        ),
+        name="table_gradient",
+    )(own, other, index)
+
+
+def rotate(value, axis, size, shift):
+    return lax.ppermute(value, axis, [(i, (i + shift) % size) for i in range(size)])
+
+
+def swap_bit(value, size, bit):
+    return lax.ppermute(value, "img", [(i, i ^ (1 << bit)) for i in range(size)])
+
+
+def exchange_images(pieces, size):
+    me = lax.axis_index("blk")
+    held = jnp.zeros_like(pieces)
+    held = lax.dynamic_update_index_in_dim(held, lax.dynamic_index_in_dim(pieces, me, 0, False), me, 0)
+    for shift in range(1, size):
+        target = lax.rem(me + shift, size)
+        source = lax.rem(me + size - shift, size)
+        got = rotate(lax.dynamic_index_in_dim(pieces, target, 0, False), "blk", size, shift)
+        held = lax.dynamic_update_index_in_dim(held, got, source, 0)
+    return held
+
+
+def halve(value, size, bit, position):
+    mine = lax.rem(lax.div(lax.axis_index("img"), 1 << bit), 2)
+    keep = lax.dynamic_index_in_dim(value, mine, position, False)
+    send = lax.dynamic_index_in_dim(value, 1 - mine, position, False)
+    got = swap_bit(send, size, bit)
+    return (keep.astype(WIDE) + got.astype(WIDE)).astype(NARROW)
+
+
+def scatter_sum(values, img, blk):
+    bits = img.bit_length() - 1
+    parts = []
+    for number, value in enumerate(values):
+        value = value.reshape((2,) * bits + (blk,) + value.shape[1:])
+        order = list(range(bits))
+        if number % 2 and bits > 2:
+            order = order[:1] + order[:0:-1]
+        left = list(range(bits))
+        for bit in order:
+            value = halve(value, img, bit, len(left) - 1 - left.index(bit))
+            left.remove(bit)
+        parts.append(value)
+    joined = jnp.concatenate(parts, 1)
+    me = lax.axis_index("blk")
+    total = lax.dynamic_index_in_dim(joined, me, 0, False).astype(WIDE)
+    for shift in range(1, blk):
+        target = lax.rem(me + shift, blk)
+        got = rotate(lax.dynamic_index_in_dim(joined, target, 0, False), "blk", blk, shift)
+        total = total + got.astype(WIDE)
+    outs = []
+    first = 0
+    for value in parts:
+        outs.append(total[first : first + value.shape[1]])
+        first += value.shape[1]
+    return outs
+
+
+def sum_all(value, img, blk):
+    for bit in range(img.bit_length() - 1):
+        value = value + swap_bit(value, img, bit)
+    bit = 1
+    while bit < blk:
+        value = value + lax.ppermute(value, "blk", [(i, i ^ bit) for i in range(blk)])
+        bit *= 2
+    return value
+
+
+def image_on_device(
+    img,
+    blk,
+    images_large,
+    images_small,
+    cotan_large,
+    cotan_small,
+    lengths_large,
+    lengths_small,
+    index_large,
+    index_small,
+    attn_gain,
+    attn_shift,
+    qkv_weight,
+    query_bias,
+    value_bias,
+    table_large,
+    table_small,
+    proj_weight,
+    proj_bias,
+    attn_scale,
+    mlp_gain,
+    mlp_shift,
+    inner_weight,
+    inner_bias,
+    outer_weight,
+    outer_bias,
+    mlp_scale,
+):
+    width = attn_gain.shape[0]
+    heads = table_large.shape[1]
+    hidden = inner_bias.shape[0]
+    rows = images_large.shape[1]
+    smalls, small_rows = images_small.shape[:2]
+    part = round_up(rows, 8)
+    while part * blk % 16:
+        part += 8
+    large = part * blk
+    small = round_up(small_rows, 16)
+    tokens = large + smalls * small
+    images = ((0, large),) + tuple((large + i * small, small) for i in range(smalls))
+    lanes_large = round_up(large, LANES)
+    lanes_small = round_up(small, LANES)
+    double = round_up(small, 32)
+    blk_me = lax.axis_index("blk")
+    core = lax.rem(lax.axis_index("img"), 2)
+
+    def gather_tokens(large_pieces, small_pieces):
+        padded = jnp.pad(large_pieces, ((0, 0), (0, part - rows), (0, 0)))
+        moved = exchange_images(padded, blk).reshape(large, width)
+        still = jnp.pad(small_pieces, ((0, 0), (0, small - small_rows), (0, 0)))
+        return jnp.concatenate([moved, still.reshape(smalls * small, width)], 0)
+
+    def return_tokens(values):
+        moved = exchange_images(values[:large].reshape(blk, part, width), blk)
+        still = values[large:].reshape(smalls, small, width)
+        return moved[:, :rows], still[:, :small_rows]
+
+    def spread_index(index, length, pieces, piece, lanes):
+        turned = jnp.transpose(index).reshape(pieces, length, pieces, length)
+        turned = jnp.pad(turned, ((0, 0), (0, piece - length), (0, 0), (0, piece - length)))
+        turned = turned.reshape(pieces * piece, pieces * piece)
+        return jnp.pad(turned, ((0, 0), (0, lanes - pieces * piece)))
+
+    x = gather_tokens(images_large, images_small)
+    dy = gather_tokens(cotan_large, cotan_small)
+    spread_large = spread_index(index_large, rows, blk, part, lanes_large)
+    spread_small = spread_index(index_small, small_rows, 1, small, lanes_small)
+
+    half = heads // 2
+    large_half = bias_lookup(lax.dynamic_slice_in_dim(table_large, core * half, half, 1), spread_large)
+    other_half = swap_bit(large_half, img, 0)
+    is_first = core == 0
+    large_bias = jnp.concatenate(
+        [jnp.where(is_first, large_half, other_half), jnp.where(is_first, other_half, large_half)], 0
+    )
+    small_bias = bias_lookup(table_small, spread_small)
+
+    place = jnp.arange(large, dtype=jnp.int32)
+    own_length = lax.dynamic_index_in_dim(lengths_large, blk_me, 0, False)
+    inside = (place % part < rows) & (place // part * rows + place % part < own_length)
+    small_place = jnp.arange(small, dtype=jnp.int32)
+    small_inside = (small_place[None, :] < lengths_small[:, None]).reshape(-1)
+    mask = jnp.where(jnp.concatenate([inside, small_inside]), 0.0, NEGATIVE).astype(NARROW)
+    mask = jnp.broadcast_to(mask[:, None], (tokens, LANES))
+
+    def row(vector):
+        return vector.astype(WIDE)[None, :]
+
+    bias_row = row(jnp.concatenate([query_bias, jnp.zeros_like(query_bias), value_bias]))
+    h, p = qkv_forward(x, row(attn_gain), row(attn_shift), qkv_weight, bias_row)
+    out, large_p, small_p = attention_forward(p, mask, large_bias, small_bias, images)
+    zeros = jnp.zeros_like(proj_bias)
+    vectors = jnp.stack(
+        [proj_bias, attn_scale, mlp_gain, mlp_shift, outer_bias, mlp_scale, zeros, zeros]
+    ).astype(WIDE)
+    result, dm, grad_out, dinner, douter, dproj, mlp_sums, dinner_bias = mlp_pass(
+        out, x, dy, proj_weight, vectors, inner_weight, row(inner_bias), outer_weight
+    )
+    result_large, result_small = return_tokens(result)
+    devices = img * blk
+    outer_sum, inner_sum = scatter_sum(
+        [
+            douter.reshape(devices, hidden // devices, width),
+            dinner.reshape(devices, width // devices, hidden).reshape(devices, hidden // devices, width),
+        ],
+        img,
+        blk,
+    )
+    dp, large_ds, small_ds = attention_backward(
+        p, grad_out, out, large_p, small_p, images, (large, lanes_large), (double, lanes_small)
+    )
+    dqkv, dx, qkv_sums = qkv_backward(dp, h, x, dm, row(attn_gain), qkv_weight)
+    grad_large, grad_small = return_tokens(dx)
+    pieces = [value.reshape(devices, width // devices, width) for value in (dqkv[0], dqkv[1], dqkv[2], dproj)]
+    first_sum, second_sum = scatter_sum(
+        [jnp.concatenate(pieces[:2], 1), jnp.concatenate(pieces[2:], 1)], img, blk
+    )
+
+    def core_share(value, axis, which):
+        size = value.shape[axis] // 2
+        return lax.dynamic_slice_in_dim(value, which * size, size, axis)
+
+    tables = []
+    for grad, index, table in ((large_ds, spread_large, table_large), (small_ds, spread_small, table_small)):
+        if index.shape[0] < grad.shape[1]:
+            index = jnp.pad(index, ((0, grad.shape[1] - index.shape[0]), (0, 0)))
+        other = swap_bit(core_share(grad, 1, 1 - core), img, 0)
+        tables.append(
+            table_gradient_sum(core_share(grad, 1, core), other, core_share(index, 0, core), table.shape[0])
+        )
+    sums = jnp.concatenate([mlp_sums[:6], qkv_sums[:4], dinner_bias.reshape(-1, width)], 0)
+    joined = jnp.concatenate(tables + [sums.reshape(-1, LANES)], 0)
+    joined = sum_all(joined, img, blk)
+    outs = []
+    first = 0
+    for table, total in ((table_large, tables[0]), (table_small, tables[1])):
+        value = joined[first : first + total.shape[0]].reshape(-1, 16, LANES)[:, :heads]
+        outs.append(jnp.transpose(value, (0, 2, 1)).reshape(-1, heads)[: table.shape[0]])
+        first += total.shape[0]
+    sums = joined[first:].reshape(-1)
+    me = lax.axis_index("img") * blk + blk_me
+    share = width // devices
+
+    def own(place, length=1):
+        return lax.dynamic_slice_in_dim(sums, place * width + me * share * length, share * length, 0)
+
+    return (
+        result_large,
+        result_small,
+        grad_large,
+        grad_small,
+        own(8),
+        own(9),
+        jnp.concatenate([first_sum[:share], first_sum[share:], second_sum[:share]], 1),
+        own(6),
+        own(7),
+        outs[0],
+        outs[1],
+        second_sum[share:],
+        own(5),
+        own(4),
+        own(2),
+        own(3),
+        inner_sum.reshape(share, hidden),
+        own(10, hidden // width),
+        outer_sum,
+        own(1),
+        own(0),
+    )
+
+
 def solution(mesh):
+    img, blk = mesh.shape["img"], mesh.shape["blk"]
+
+    def by_device(*args):
+        if args[0].shape[0] == blk:
+            return image_on_device(img, blk, *args)
+        return on_device(*args)
+
     return jax.shard_map(
-        on_device,
+        by_device,
         mesh=mesh,
         in_specs=(
             P("img", "blk", None),

time: 2070 us -> 616 us (0.30)
  matrix products: 858 us -> 0 us
  waiting for transfers between devices: 844 us -> 71.4 us
  Pallas kernels: 0 us -> 224 us
  local copies, waits for them, and re-layouts: 271 us -> 214 us
  starting transfers between devices: 0.84 us -> 54.1 us
  other arithmetic: 64 us -> 38.5 us
    dot_general x112 -> x0, matrix products: 858 us -> none  [the longest x44 368 us: table_one_query(): jnp.dot(selector.T, grad_row, precision=HIGHEST, preferred_element_type=j...]
    reduce_scatter x4 -> x0, waiting for transfers between devices: 515 us -> none  [the longest x1 142 us: on_device(): lax.psum_scatter(grad_outer_weight, ('img', 'blk'), scatter_dimension=0,...]
    pallas_call x0 -> x9, Pallas kernels: none -> 224 us  [the longest x2 63.8 us: table_gradient_sum(): pl.pallas_call(functools.partial(table_kernel, heads, groups, batch), gri...]
    unnamed x11 -> x0, waiting for transfers between devices: 214 us -> none
    dynamic_update_slice x0 -> x18, local copies, waits for them, and re-layouts: none -> 125 us  [the longest x14 94.7 us: exchange_images(): held = lax.dynamic_update_index_in_dim(held, got, source, 0)]
    psum x1 -> x0, waiting for transfers between devices: 115 us -> none  [on_device(): lax.psum((large_table_grad, small_table_grad), ('img', 'blk'))]
    ppermute x0 -> x38, waiting for transfers between devices: none -> 71.4 us  [the longest x18 29.3 us: rotate(): lax.ppermute(value, axis, [(i, (i + shift) % size) for i in range(size)])]
    reshape x16 -> x10, local copies, waits for them, and re-layouts: 74.7 us -> 11.7 us  [the longest x2 7.94 us: spread_index(): turned = jnp.transpose(index).reshape(pieces, length, pieces, length)]
  transfers between devices with their start and end apart: 9 -> 38, of which waited for: 7 -> 13; matrix products, arithmetic and copies ran while one was open for 28% -> 34% of each run, Pallas kernels for 0% -> 13%
where the time goes in v1:
time: 616 us; the launch traced here: 604 us
  Pallas kernels  224 us (36%)
  local copies, waits for them, and re-layouts  214 us (35%)
  waiting for transfers between devices  71.4 us (12%)
  starting transfers between devices  54.1 us (9%)
  other arithmetic  38.5 us (6%)
    dynamic_update_slice x14, local copies, waits for them, and re-layouts, exchange_images(): held = lax.dynamic_update_index_in_dim(held, got, source, 0)  94.7 us
    pallas_call x2, Pallas kernels, table_gradient_sum(): pl.pallas_call(functools.partial(table_kernel, heads, groups, batch), gri...  63.8 us
    pallas_call x1, Pallas kernels, mlp_pass(): pl.pallas_call(mlp_kernel, grid=(hidden // block,), in_specs=[whole((toke...  58.1 us
    pallas_call x2, Pallas kernels, bias_lookup(): pl.pallas_call(functools.partial(bias_kernel, pairs, groups), grid=(rows...  35.5 us
    ppermute x18, starting transfers between devices, rotate(): lax.ppermute(value, axis, [(i, (i + shift) % size) for i in range(size)])  35.3 us
    dynamic_update_slice x4, local copies, waits for them, and re-layouts, exchange_images(): lax.dynamic_update_index_in_dim(held, lax.dynamic_index_in_dim(pieces, me...  30.4 us
    ppermute x18, waiting for transfers between devices, rotate(): lax.ppermute(value, axis, [(i, (i + shift) % size) for i in range(size)])  29.3 us
    ppermute x18, waiting for transfers between devices, swap_bit(): return lax.ppermute(value, 'img', [(i, i ^ 1 << bit) for i in range(size)])  26.9 us
  transfers between devices with their start and end apart: 38, of which 13 were waited for; matrix products, arithmetic and copies ran while one was open for 34% of the time, Pallas kernels for 13%

profile of v1, /device:TPU:0, one launch (start us, length us, event | category | flops | bytes accessed | tf_op | source)
XLA Modules:
  0.0 603.9 jit_solution(15329579290191931351)
XLA Ops:
  14.6 31.1 %bias_lookup.2 = bf16[6,608,640]{2,1,0:T(8,128)(2,1)} custom-call(s32[54,8,128]{2,1,0:T(8,128)S(1)} %broadcast_in_dim.103.table_ref, s32[608,640]{1,0:T(8,128)S(1)} %pad.46.index_ref), custom_call_target="tpu_custom_call" | custom-call | flops 1260748800 | bytes 4669440 | tf_op jit(solution)/shard_map/bias_lookup/pallas_call | solution.py:436
  61.1 8.7 %dynamic_update_slice.53 = bf16[4,152,768]{2,0,1:T(4,128)(2,1)S(1)} dynamic-update-slice(bf16[4,152,768]{2,0,1:T(4,128)(2,1)S(1)} %broadcast.82.clone.2, bf16[1,152,768]{2,0,1:T(2,128)(2,1)} %copy.74, s32[]{:T(128)S(6)} %select_n.188, s32[]{:T(128)} %constant.263.clone.1, s32[]{:T(128)} %constant.263.clone.1) | dynamic-update-slice | bytes 466948 | tf_op jit(solution)/shard_map/jit(dynamic_update_index_in_dim)/dynamic_update_slice | solution.py:945
  71.0 9.0 %dynamic_update_slice.49 = bf16[4,152,768]{2,0,1:T(4,128)(2,1)} dynamic-update-slice(bf16[4,152,768]{2,0,1:T(4,128)(2,1)} %broadcast.82.clone.1, bf16[1,152,768]{2,0,1:T(2,128)(2,1)S(1)} %copy.64, s32[]{:T(128)S(6)} %select_n.188, s32[]{:T(128)} %constant.263.clone.1, s32[]{:T(128)} %constant.263.clone.1) | dynamic-update-slice | bytes 466948 | tf_op jit(solution)/shard_map/jit(dynamic_update_index_in_dim)/dynamic_update_slice | solution.py:945
  97.9 9.0 %dynamic_update_slice.54 = bf16[4,152,768]{2,0,1:T(4,128)(2,1)} dynamic-update-slice(bf16[4,152,768]{2,0,1:T(4,128)(2,1)} %copy-done.17, bf16[1,152,768]{2,0,1:T(2,128)(2,1)S(1)} %copy.75, s32[]{:T(128)S(6)} %select_n.190, s32[]{:T(128)} %constant.263.clone.1, s32[]{:T(128)} %constant.263.clone.1) | dynamic-update-slice | bytes 466948 | tf_op jit(solution)/shard_map/jit(dynamic_update_index_in_dim)/dynamic_update_slice | solution.py:950
  107.0 9.0 %dynamic_update_slice.55 = bf16[4,152,768]{2,0,1:T(4,128)(2,1)} dynamic-update-slice(bf16[4,152,768]{2,0,1:T(4,128)(2,1)} %dynamic_update_slice.54, bf16[1,152,768]{2,0,1:T(2,128)(2,1)S(1)} %copy.76, s32[]{:T(128)S(6)} %select_n.191, s32[]{:T(128)} %constant.263.clone.1, s32[]{:T(128)} %constant.263.clone.1) | dynamic-update-slice | bytes 466948 | tf_op jit(solution)/shard_map/jit(dynamic_update_index_in_dim)/dynamic_update_slice | solution.py:950
  116.0 9.0 %dynamic_update_slice.56 = bf16[4,152,768]{2,0,1:T(4,128)(2,1)} dynamic-update-slice(bf16[4,152,768]{2,0,1:T(4,128)(2,1)} %dynamic_update_slice.55, bf16[1,152,768]{2,0,1:T(2,128)(2,1)S(1)} %copy.77, s32[]{:T(128)S(6)} %select_n.189, s32[]{:T(128)} %constant.263.clone.1, s32[]{:T(128)} %constant.263.clone.1) | dynamic-update-slice | bytes 466948 | tf_op jit(solution)/shard_map/jit(dynamic_update_index_in_dim)/dynamic_update_slice | solution.py:950
  131.0 9.0 %dynamic_update_slice.50 = bf16[4,152,768]{2,0,1:T(4,128)(2,1)} dynamic-update-slice(bf16[4,152,768]{2,0,1:T(4,128)(2,1)} %dynamic_update_slice.49, bf16[1,152,768]{2,0,1:T(2,128)(2,1)S(1)} %copy.65, s32[]{:T(128)S(6)} %select_n.190, s32[]{:T(128)} %constant.263.clone.1, s32[]{:T(128)} %constant.263.clone.1) | dynamic-update-slice | bytes 466948 | tf_op jit(solution)/shard_map/jit(dynamic_update_index_in_dim)/dynamic_update_slice | solution.py:950
  140.0 9.0 %dynamic_update_slice.51 = bf16[4,152,768]{2,0,1:T(4,128)(2,1)} dynamic-update-slice(bf16[4,152,768]{2,0,1:T(4,128)(2,1)} %dynamic_update_slice.50, bf16[1,152,768]{2,0,1:T(2,128)(2,1)S(1)} %copy.66, s32[]{:T(128)S(6)} %select_n.191, s32[]{:T(128)} %constant.263.clone.1, s32[]{:T(128)} %constant.263.clone.1) | dynamic-update-slice | bytes 466948 | tf_op jit(solution)/shard_map/jit(dynamic_update_index_in_dim)/dynamic_update_slice | solution.py:950
  149.0 9.1 %dynamic_update_slice.52 = bf16[4,152,768]{2,0,1:T(4,128)(2,1)} dynamic-update-slice(bf16[4,152,768]{2,0,1:T(4,128)(2,1)} %dynamic_update_slice.51, bf16[1,152,768]{2,0,1:T(2,128)(2,1)} %copy.67, s32[]{:T(128)S(6)} %select_n.189, s32[]{:T(128)} %constant.263.clone.1, s32[]{:T(128)} %constant.263.clone.1) | dynamic-update-slice | bytes 466948 | tf_op jit(solution)/shard_map/jit(dynamic_update_index_in_dim)/dynamic_update_slice | solution.py:950
  162.0 8.8 %qkv_forward.1 = (bf16[1024,768]{1,0:T(8,128)(2,1)S(1)}, bf16[1024,2304]{1,0:T(8,128)(2,1)}) custom-call(bf16[1024,768]{1,0:T(8,128)(2,1)S(1)} %get-tuple-element.110.x_ref, f32[1,768]{1,0:T(1,128)S(1)} %reshape.231.gain_ref, f32[1,768]{1,0:T(1,128)S(1)} %reshape.232.shift_ref, bf16[768,2304]{1,0:T(8,128)(2,1)} %weight_ref.3, f32[1,2304]{1,0:T(1,128)S(1)} %fusion.45.bias_ref), custom_call_target="tpu_custom_call" | custom-call | flops 3623878656 | bytes 8257536 | tf_op jit(solution)/shard_map/qkv_forward/pallas_call | solution.py:463
  170.9 7.3 %broadcast_select_fusion.1 = (bf16[6,608,640]{2,1,0:T(8,128)(2,1)S(1)}, bf16[6,608,640]{2,1,0:T(8,128)(2,1)}) fusion(bf16[6,608,640]{2,1,0:T(8,128)(2,1)} %bias_lookup.2, bf16[6,608,640]{2,1,0:T(8,128)(2,1)} %collective-permute-done.3, pred[]{:T(512)S(6)} %eq.6), kind=kLoop, calls=%fused_computation.6 | loop fusion | flops 4669440 | bytes 18677760 | tf_op jit(solution)/shard_map/jit(_where)/select_n | solution.py:1074
  178.2 7.1 %pad_maximum_fusion.large_bias_ref = bf16[12,608,640]{2,1,0:T(8,128)(2,1)} fusion(bf16[6,608,640]{2,1,0:T(8,128)(2,1)} %get-tuple-element.62, bf16[6,608,640]{2,1,0:T(8,128)(2,1)S(1)} %get-tuple-element.61), kind=kLoop, calls=%fused_computation | loop fusion | flops 4669440 | bytes 18677760 | tf_op jit(solution)/shard_map/concatenate | solution.py:1073
  185.5 19.8 %attention_forward.1 = (bf16[1024,768]{1,0:T(8,128)(2,1)S(1)}, bf16[12,608,608]{2,1,0:T(8,128)(2,1)}, bf16[12,2,208,208]{3,2,1,0:T(8,128)(2,1)S(1)}) custom-call(bf16[1024,2304]{1,0:T(8,128)(2,1)} %get-tuple-element.40.q_ref.k_ref.v_ref, bf16[1024,2304]{1,0:T(8,128)(2,1)} %get-tuple-element.40.q_ref.k_ref.v_ref, ...), custom_call_target="tpu_custom_call" | custom-call | flops 5605687296 | bytes 21897216 | tf_op jit(solution)/shard_map/attention_forward/pallas_call | solution.py:528
  207.8 58.1 %mlp_pass.1 = (bf16[1024,768]{1,0:T(8,128)(2,1)}, f32[1024,768]{1,0:T(8,128)}, bf16[1024,768]{1,0:T(8,128)(2,1)}, bf16[768,3072]{1,0:T(8,128)(2,1)}, bf16[3072,7...) custom-call(bf16[1024,768]{1,0:T(8,128)(2,1)} %copy-done.5, ...), custom_call_target="tpu_custom_call" | custom-call | flops 28991029248 | bytes 18874368 | tf_op jit(solution)/shard_map/mlp_pass/pallas_call | solution.py:757
  266.0 8.6 %reshape_reshape_reshape.3 = bf16[2,2,2,4,96,768]{5,4,3,2,1,0:T(8,128)(2,1)} reshape(bf16[768,3072]{1,0:T(8,128)(2,1)} %get-tuple-element.58) | data formatting | bytes 9437184 | tf_op jit(solution)/shard_map/reshape;reshape;reshape | solution.py:966
  276.0 22.3 %attention_backward.1 = (bf16[3,1024,768]{2,1,0:T(8,128)(2,1)}, bf16[12,608,640]{2,1,0:T(8,128)(2,1)}, bf16[12,224,256]{2,1,0:T(8,128)(2,1)S(1)}) custom-call(bf16[1024,2304]{1,0:T(8,128)(2,1)} %get-tuple-element.40.q_ref.k_ref.v_ref, bf16[1024,2304]{1,0:T(8,128)(2,1)} %get-tuple-element.40.q_ref.k_ref.v_ref, ...), custom_call_target="tpu_custom_call" | custom-call | flops 11211374592 | bytes 21897216 | tf_op jit(solution)/shard_map/attention_backward/pallas_call | solution.py:613
  298.3 15.3 %qkv_backward.1 = (bf16[3,768,768]{2,1,0:T(8,128)(2,1)}, bf16[1024,768]{1,0:T(8,128)(2,1)S(1)}, f32[8,768]{1,0:T(8,128)S(1)}) custom-call(bf16[3,1024,768]{2,1,0:T(8,128)(2,1)} %get-tuple-element.46.dp_ref, bf16[1024,768]{1,0:T(8,128)(2,1)S(1)} %copy-done.8, bf16[1024,768]{1,0:T(8,128)(2,1)S(1)} %copy-done.1, f32[1024,768]{1,0:T(8,128)} %get-tuple-element.48.dm_ref, ...), custom_call_target="tpu_custom_call" | custom-call | flops 7247757312 | bytes 15728640 | tf_op jit(solution)/shard_map/qkv_backward/pallas_call | solution.py:841
  327.0 8.1 %constant_dynamic-slice_fusion.5 = (bf16[12,304,640]{2,1,0:T(8,128)(2,1)}, bf16[12,304,640]{2,1,0:T(8,128)(2,1)}) fusion(bf16[12,608,640]{2,1,0:T(8,128)(2,1)} %get-tuple-element.50, s32[]{:T(128)S(6)} %select_n.200, s32[]{:T(128)S(6)} %select_n.199), kind=kLoop, calls=%fused_computation.133 | loop fusion | bytes 18677768 | tf_op jit(solution)/shard_map/dynamic_slice | solution.py:1121
  341.9 7.7 %collective-permute-done.11 = bf16[152,768]{1,0:T(8,128)(2,1)S(1)} collective-permute-done((bf16[152,768]{1,0:T(8,128)(2,1)S(1)}, bf16[152,768]{1,0:T(8,128)(2,1)S(1)}, u32[]{:S(2)}, u32[]{:S(2)}) %collective-permute-start.11) | collective-permute-done | bytes 233504 | tf_op jit(solution)/shard_map/ppermute | solution.py:935
  374.3 7.9 %collective-permute-done.8 = bf16[152,768]{1,0:T(8,128)(2,1)S(1)} collective-permute-done((bf16[152,768]{1,0:T(8,128)(2,1)}, bf16[152,768]{1,0:T(8,128)(2,1)S(1)}, u32[]{:S(2)}, u32[]{:S(2)}) %collective-permute-start.8) | collective-permute-done | bytes 233504 | tf_op jit(solution)/shard_map/ppermute | solution.py:935
  396.4 6.3 %dynamic_update_slice.61 = bf16[4,152,768]{2,0,1:T(4,128)(2,1)S(1)} dynamic-update-slice(bf16[4,152,768]{2,0,1:T(4,128)(2,1)S(1)} %broadcast.82.clone.3, bf16[1,152,768]{2,0,1:T(2,128)(2,1)S(1)} %copy.99, s32[]{:T(128)S(6)} %select_n.188, s32[]{:T(128)} %constant.263.clone.1, s32[]{:T(128)} %constant.263.clone.1) | dynamic-update-slice | bytes 466948 | tf_op jit(solution)/shard_map/jit(dynamic_update_index_in_dim)/dynamic_update_slice | solution.py:945
  412.3 6.3 %dynamic_update_slice.62 = bf16[4,152,768]{2,0,1:T(4,128)(2,1)S(1)} dynamic-update-slice(bf16[4,152,768]{2,0,1:T(4,128)(2,1)S(1)} %dynamic_update_slice.61, bf16[1,152,768]{2,0,1:T(2,128)(2,1)S(1)} %copy.84, s32[]{:T(128)S(6)} %select_n.190, s32[]{:T(128)} %constant.263.clone.1, s32[]{:T(128)} %constant.263.clone.1) | dynamic-update-slice | bytes 466948 | tf_op jit(solution)/shard_map/jit(dynamic_update_index_in_dim)/dynamic_update_slice | solution.py:950
  418.6 6.3 %dynamic_update_slice.63 = bf16[4,152,768]{2,0,1:T(4,128)(2,1)S(1)} dynamic-update-slice(bf16[4,152,768]{2,0,1:T(4,128)(2,1)S(1)} %dynamic_update_slice.62, bf16[1,152,768]{2,0,1:T(2,128)(2,1)S(1)} %copy.85, s32[]{:T(128)S(6)} %select_n.191, s32[]{:T(128)} %constant.263.clone.1, s32[]{:T(128)} %constant.263.clone.1) | dynamic-update-slice | bytes 466948 | tf_op jit(solution)/shard_map/jit(dynamic_update_index_in_dim)/dynamic_update_slice | solution.py:950
  425.0 6.3 %dynamic_update_slice.64 = bf16[4,152,768]{2,0,1:T(4,128)(2,1)S(1)} dynamic-update-slice(bf16[4,152,768]{2,0,1:T(4,128)(2,1)S(1)} %dynamic_update_slice.63, bf16[1,152,768]{2,0,1:T(2,128)(2,1)S(1)} %copy.86, s32[]{:T(128)S(6)} %select_n.189, s32[]{:T(128)} %constant.263.clone.1, s32[]{:T(128)} %constant.263.clone.1) | dynamic-update-slice | bytes 466948 | tf_op jit(solution)/shard_map/jit(dynamic_update_index_in_dim)/dynamic_update_slice | solution.py:950
  433.7 6.3 %dynamic_update_slice.58 = bf16[4,152,768]{2,0,1:T(4,128)(2,1)S(1)} dynamic-update-slice(bf16[4,152,768]{2,0,1:T(4,128)(2,1)S(1)} %dynamic_update_slice.57, bf16[1,152,768]{2,0,1:T(2,128)(2,1)S(1)} %copy.80, s32[]{:T(128)S(6)} %select_n.190, s32[]{:T(128)} %constant.263.clone.1, s32[]{:T(128)} %constant.263.clone.1) | dynamic-update-slice | bytes 466948 | tf_op jit(solution)/shard_map/jit(dynamic_update_index_in_dim)/dynamic_update_slice | solution.py:950
  440.0 6.3 %dynamic_update_slice.59 = bf16[4,152,768]{2,0,1:T(4,128)(2,1)S(1)} dynamic-update-slice(bf16[4,152,768]{2,0,1:T(4,128)(2,1)S(1)} %dynamic_update_slice.58, bf16[1,152,768]{2,0,1:T(2,128)(2,1)S(1)} %copy.81, s32[]{:T(128)S(6)} %select_n.191, s32[]{:T(128)} %constant.263.clone.1, s32[]{:T(128)} %constant.263.clone.1) | dynamic-update-slice | bytes 466948 | tf_op jit(solution)/shard_map/jit(dynamic_update_index_in_dim)/dynamic_update_slice | solution.py:950
  446.3 6.3 %dynamic_update_slice.60 = bf16[4,152,768]{2,0,1:T(4,128)(2,1)S(1)} dynamic-update-slice(bf16[4,152,768]{2,0,1:T(4,128)(2,1)S(1)} %dynamic_update_slice.59, bf16[1,152,768]{2,0,1:T(2,128)(2,1)S(1)} %copy.82, s32[]{:T(128)S(6)} %select_n.189, s32[]{:T(128)} %constant.263.clone.1, s32[]{:T(128)} %constant.263.clone.1) | dynamic-update-slice | bytes 466948 | tf_op jit(solution)/shard_map/jit(dynamic_update_index_in_dim)/dynamic_update_slice | solution.py:950
  469.7 8.5 %table_gradient.3 = f32[96,128]{1,0:T(8,128)S(1)} custom-call(bf16[12,112,256]{2,1,0:T(8,128)(2,1)S(1)} %copy-done.3, bf16[12,112,256]{2,1,0:T(8,128)(2,1)S(1)} %collective-permute-done.14.other_ref, s32[112,256]{1,0:T(8,128)S(1)} %pad_dynamic-slice_fusion.32.index_ref), custom_call_target="tpu_custom_call" | custom-call | flops 5734400000 | bytes 1376256 | tf_op jit(solution)/shard_map/table_gradient/pallas_call | solution.py:911
  478.9 12.6 %collective-permute-done.33 = bf16[2,4,96,768]{3,2,1,0:T(8,128)(2,1)S(1)} collective-permute-done((bf16[2,4,96,768]{3,2,1,0:T(8,128)(2,1)S(1)}, bf16[2,4,96,768]{3,2,1,0:T(8,128)(2,1)S(1)}, u32[]{:S(2)}, u32[]{:S(2)}) %collective-permute-start.33) | collective-permute-done | bytes 1179680 | tf_op jit(solution)/shard_map/ppermute | solution.py:939
  499.5 55.4 %table_gradient.2 = f32[288,128]{1,0:T(8,128)S(1)} custom-call(bf16[12,304,640]{2,1,0:T(8,128)(2,1)S(1)} %bitcast.187, bf16[12,304,640]{2,1,0:T(8,128)(2,1)} %collective-permute-done.13.other_ref, s32[304,640]{1,0:T(8,128)S(1)} %copy-done.2), custom_call_target="tpu_custom_call" | custom-call | flops 38912000000 | bytes 9338880 | tf_op jit(solution)/shard_map/table_gradient/pallas_call | solution.py:911
  573.7 8.0 %collective-permute-done.36 = bf16[192,768]{1,0:T(8,128)(2,1)S(1)} collective-permute-done((bf16[192,768]{1,0:T(8,128)(2,1)S(1)}, bf16[192,768]{1,0:T(8,128)(2,1)S(1)}, u32[]{:S(2)}, u32[]{:S(2)}) %collective-permute-start.36) | collective-permute-done | bytes 294944 | tf_op jit(solution)/shard_map/ppermute | solution.py:935
  590.3 10.3 %collective-permute-done.19 = f32[468,128]{1,0:T(8,128)S(1)} collective-permute-done((f32[468,128]{1,0:T(8,128)S(1)}, f32[468,128]{1,0:T(8,128)S(1)}, u32[]{:S(2)}, u32[]{:S(2)}) %collective-permute-start.19) | collective-permute-done | bytes 239648 | tf_op jit(solution)/shard_map/ppermute | solution.py:995
  (347 shorter events, 188.1 us)
Async XLA Ops:
  45.7 125.2 %collective-permute-start.3 = (bf16[6,608,640]{2,1,0:T(8,128)(2,1)}, bf16[6,608,640]{2,1,0:T(8,128)(2,1)}, u32[]{:S(2)}, u32[]{:S(2)}) collective-permute-start(bf16[6,608,640]{2,1,0:T(8,128)(2,1)} %bias_lookup.2), channel_id=1, source_target_pairs={{0,4},{4,0},{8,12},{12,8},{16,20},{20,16},{24,28},{28,24},{1,5},{5... | collective-permute-start | bytes 14008328 | tf_op jit(solution)/shard_map/ppermute | solution.py:939
  47.2 41.9 %collective-permute-start.4 = (bf16[152,768]{1,0:T(8,128)(2,1)}, bf16[152,768]{1,0:T(8,128)(2,1)}, u32[]{:S(2)}, u32[]{:S(2)}) collective-permute-start(bf16[152,768]{1,0:T(8,128)(2,1)} %get-tuple-element.84), channel_id=1, source_target_pairs={{0,1},{1,2},{2,3},{3,0},{4,5},{5,6},{6,7},{7,4},{8,9},{9,10},{10,1... | collective-permute-start | bytes 700424 | tf_op jit(solution)/shard_map/ppermute | solution.py:935
  49.8 39.8 %collective-permute-start.5 = (bf16[152,768]{1,0:T(8,128)(2,1)}, bf16[152,768]{1,0:T(8,128)(2,1)}, u32[]{:S(2)}, u32[]{:S(2)}) collective-permute-start(bf16[152,768]{1,0:T(8,128)(2,1)} %get-tuple-element.85), channel_id=1, source_target_pairs={{0,2},{1,3},{2,0},{3,1},{4,6},{5,7},{6,4},{7,5},{8,10},{9,11},{10,... | collective-permute-start | bytes 700424 | tf_op jit(solution)/shard_map/ppermute | solution.py:935
  52.4 44.2 %collective-permute-start.6 = (bf16[152,768]{1,0:T(8,128)(2,1)}, bf16[152,768]{1,0:T(8,128)(2,1)}, u32[]{:S(2)}, u32[]{:S(2)}) collective-permute-start(bf16[152,768]{1,0:T(8,128)(2,1)} %get-tuple-element.83), channel_id=1, source_target_pairs={{0,3},{1,0},{2,1},{3,2},{4,7},{5,4},{6,5},{7,6},{8,11},{9,8},{10,9... | collective-permute-start | bytes 700424 | tf_op jit(solution)/shard_map/ppermute | solution.py:935
  56.0 70.3 %collective-permute-start = (bf16[152,768]{1,0:T(8,128)(2,1)}, bf16[152,768]{1,0:T(8,128)(2,1)}, u32[]{:S(2)}, u32[]{:S(2)}) collective-permute-start(bf16[152,768]{1,0:T(8,128)(2,1)} %get-tuple-element.88), channel_id=1, source_target_pairs={{0,1},{1,2},{2,3},{3,0},{4,5},{5,6},{6,7},{7,4},{8,9},{9,10},{10,1... | collective-permute-start | bytes 700424 | tf_op jit(solution)/shard_map/ppermute | solution.py:935
  89.1 38.5 %collective-permute-start.1 = (bf16[152,768]{1,0:T(8,128)(2,1)S(1)}, bf16[152,768]{1,0:T(8,128)(2,1)}, u32[]{:S(2)}, u32[]{:S(2)}) collective-permute-start(bf16[152,768]{1,0:T(8,128)(2,1)S(1)} %get-tuple-element.89), channel_id=1, source_target_pairs={{0,2},{1,3},{2,0},{3,1},{4,6},{5,7},{6,4},{7,5},{8,10},{9,11},{10,... | collective-permute-start | bytes 700424 | tf_op jit(solution)/shard_map/ppermute | solution.py:935
  89.5 39.4 %collective-permute-start.2 = (bf16[152,768]{1,0:T(8,128)(2,1)}, bf16[152,768]{1,0:T(8,128)(2,1)}, u32[]{:S(2)}, u32[]{:S(2)}) collective-permute-start(bf16[152,768]{1,0:T(8,128)(2,1)} %get-tuple-element.87), channel_id=1, source_target_pairs={{0,3},{1,0},{2,1},{3,2},{4,7},{5,4},{6,5},{7,6},{8,11},{9,8},{10,9... | collective-permute-start | bytes 700424 | tf_op jit(solution)/shard_map/ppermute | solution.py:935
  317.3 17.9 %collective-permute-start.23 = (bf16[2,2,4,48,768]{4,3,2,1,0:T(8,128)(2,1)}, bf16[2,2,4,48,768]{4,3,2,1,0:T(8,128)(2,1)}, u32[]{:S(2)}, u32[]{:S(2)}) collective-permute-start(bf16[2,2,4,48,768]{4,3,2,1,0:T(8,128)(2,1)} %fusion.7), channel_id=1, source_target_pairs={{0,4},{4,0},{8,12},{12,8},{16,20},{20,16},{24,28},{28,24},{1,5},{5... | collective-permute-start | bytes 3538952 | tf_op jit(solution)/shard_map/ppermute | solution.py:939
  319.4 136.8 %collective-permute-start.32 = (bf16[2,2,4,96,768]{4,3,2,1,0:T(8,128)(2,1)}, bf16[2,2,4,96,768]{4,3,2,1,0:T(8,128)(2,1)}, u32[]{:S(2)}, u32[]{:S(2)}) collective-permute-start(bf16[2,2,4,96,768]{4,3,2,1,0:T(8,128)(2,1)} %dynamic-slice_bitcast_fusion), channel_id=1, source_target_pairs={{0,4},{4,0},{8,12},{12,8},{16,20},{20,16},{24,28},{28,24},{1,5},{5... | collective-permute-start | bytes 7077896 | tf_op jit(solution)/shard_map/ppermute | solution.py:939
  320.6 32.9 %collective-permute-start.20 = (bf16[2,2,4,48,768]{4,3,2,0,1:T(8,128)(2,1)}, bf16[2,2,4,48,768]{4,3,2,0,1:T(8,128)(2,1)}, u32[]{:S(2)}, u32[]{:S(2)}) collective-permute-start(bf16[2,2,4,48,768]{4,3,2,0,1:T(8,128)(2,1)} %bitcast.180), channel_id=1, source_target_pairs={{0,4},{4,0},{8,12},{12,8},{16,20},{20,16},{24,28},{28,24},{1,5},{5... | collective-permute-start | bytes 3538952 | tf_op jit(solution)/shard_map/ppermute | solution.py:939
  324.5 139.1 %collective-permute-start.29 = (bf16[2,2,4,96,768]{4,3,2,0,1:T(8,128)(2,1)}, bf16[2,2,4,96,768]{4,3,2,0,1:T(8,128)(2,1)}, u32[]{:S(2)}, u32[]{:S(2)}) collective-permute-start(bf16[2,2,4,96,768]{4,3,2,0,1:T(8,128)(2,1)} %bitcast.179), channel_id=1, source_target_pairs={{0,4},{4,0},{8,12},{12,8},{16,20},{20,16},{24,28},{28,24},{1,5},{5... | collective-permute-start | bytes 7077896 | tf_op jit(solution)/shard_map/ppermute | solution.py:939
  325.4 14.1 %collective-permute-start.10 = (bf16[152,768]{1,0:T(8,128)(2,1)S(1)}, bf16[152,768]{1,0:T(8,128)(2,1)S(1)}, u32[]{:S(2)}, u32[]{:S(2)}) collective-permute-start(bf16[152,768]{1,0:T(8,128)(2,1)S(1)} %get-tuple-element.77), channel_id=1, source_target_pairs={{0,1},{1,2},{2,3},{3,0},{4,5},{5,6},{6,7},{7,4},{8,9},{9,10},{10,1... | collective-permute-start | bytes 700424 | tf_op jit(solution)/shard_map/ppermute | solution.py:935
  335.1 14.5 %collective-permute-start.11 = (bf16[152,768]{1,0:T(8,128)(2,1)S(1)}, bf16[152,768]{1,0:T(8,128)(2,1)S(1)}, u32[]{:S(2)}, u32[]{:S(2)}) collective-permute-start(bf16[152,768]{1,0:T(8,128)(2,1)S(1)} %get-tuple-element.76), channel_id=1, source_target_pairs={{0,2},{1,3},{2,0},{3,1},{4,6},{5,7},{6,4},{7,5},{8,10},{9,11},{10,... | collective-permute-start | bytes 700424 | tf_op jit(solution)/shard_map/ppermute | solution.py:935
  339.6 17.2 %collective-permute-start.12 = (bf16[152,768]{1,0:T(8,128)(2,1)S(1)}, bf16[152,768]{1,0:T(8,128)(2,1)S(1)}, u32[]{:S(2)}, u32[]{:S(2)}) collective-permute-start(bf16[152,768]{1,0:T(8,128)(2,1)S(1)} %get-tuple-element.75), channel_id=1, source_target_pairs={{0,3},{1,0},{2,1},{3,2},{4,7},{5,4},{6,5},{7,6},{8,11},{9,8},{10,9... | collective-permute-start | bytes 700424 | tf_op jit(solution)/shard_map/ppermute | solution.py:935
  349.6 12.7 %collective-permute-start.7 = (bf16[152,768]{1,0:T(8,128)(2,1)S(1)}, bf16[152,768]{1,0:T(8,128)(2,1)S(1)}, u32[]{:S(2)}, u32[]{:S(2)}) collective-permute-start(bf16[152,768]{1,0:T(8,128)(2,1)S(1)} %get-tuple-element.81), channel_id=1, source_target_pairs={{0,1},{1,2},{2,3},{3,0},{4,5},{5,6},{6,7},{7,4},{8,9},{9,10},{10,1... | collective-permute-start | bytes 700424 | tf_op jit(solution)/shard_map/ppermute | solution.py:935
  353.6 15.3 %collective-permute-start.24 = (bf16[2,4,48,768]{3,2,1,0:T(8,128)(2,1)}, bf16[2,4,48,768]{3,2,1,0:T(8,128)(2,1)}, u32[]{:S(2)}, u32[]{:S(2)}) collective-permute-start(bf16[2,4,48,768]{3,2,1,0:T(8,128)(2,1)} %dynamic-slice_bitcast_fusion.5), channel_id=1, source_target_pairs={{0,16},{4,20},{8,24},{12,28},{16,0},{20,4},{24,8},{28,12},{1,17},{... | collective-permute-start | bytes 1769480 | tf_op jit(solution)/shard_map/ppermute | solution.py:939
  356.8 142.7 %collective-permute-start.13 = (bf16[12,304,640]{2,1,0:T(8,128)(2,1)}, bf16[12,304,640]{2,1,0:T(8,128)(2,1)}, u32[]{:S(2)}, u32[]{:S(2)}) collective-permute-start(bf16[12,304,640]{2,1,0:T(8,128)(2,1)} %get-tuple-element.59), channel_id=1, source_target_pairs={{0,4},{4,0},{8,12},{12,8},{16,20},{20,16},{24,28},{28,24},{1,5},{5... | collective-permute-start | bytes 14008328 | tf_op jit(solution)/shard_map/ppermute | solution.py:939
  362.3 22.9 %collective-permute-start.21 = (bf16[2,4,48,768]{3,2,1,0:T(8,128)(2,1)}, bf16[2,4,48,768]{3,2,1,0:T(8,128)(2,1)}, u32[]{:S(2)}, u32[]{:S(2)}) collective-permute-start(bf16[2,4,48,768]{3,2,1,0:T(8,128)(2,1)} %dynamic-slice_bitcast_fusion.6), channel_id=1, source_target_pairs={{0,8},{4,12},{8,0},{12,4},{16,24},{20,28},{24,16},{28,20},{1,9},{5... | collective-permute-start | bytes 1769480 | tf_op jit(solution)/shard_map/ppermute | solution.py:939
  368.9 13.3 %collective-permute-start.8 = (bf16[152,768]{1,0:T(8,128)(2,1)}, bf16[152,768]{1,0:T(8,128)(2,1)S(1)}, u32[]{:S(2)}, u32[]{:S(2)}) collective-permute-start(bf16[152,768]{1,0:T(8,128)(2,1)} %get-tuple-element.80), channel_id=1, source_target_pairs={{0,2},{1,3},{2,0},{3,1},{4,6},{5,7},{6,4},{7,5},{8,10},{9,11},{10,... | collective-permute-start | bytes 700424 | tf_op jit(solution)/shard_map/ppermute | solution.py:935
  385.2 68.7 %collective-permute-start.25 = (bf16[4,48,768]{2,1,0:T(8,128)(2,1)}, bf16[4,48,768]{2,1,0:T(8,128)(2,1)}, u32[]{:S(2)}, u32[]{:S(2)}) collective-permute-start(bf16[4,48,768]{2,1,0:T(8,128)(2,1)} %dynamic-slice_bitcast_fusion.7), channel_id=1, source_target_pairs={{0,8},{4,12},{8,0},{12,4},{16,24},{20,28},{24,16},{28,20},{1,9},{5... | collective-permute-start | bytes 884744 | tf_op jit(solution)/shard_map/ppermute | solution.py:939
  390.0 65.0 %collective-permute-start.22 = (bf16[4,48,768]{2,1,0:T(8,128)(2,1)}, bf16[4,48,768]{2,1,0:T(8,128)(2,1)}, u32[]{:S(2)}, u32[]{:S(2)}) collective-permute-start(bf16[4,48,768]{2,1,0:T(8,128)(2,1)} %dynamic-slice_bitcast_fusion.8), channel_id=1, source_target_pairs={{0,16},{4,20},{8,24},{12,28},{16,0},{20,4},{24,8},{28,12},{1,17},{... | collective-permute-start | bytes 884744 | tf_op jit(solution)/shard_map/ppermute | solution.py:939
  453.9 13.9 %collective-permute-start.14 = (bf16[12,112,256]{2,1,0:T(8,128)(2,1)S(1)}, bf16[12,112,256]{2,1,0:T(8,128)(2,1)S(1)}, u32[]{:S(2)}, u32[]{:S(2)}) collective-permute-start(bf16[12,112,256]{2,1,0:T(8,128)(2,1)S(1)} %copy-done.25), channel_id=1, source_target_pairs={{0,4},{4,0},{8,12},{12,8},{16,20},{20,16},{24,28},{28,24},{1,5},{5... | collective-permute-start | bytes 2064392 | tf_op jit(solution)/shard_map/ppermute | solution.py:939
  456.2 22.0 %collective-permute-start.27 = (bf16[96,768]{1,0:T(8,128)(2,1)S(1)}, bf16[96,768]{1,0:T(8,128)(2,1)S(1)}, u32[]{:S(2)}, u32[]{:S(2)}) collective-permute-start(bf16[96,768]{1,0:T(8,128)(2,1)S(1)} %get-tuple-element.94), channel_id=1, source_target_pairs={{0,2},{1,3},{2,0},{3,1},{4,6},{5,7},{6,4},{7,5},{8,10},{9,11},{10,... | collective-permute-start | bytes 442376 | tf_op jit(solution)/shard_map/ppermute | solution.py:935
  463.7 27.9 %collective-permute-start.33 = (bf16[2,4,96,768]{3,2,1,0:T(8,128)(2,1)S(1)}, bf16[2,4,96,768]{3,2,1,0:T(8,128)(2,1)S(1)}, u32[]{:S(2)}, u32[]{:S(2)}) collective-permute-start(bf16[2,4,96,768]{3,2,1,0:T(8,128)(2,1)S(1)} %dynamic-slice_bitcast_fusion.1), channel_id=1, source_target_pairs={{0,16},{4,20},{8,24},{12,28},{16,0},{20,4},{24,8},{28,12},{1,17},{... | collective-permute-start | bytes 3538952 | tf_op jit(solution)/shard_map/ppermute | solution.py:939
  468.1 29.0 %collective-permute-start.30 = (bf16[2,4,96,768]{3,2,1,0:T(8,128)(2,1)S(1)}, bf16[2,4,96,768]{3,2,1,0:T(8,128)(2,1)}, u32[]{:S(2)}, u32[]{:S(2)}) collective-permute-start(bf16[2,4,96,768]{3,2,1,0:T(8,128)(2,1)S(1)} %dynamic-slice_bitcast_fusion.2), channel_id=1, source_target_pairs={{0,8},{4,12},{8,0},{12,4},{16,24},{20,28},{24,16},{28,20},{1,9},{5... | collective-permute-start | bytes 3538952 | tf_op jit(solution)/shard_map/ppermute | solution.py:939
  491.9 63.1 %collective-permute-start.34 = (bf16[4,96,768]{2,1,0:T(8,128)(2,1)S(1)}, bf16[4,96,768]{2,1,0:T(8,128)(2,1)S(1)}, u32[]{:S(2)}, u32[]{:S(2)}) collective-permute-start(bf16[4,96,768]{2,1,0:T(8,128)(2,1)S(1)} %dynamic-slice_bitcast_fusion.3), channel_id=1, source_target_pairs={{0,8},{4,12},{8,0},{12,4},{16,24},{20,28},{24,16},{28,20},{1,9},{5... | collective-permute-start | bytes 1769480 | tf_op jit(solution)/shard_map/ppermute | solution.py:939
  498.8 59.3 %collective-permute-start.31 = (bf16[4,96,768]{2,1,0:T(8,128)(2,1)S(1)}, bf16[4,96,768]{2,1,0:T(8,128)(2,1)S(1)}, u32[]{:S(2)}, u32[]{:S(2)}) collective-permute-start(bf16[4,96,768]{2,1,0:T(8,128)(2,1)S(1)} %dynamic-slice_bitcast_fusion.4), channel_id=1, source_target_pairs={{0,16},{4,20},{8,24},{12,28},{16,0},{20,4},{24,8},{28,12},{1,17},{... | collective-permute-start | bytes 1769480 | tf_op jit(solution)/shard_map/ppermute | solution.py:939
  558.3 15.4 %collective-permute-start.35 = (bf16[192,768]{1,0:T(8,128)(2,1)S(1)}, bf16[192,768]{1,0:T(8,128)(2,1)S(1)}, u32[]{:S(2)}, u32[]{:S(2)}) collective-permute-start(bf16[192,768]{1,0:T(8,128)(2,1)S(1)} %get-tuple-element.72), channel_id=1, source_target_pairs={{0,1},{1,2},{2,3},{3,0},{4,5},{5,6},{6,7},{7,4},{8,9},{9,10},{10,1... | collective-permute-start | bytes 884744 | tf_op jit(solution)/shard_map/ppermute | solution.py:935
  560.3 21.4 %collective-permute-start.36 = (bf16[192,768]{1,0:T(8,128)(2,1)S(1)}, bf16[192,768]{1,0:T(8,128)(2,1)S(1)}, u32[]{:S(2)}, u32[]{:S(2)}) collective-permute-start(bf16[192,768]{1,0:T(8,128)(2,1)S(1)} %get-tuple-element.73), channel_id=1, source_target_pairs={{0,2},{1,3},{2,0},{3,1},{4,6},{5,7},{6,4},{7,5},{8,10},{9,11},{10,... | collective-permute-start | bytes 884744 | tf_op jit(solution)/shard_map/ppermute | solution.py:935
  560.3 21.4 %collective-permute-start.37 = (bf16[192,768]{1,0:T(8,128)(2,1)S(1)}, bf16[192,768]{1,0:T(8,128)(2,1)S(1)}, u32[]{:S(2)}, u32[]{:S(2)}) collective-permute-start(bf16[192,768]{1,0:T(8,128)(2,1)S(1)} %get-tuple-element.74), channel_id=1, source_target_pairs={{0,3},{1,0},{2,1},{3,2},{4,7},{5,4},{6,5},{7,6},{8,11},{9,8},{10,9... | collective-permute-start | bytes 884744 | tf_op jit(solution)/shard_map/ppermute | solution.py:935
  571.7 15.1 %collective-permute-start.18 = (f32[468,128]{1,0:T(8,128)S(1)}, f32[468,128]{1,0:T(8,128)S(1)}, u32[]{:S(2)}, u32[]{:S(2)}) collective-permute-start(f32[468,128]{1,0:T(8,128)S(1)} %add.343), channel_id=1, source_target_pairs={{0,1},{1,0},{2,3},{3,2},{4,5},{5,4},{6,7},{7,6},{8,9},{9,8},{10,11... | collective-permute-start | bytes 718856 | tf_op jit(solution)/shard_map/ppermute | solution.py:995
  586.7 13.9 %collective-permute-start.19 = (f32[468,128]{1,0:T(8,128)S(1)}, f32[468,128]{1,0:T(8,128)S(1)}, u32[]{:S(2)}, u32[]{:S(2)}) collective-permute-start(f32[468,128]{1,0:T(8,128)S(1)} %add.344), channel_id=1, source_target_pairs={{0,2},{1,3},{2,0},{3,1},{4,6},{5,7},{6,4},{7,5},{8,10},{9,11},{10,... | collective-permute-start | bytes 718856 | tf_op jit(solution)/shard_map/ppermute | solution.py:995
  (66 other events, 604.1 us)

commit v2 on v0

--- a/solution.py
+++ b/solution.py
@@ -1,6 +1,10 @@
+import functools
+
 import jax
 import jax.numpy as jnp
 from jax import lax
+from jax.experimental import pallas as pl
+from jax.experimental.pallas import tpu as pltpu
 from jax.sharding import PartitionSpec as P
 
 HEAD = 64
@@ -350,9 +354,1191 @@
     )
 
 
+NT = (((1,), (1,)), ((), ()))
+TN = (((0,), (0,)), ((), ()))
+WIDE = jnp.float32
+NARROW = jnp.bfloat16
+LANES = 128
+TERM = jnp.float8_e4m3fn
+MEGA = 1 << 20
+
+
+def round_up(count, step):
+    return -(-count // step) * step
+
+
+def params(limit, *names):
+    return pltpu.CompilerParams(vmem_limit_bytes=limit * MEGA, dimension_semantics=("arbitrary",))
+
+
+def cost(micros):
+    return pl.CostEstimate(flops=int(micros * 1.15e9), bytes_accessed=int(micros * 3.2e6), transcendentals=0)
+
+
+def whole(*shape):
+    return pl.BlockSpec(shape, lambda *steps: (0,) * len(shape), pipeline_mode=pl.Buffered(1))
+
+
+def whole_of(value):
+    return whole(*value.shape)
+
+
+BLK, CORE = 0, 1
+
+
+def assemble(held_ref, me, part, mine, gots, small_ref, large, small):
+    held_ref[...] = jnp.zeros_like(held_ref)
+    size = len(gots) + 1
+    for shift, piece in enumerate([mine] + [got[...] for got in gots]):
+        start = pl.multiple_of(lax.rem(me + (size - shift), size) * part, 8)
+        held_ref[pl.ds(start, piece.shape[0]), :] = piece.astype(WIDE)
+    for number in range(small_ref.shape[0]):
+        start = large + number * small
+        held_ref[start : start + small_ref.shape[1], :] = small_ref[number].astype(WIDE)
+
+
+def dismantle(held_ref, me, part, piece_refs, small_ref, large):
+    size = len(piece_refs)
+    for shift, piece_ref in enumerate(piece_refs):
+        start = pl.multiple_of(lax.rem(me + shift, size) * part, 8)
+        piece_ref[...] = held_ref[pl.ds(start, part), :].astype(NARROW)
+    small_ref[...] = held_ref[large:, :].astype(NARROW)
+
+
+def deal_rows(value, half, is_first, mine_ref, theirs_ref):
+    for number in range(value.shape[0] // (2 * half)):
+        start = 2 * half * number
+        first, second = value[start : start + half], value[start + half : start + 2 * half]
+        rows = slice(half * number, half * number + half)
+        mine_ref[rows, :] = jnp.where(is_first, first, second)
+        theirs_ref[rows, :] = jnp.where(is_first, second, first)
+
+
+def row_norm(values):
+    center = values - jnp.mean(values, -1, keepdims=True)
+    spread = jnp.mean(center * center, -1, keepdims=True)
+    inverse = lax.rsqrt(spread + EPSILON)
+    return center * inverse, inverse
+
+
+def norm_backward(grad, normal, inverse, gain):
+    scaled = grad * gain
+    first = jnp.mean(scaled, -1, keepdims=True)
+    second = jnp.mean(scaled * normal, -1, keepdims=True)
+    return inverse * (scaled - first - normal * second)
+
+
+def bias_kernel(heads, groups, place_ref, table_ref, index_ref, out_ref):
+    rows = index_ref.shape[0]
+    for first in range(0, rows, 16):
+        found = []
+        for half in (0, 8):
+            index = index_ref[first + half : first + half + 8, :]
+            low = lax.bitwise_and(index, LANES - 1)
+            high = lax.shift_right_logical(index, 7)
+            picked = [None] * heads
+            for group in range(groups):
+                here = high == group
+                for head in range(heads):
+                    value = jnp.take_along_axis(table_ref[group * heads + head], low, axis=1)
+                    picked[head] = value if group == 0 else jnp.where(here, value, picked[head])
+            found.append(picked)
+        for head in range(heads):
+            both = jnp.concatenate([found[0][head], found[1][head]], 0)
+            out_ref[head, first : first + 16, :] = both.astype(NARROW)
+
+
+def spread_kernel(pieces, length, piece, index_ref, out_ref):
+    out_ref[...] = jnp.zeros_like(out_ref)
+    turned = jnp.transpose(index_ref[...])
+    for key in range(pieces):
+        for query in range(pieces):
+            out_ref[key * piece : key * piece + length, query * piece : query * piece + length] = turned[
+                key * length : (key + 1) * length, query * length : (query + 1) * length
+            ]
+
+
+def spread_index(index, pieces, piece, rows, lanes):
+    length = index.shape[0] // pieces
+    return pl.pallas_call(
+        functools.partial(spread_kernel, pieces, length, piece),
+        out_shape=jax.ShapeDtypeStruct((rows, lanes), jnp.int32),
+        compiler_params=pltpu.CompilerParams(vmem_limit_bytes=32 * MEGA),
+        cost_estimate=cost(rows * lanes * 1e-5),
+        name="spread_index",
+    )(index)
+
+
+def bias_lookup(place, table, index, shares):
+    heads = table.shape[1]
+    groups = round_up(table.shape[0], LANES) // LANES
+    table = jnp.pad(table.astype(WIDE), ((0, groups * LANES - table.shape[0]), (0, 0)))
+    table = jnp.transpose(table.reshape(groups, LANES, heads), (0, 2, 1)).reshape(-1, 1, LANES)
+    table = jnp.broadcast_to(table, (groups * heads, 8, LANES))
+    rows, lanes = index.shape
+    rows //= shares
+    return pl.pallas_call(
+        functools.partial(bias_kernel, heads, groups),
+        grid_spec=pltpu.PrefetchScalarGridSpec(
+            num_scalar_prefetch=1,
+            grid=(lanes // LANES,),
+            in_specs=[
+                pl.BlockSpec((groups * heads, 8, LANES), lambda i, place: (0, 0, 0)),
+                pl.BlockSpec((rows, LANES), lambda i, place: (place[CORE] if shares > 1 else 0, i)),
+            ],
+            out_specs=pl.BlockSpec((heads, rows, LANES), lambda i, place: (0, 0, i)),
+        ),
+        out_shape=jax.ShapeDtypeStruct((heads, rows, lanes), NARROW),
+        compiler_params=params(32),
+        cost_estimate=cost(rows * lanes * groups * heads * 6e-7),
+        name="bias_lookup",
+    )(place, table, index)
+
+
+def qkv_kernel(
+    part,
+    large,
+    small,
+    gots,
+    place_ref,
+    mine_ref,
+    *refs,
+):
+    got_refs = refs[:gots]
+    small_ref, gain_ref, shift_ref, weight_ref, bias_ref, x_ref, h_ref, p_ref, held_ref = refs[gots:]
+
+    @pl.when(pl.program_id(0) == 0)
+    def _():
+        assemble(held_ref, place_ref[BLK], part, mine_ref[...], got_refs, small_ref, large, small)
+        x = held_ref[...]
+        x_ref[...] = x.astype(NARROW)
+        normal, _ = row_norm(x)
+        h_ref[...] = (normal * gain_ref[...] + shift_ref[...]).astype(NARROW)
+
+    product = jnp.dot(h_ref[...], weight_ref[...], preferred_element_type=WIDE)
+    p_ref[...] = (product + bias_ref[...]).astype(NARROW)
+
+
+def qkv_forward(place, pieces, gots, smalls, gain, shift, weight, bias, part, large, small):
+    width = smalls.shape[2]
+    tokens = large + smalls.shape[0] * small
+    total = weight.shape[1]
+    return pl.pallas_call(
+        functools.partial(qkv_kernel, part, large, small, len(gots)),
+        grid_spec=pltpu.PrefetchScalarGridSpec(
+            num_scalar_prefetch=1,
+            grid=(total // width,),
+            in_specs=[pl.BlockSpec((None,) + pieces.shape[1:], lambda i, place: (place[BLK], 0, 0))]
+            + [whole_of(got) for got in gots]
+            + [
+                whole_of(smalls),
+                whole(1, width),
+                whole(1, width),
+                pl.BlockSpec((width, width), lambda i, place: (0, i)),
+                pl.BlockSpec((1, width), lambda i, place: (0, i)),
+            ],
+            out_specs=[
+                whole(tokens, width),
+                whole(tokens, width),
+                pl.BlockSpec((tokens, width), lambda i, place: (0, i)),
+            ],
+            scratch_shapes=[pltpu.VMEM((tokens, width), WIDE)],
+        ),
+        out_shape=[
+            jax.ShapeDtypeStruct((tokens, width), NARROW),
+            jax.ShapeDtypeStruct((tokens, width), NARROW),
+            jax.ShapeDtypeStruct((tokens, total), NARROW),
+        ],
+        compiler_params=params(48),
+        cost_estimate=cost(tokens * width * total * 5e-9),
+        name="qkv_forward",
+    )(place, pieces, *gots, smalls, gain, shift, weight, bias)
+
+
+def head_parts(first_half, value, other):
+    return jnp.where(first_half, value, other), jnp.where(first_half, other, value)
+
+
+def attention_forward_kernel(
+    images,
+    place_ref,
+    q_ref,
+    k_ref,
+    v_ref,
+    mask_ref,
+    own_bias_ref,
+    other_bias_ref,
+    small_bias_ref,
+    o_ref,
+    large_p_ref,
+    small_p_ref,
+):
+    is_first = place_ref[CORE] == 0
+    lane = lax.broadcasted_iota(jnp.int32, (1, LANES), 1)
+    first_half = lane < HEAD
+    for number, (start, rows) in enumerate(images):
+        here = slice(start, start + rows)
+        query = q_ref[here, :] * jnp.asarray(HEAD ** (-0.5), NARROW)
+        ones = jnp.where(lane % HEAD == 0, 1.0, 0.0).astype(NARROW)
+        ones = jnp.broadcast_to(ones, query.shape)
+        queries = head_parts(first_half, query, ones)
+        keys = head_parts(first_half, k_ref[here, :], mask_ref[here, :])
+        value = v_ref[here, :]
+        outs = []
+        for head in range(2):
+            if number == 0:
+                own, other = own_bias_ref[head, :, :rows], other_bias_ref[head, :, :rows]
+                bias = jnp.concatenate([jnp.where(is_first, own, other), jnp.where(is_first, other, own)], 0)
+            else:
+                bias = small_bias_ref[head, :rows, :rows]
+            scores = lax.dot_general(keys[head], queries[head], NT, preferred_element_type=WIDE)
+            scores = scores + bias.astype(WIDE)
+            weights = jnp.exp(scores - jnp.max(scores, 0, keepdims=True))
+            probs = (weights * (1.0 / jnp.sum(weights, 0, keepdims=True))).astype(NARROW)
+            if number == 0:
+                large_p_ref[head] = probs
+            else:
+                small_p_ref[head, number - 1] = probs
+            outs.append(lax.dot_general(probs, value, TN, preferred_element_type=WIDE))
+        o_ref[here, :] = jnp.where(first_half, outs[0], outs[1]).astype(NARROW)
+
+
+def attention_forward(place, p, mask, own_bias, other_bias, small_bias, images):
+    tokens = p.shape[0]
+    heads = small_bias.shape[0]
+    pairs = heads // 2
+    large, small, smalls = images[0][1], images[1][1], len(images) - 1
+    area = large * large + smalls * small * small
+
+    def column(offset):
+        return pl.BlockSpec((tokens, LANES), lambda i, place: (0, offset + i))
+
+    def by_pair(*shape):
+        return pl.BlockSpec((2,) + shape, lambda i, place: (i,) + (0,) * len(shape))
+
+    return pl.pallas_call(
+        functools.partial(attention_forward_kernel, images),
+        grid_spec=pltpu.PrefetchScalarGridSpec(
+            num_scalar_prefetch=1,
+            grid=(pairs,),
+            in_specs=[
+                column(0),
+                column(pairs),
+                column(2 * pairs),
+                pl.BlockSpec((tokens, LANES), lambda i, place: (0, 0)),
+                by_pair(*own_bias.shape[1:]),
+                by_pair(*other_bias.shape[1:]),
+                by_pair(*small_bias.shape[1:]),
+            ],
+            out_specs=[
+                column(0),
+                by_pair(large, large),
+                by_pair(smalls, small, small),
+            ],
+        ),
+        out_shape=[
+            jax.ShapeDtypeStruct((tokens, heads * HEAD), NARROW),
+            jax.ShapeDtypeStruct((heads, large, large), NARROW),
+            jax.ShapeDtypeStruct((heads, smalls, small, small), NARROW),
+        ],
+        compiler_params=params(60),
+        cost_estimate=cost(heads * area * 3.8e-6),
+        name="attention_forward",
+    )(place, p, p, p, mask, own_bias, other_bias, small_bias)
+
+
+def attention_backward_kernel(
+    images,
+    place_ref,
+    q_ref,
+    k_ref,
+    v_ref,
+    do_ref,
+    o_ref,
+    large_p_ref,
+    small_p_ref,
+    dp_ref,
+    mine_ref,
+    theirs_ref,
+):
+    is_first = place_ref[CORE] == 0
+    mine_ref[...] = jnp.zeros_like(mine_ref)
+    theirs_ref[...] = jnp.zeros_like(theirs_ref)
+    large_half = images[0][1] // 2
+
+    def deal(head, grad_scores, start, half):
+        count, lanes = grad_scores.shape
+        lower = grad_scores[:half]
+        upper = grad_scores[half:]
+        rest = count - half
+        rows = slice(start, start + rest)
+        mine_ref[head, rows, :lanes] = jnp.where(is_first, lower[:rest], upper)
+        theirs_ref[head, rows, :lanes] = jnp.where(is_first, upper, lower[:rest])
+        if rest < half:
+            zeros = jnp.zeros((half - rest, lanes), NARROW)
+            rows = slice(start + rest, start + half)
+            mine_ref[head, rows, :lanes] = jnp.where(is_first, lower[rest:], zeros)
+            theirs_ref[head, rows, :lanes] = jnp.where(is_first, zeros, lower[rest:])
+
+    lane = lax.broadcasted_iota(jnp.int32, (1, LANES), 1)
+    first_half = lane < HEAD
+    small_sum = [None, None]
+    scale = HEAD ** (-0.5)
+    for number, (start, rows) in enumerate(images):
+        here = slice(start, start + rows)
+        query = q_ref[here, :] * jnp.asarray(scale, NARROW)
+        key = k_ref[here, :]
+        value = v_ref[here, :]
+        grad = do_ref[here, :]
+        product = jnp.transpose(grad.astype(WIDE) * o_ref[here, :].astype(WIDE))
+        grads = head_parts(first_half, grad, jnp.zeros_like(grad))
+        parts = []
+        for head in range(2):
+            inner = jnp.sum(product[head * HEAD : (head + 1) * HEAD], 0, keepdims=True)
+            probs = large_p_ref[head] if number == 0 else small_p_ref[head, number - 1]
+            grad_probs = lax.dot_general(value, grads[head], NT, preferred_element_type=WIDE)
+            grad_scores = (probs.astype(WIDE) * (grad_probs - inner)).astype(NARROW)
+            if number == 0:
+                deal(head, grad_scores, 0, large_half)
+            elif small_sum[head] is None:
+                small_sum[head] = grad_scores.astype(WIDE)
+            else:
+                small_sum[head] = small_sum[head] + grad_scores.astype(WIDE)
+            parts.append(
+                (
+                    lax.dot_general(grad_scores, key, TN, preferred_element_type=WIDE) * scale,
+                    jnp.dot(grad_scores, query, preferred_element_type=WIDE),
+                    jnp.dot(probs, grad, preferred_element_type=WIDE),
+                )
+            )
+        for which in range(3):
+            dp_ref[which, here, :] = jnp.where(first_half, parts[0][which], parts[1][which]).astype(NARROW)
+    for head in range(2):
+        deal(head, small_sum[head].astype(NARROW), large_half, mine_ref.shape[1] - large_half)
+
+
+def attention_backward(place, p, grad_out, out, large_p, small_p, images, share, first, count):
+    tokens = p.shape[0]
+    pairs = large_p.shape[0] // 2
+    large, small, smalls = images[0][1], images[1][1], len(images) - 1
+    area = large * large + smalls * small * small
+
+    def column(offset):
+        return pl.BlockSpec((tokens, LANES), lambda i, place: (0, offset + first + i))
+
+    def by_pair(*shape):
+        return pl.BlockSpec((2,) + shape, lambda i, place: (first + i,) + (0,) * len(shape))
+
+    share_spec = pl.BlockSpec((2,) + share, lambda i, place: (i, 0, 0))
+    return pl.pallas_call(
+        functools.partial(attention_backward_kernel, images),
+        grid_spec=pltpu.PrefetchScalarGridSpec(
+            num_scalar_prefetch=1,
+            grid=(count,),
+            in_specs=[
+                column(0),
+                column(pairs),
+                column(2 * pairs),
+                column(0),
+                column(0),
+                by_pair(large, large),
+                by_pair(smalls, small, small),
+            ],
+            out_specs=[pl.BlockSpec((3, tokens, LANES), lambda i, place: (0, 0, i)), share_spec, share_spec],
+        ),
+        out_shape=[jax.ShapeDtypeStruct((3, tokens, count * LANES), NARROW)]
+        + [jax.ShapeDtypeStruct((2 * count,) + share, NARROW)] * 2,
+        compiler_params=params(60),
+        cost_estimate=cost(2 * count * area * 4.2e-6),
+        name="attention_backward",
+    )(place, p, p, p, grad_out, out, large_p, small_p)
+
+
+def gelu_parts(value):
+    size = jnp.abs(value)
+    inverse = 1.0 / (1.0 + (0.3275911 * 0.7071067811865476) * size)
+    series = inverse * (
+        0.127414796
+        + inverse
+        * (-0.142248368 + inverse * (0.7107068705 + inverse * (-0.7265760135 + inverse * 0.5307027145)))
+    )
+    bell = jnp.exp(-0.5 * value * value)
+    tail = series * bell
+    share = jnp.where(value < 0, tail, 1.0 - tail)
+    return value * share, share + value * (bell * 0.3989422804014327)
+
+
+def mlp_kernel(
+    part,
+    large,
+    small,
+    share,
+    gots,
+    place_ref,
+    mine_ref,
+    *refs,
+):
+    got_refs, refs = refs[:gots], refs[gots:]
+    small_ref, o_ref, x_ref, proj_ref, vector_ref, inner_ref, inner_bias_ref, outer_ref = refs[:8]
+    back_refs, refs = refs[8 : 9 + gots], refs[9 + gots :]
+    small_back_ref, dm_ref, do_ref, weights_ref, dvector_ref, dbias_ref = refs[:6]
+    r_ref, g_ref, dy_ref, dz_ref, z_ref, dg_ref, wide_ref, tall_ref, sems = refs[6:]
+    step = pl.program_id(0)
+    steps = pl.num_programs(0) - 1
+    me = place_ref[BLK]
+    proj_bias, attn_scale, gain, shift, outer_bias, mlp_scale = (vector_ref[i : i + 1, :] for i in range(6))
+    tokens = x_ref.shape[0]
+    chunk = next(c for c in (128, 64, 32, 16) if tokens % c == 0)
+    width = x_ref.shape[1]
+    pieces = tall_ref.shape[1] // width
+
+    def wide_copy(number):
+        columns = pl.ds(pl.multiple_of(number * width, LANES), width)
+        return pltpu.make_async_copy(wide_ref, weights_ref.at[:, columns], sems.at[0])
+
+    def tall_copy(number):
+        count = tall_ref.shape[0]
+        rows = pl.ds(pl.multiple_of(number * count, 16), count)
+        columns = slice(weights_ref.shape[1] - tall_ref.shape[1], weights_ref.shape[1])
+        return pltpu.make_async_copy(tall_ref, weights_ref.at[rows, columns], sems.at[1])
+
+    @pl.when(step == 0)
+    def _():
+        r_ref[...] = jnp.dot(o_ref[...], proj_ref[...], preferred_element_type=WIDE) + proj_bias
+        assemble(z_ref, me, part, mine_ref[...], got_refs, small_ref, large, small)
+
+        @pl.loop(0, tokens // chunk)
+        def _(i):
+            rows = pl.ds(pl.multiple_of(i * chunk, chunk), chunk)
+            middle = x_ref[rows, :].astype(WIDE) + attn_scale * r_ref[rows, :]
+            normal, _ = row_norm(middle)
+            g_ref[rows, :] = (normal * gain + shift).astype(NARROW)
+            dy = z_ref[rows, :]
+            dy_ref[rows, :] = dy.astype(NARROW)
+            dz_ref[rows, :] = (mlp_scale * dy).astype(NARROW)
+
+    @pl.when(step < pl.num_programs(0) - 1)
+    def _():
+        pre = jnp.dot(g_ref[...], inner_ref[...], preferred_element_type=WIDE) + inner_bias_ref[...]
+        active, slope = gelu_parts(pre)
+        active = active.astype(NARROW)
+        dz = dz_ref[...]
+        dactive = lax.dot_general(dz, outer_ref[...], NT, preferred_element_type=WIDE)
+        dpre = (dactive * slope).astype(NARROW)
+        douter = lax.dot_general(active, dz, TN, preferred_element_type=WIDE)
+        dinner = lax.dot_general(g_ref[...], dpre, TN, preferred_element_type=WIDE).astype(NARROW)
+
+        @pl.when(step > 0)
+        def _():
+            wide_copy(step - 1).wait()
+            tall_copy(step - 1).wait()
+
+        wide_ref[...] = dinner
+        wide_copy(step).start()
+        douter = douter.reshape(-1, pieces, share, width)
+        for piece in range(pieces):
+            tall_ref[:, piece * width : (piece + 1) * width] = (
+                douter[:, piece].reshape(tall_ref.shape[0], width).astype(NARROW)
+            )
+        tall_copy(step).start()
+        dbias_ref[...] = jnp.sum(dpre.astype(WIDE), 0, keepdims=True)
+        z = jnp.dot(active, outer_ref[...], preferred_element_type=WIDE)
+        dg = lax.dot_general(dpre, inner_ref[...], NT, preferred_element_type=WIDE)
+
+        @pl.when(step == 0)
+        def _():
+            z_ref[...] = z
+            dg_ref[...] = dg
+
+        @pl.when(step > 0)
+        def _():
+            z_ref[...] += z
+            dg_ref[...] += dg
+
+    @pl.when(step == pl.num_programs(0) - 1)
+    def _():
+        dvector_ref[...] = jnp.zeros_like(dvector_ref)
+
+        @pl.loop(0, tokens // chunk)
+        def _(i):
+            rows = pl.ds(pl.multiple_of(i * chunk, chunk), chunk)
+            branch = r_ref[rows, :]
+            middle = x_ref[rows, :].astype(WIDE) + attn_scale * branch
+            normal, inverse = row_norm(middle)
+            outer = z_ref[rows, :] + outer_bias
+            dy = dy_ref[rows, :].astype(WIDE)
+            r_ref[rows, :] = middle + mlp_scale * outer
+            grad = dg_ref[rows, :]
+            dm = dy + norm_backward(grad, normal, inverse, gain)
+            dm_ref[rows, :] = dm
+            dr = (attn_scale * dm).astype(NARROW)
+            g_ref[rows, :] = dr
+            sums = [
+                dy * outer,
+                dz_ref[rows, :].astype(WIDE),
+                grad * normal,
+                grad,
+                dm * branch,
+                dr.astype(WIDE),
+            ]
+            for place, term in enumerate(sums):
+                dvector_ref[place : place + 1, :] += jnp.sum(term, 0, keepdims=True)
+
+        dr = g_ref[...]
+        dproj = lax.dot_general(o_ref[...], dr, TN, preferred_element_type=WIDE).astype(NARROW)
+        wide_copy(steps - 1).wait()
+        tall_copy(steps - 1).wait()
+        wide_ref[...] = dproj
+        wide_copy(steps).start()
+        do_ref[...] = lax.dot_general(dr, proj_ref[...], NT, preferred_element_type=WIDE).astype(NARROW)
+        dismantle(r_ref, me, part, back_refs, small_back_ref, large)
+        wide_copy(steps).wait()
+
+
+def mlp_pass(place, pieces, gots, smalls, out, x, proj, vectors, inner, inner_bias, outer, part, large, small, devices):
+    tokens, width = x.shape
+    hidden = inner.shape[1]
+    steps = hidden // width
+    blk = len(gots) + 1
+    share = width // devices
+    tall = steps * width
+
+    def feed(i):
+        return jnp.minimum(i, steps - 1)
+
+    shapes = [jax.ShapeDtypeStruct((part, width), NARROW)] * blk + [
+        jax.ShapeDtypeStruct((tokens - large, width), NARROW),
+        jax.ShapeDtypeStruct((tokens, width), WIDE),
+        jax.ShapeDtypeStruct((tokens, width), NARROW),
+        jax.ShapeDtypeStruct((width, hidden + width + tall), NARROW),
+        jax.ShapeDtypeStruct((8, width), WIDE),
+        jax.ShapeDtypeStruct((1, hidden), WIDE),
+    ]
+    return pl.pallas_call(
+        functools.partial(mlp_kernel, part, large, small, share, len(gots)),
+        grid_spec=pltpu.PrefetchScalarGridSpec(
+            num_scalar_prefetch=1,
+            grid=(steps + 1,),
+            in_specs=[
+                pl.BlockSpec(
+                    (None,) + pieces.shape[1:],
+                    lambda i, place: (place[BLK], 0, 0),
+                    pipeline_mode=pl.Buffered(1),
+                )
+            ]
+            + [whole_of(got) for got in gots]
+            + [
+                whole_of(smalls),
+                whole(tokens, width),
+                whole(tokens, width),
+                whole(width, width),
+                whole(8, width),
+                pl.BlockSpec((width, width), lambda i, place: (0, feed(i))),
+                pl.BlockSpec((1, width), lambda i, place: (0, feed(i))),
+                pl.BlockSpec((width, width), lambda i, place: (feed(i), 0)),
+            ],
+            out_specs=[whole(part, width)] * blk
+            + [
+                whole(tokens - large, width),
+                whole(tokens, width),
+                whole(tokens, width),
+                pl.BlockSpec(memory_space=pl.ANY),
+                whole(8, width),
+                pl.BlockSpec((1, width), lambda i, place: (0, feed(i))),
+            ],
+            scratch_shapes=[
+                pltpu.VMEM((tokens, width), WIDE),
+                pltpu.VMEM((tokens, width), NARROW),
+                pltpu.VMEM((tokens, width), NARROW),
+                pltpu.VMEM((tokens, width), NARROW),
+                pltpu.VMEM((tokens, width), WIDE),
+                pltpu.VMEM((tokens, width), WIDE),
+                pltpu.VMEM((width, width), NARROW),
+                pltpu.VMEM((width // steps, tall), NARROW),
+                pltpu.SemaphoreType.DMA((2,)),
+            ],
+        ),
+        out_shape=shapes,
+        compiler_params=params(60),
+        cost_estimate=cost(tokens * width * hidden * 2.4e-8),
+        name="mlp_pass",
+    )(place, pieces, *gots, smalls, out, x, proj, vectors, inner, inner_bias, outer)
+
+
+def qkv_backward_kernel(part, large, half, pieces, place_ref, *refs):
+    result_refs, refs = refs[:pieces], refs[pieces:]
+    dp_ref, h_ref, x_ref, dm_ref, gain_ref, weight_ref, mine_ref, theirs_ref = refs[:8]
+    back_refs = refs[8 : 8 + pieces]
+    small_back_ref, dvector_ref, dh_ref = refs[8 + pieces :]
+    step = pl.program_id(0)
+    grad = dp_ref[0]
+    dweight = lax.dot_general(h_ref[...], grad, TN, preferred_element_type=WIDE).astype(NARROW)
+    deal_rows(dweight, half, place_ref[CORE] == 0, mine_ref, theirs_ref)
+    term = lax.dot_general(grad, weight_ref[...], NT, preferred_element_type=WIDE)
+    column_sum = jnp.sum(grad.astype(WIDE), 0, keepdims=True)
+    tokens = x_ref.shape[0]
+    chunk = next(c for c in (128, 64, 32, 16) if tokens % c == 0)
+
+    @pl.when(step == 0)
+    def _():
+        dvector_ref[...] = jnp.zeros_like(dvector_ref)
+        dh_ref[...] = term
+        dvector_ref[0:1, :] = column_sum
+
+    @pl.when(step > 0)
+    def _():
+        dh_ref[...] += term
+
+    @pl.when(step == pl.num_programs(0) - 1)
+    def _():
+        dvector_ref[1:2, :] = column_sum
+
+        @pl.loop(0, tokens // chunk)
+        def _(i):
+            rows = pl.ds(pl.multiple_of(i * chunk, chunk), chunk)
+            normal, inverse = row_norm(x_ref[rows, :].astype(WIDE))
+            dh = dh_ref[rows, :]
+            dh_ref[rows, :] = dm_ref[rows, :] + norm_backward(dh, normal, inverse, gain_ref[...])
+            dvector_ref[2:3, :] += jnp.sum(dh * normal, 0, keepdims=True)
+            dvector_ref[3:4, :] += jnp.sum(dh, 0, keepdims=True)
+
+        for back_ref, result_ref in zip(back_refs, result_refs):
+            back_ref[0] = result_ref[...]
+        dismantle(dh_ref, place_ref[BLK], part, [back_ref.at[1] for back_ref in back_refs], small_back_ref, large)
+
+
+def qkv_backward(place, results, dp, h, x, dm, gain, weight, part, large, devices):
+    blk = len(results)
+    tokens, width = x.shape
+    half_spec = pl.BlockSpec((width // 2, width), lambda i, place: (0, i))
+    return pl.pallas_call(
+        functools.partial(qkv_backward_kernel, part, large, blk * width // devices, blk),
+        grid_spec=pltpu.PrefetchScalarGridSpec(
+            num_scalar_prefetch=1,
+            grid=(3,),
+            in_specs=[whole_of(result) for result in results]
+            + [
+                pl.BlockSpec((1, tokens, width), lambda i, place: (i, 0, 0)),
+                whole(tokens, width),
+                whole(tokens, width),
+                whole(tokens, width),
+                whole(1, width),
+                pl.BlockSpec((width, width), lambda i, place: (0, i)),
+            ],
+            out_specs=[half_spec, half_spec]
+            + [whole(2, part, width)] * blk
+            + [whole(tokens - large, width), whole(8, width)],
+            scratch_shapes=[pltpu.VMEM((tokens, width), WIDE)],
+        ),
+        out_shape=[jax.ShapeDtypeStruct((width // 2, 3 * width), NARROW)] * 2
+        + [jax.ShapeDtypeStruct((2, part, width), NARROW)] * blk
+        + [
+            jax.ShapeDtypeStruct((tokens - large, width), NARROW),
+            jax.ShapeDtypeStruct((8, width), WIDE),
+        ],
+        compiler_params=params(48),
+        cost_estimate=cost(tokens * width * width * 2.5e-8),
+        name="qkv_backward",
+    )(place, *results, dp, h, x, dm, gain, weight)
+
+
+def place_kernel(rows, small, smalls, pieces, place_ref, *refs):
+    backs, refs = refs[:pieces], refs[pieces:]
+    still, outs = refs[:2], refs[2:]
+    me = place_ref[BLK]
+    for which in range(2):
+        for shift in range(pieces):
+            source = lax.rem(me + (pieces - shift), pieces)
+            outs[2 * which][pl.ds(source, 1)] = backs[shift][which, :rows, :][None]
+        for number in range(smalls):
+            out_ref = outs[2 * which + 1]
+            out_ref[number] = still[which][number * small : number * small + out_ref.shape[1], :]
+
+
+def place_results(place, backs, still, rows, small, smalls, small_rows):
+    width = still[0].shape[1]
+    pieces = len(backs)
+    shapes = [(pieces, rows, width), (smalls, small_rows, width)] * 2
+    return pl.pallas_call(
+        functools.partial(place_kernel, rows, small, smalls, pieces),
+        grid_spec=pltpu.PrefetchScalarGridSpec(
+            num_scalar_prefetch=1,
+            grid=(1,),
+            in_specs=[whole_of(value) for value in backs + still],
+            out_specs=[whole(*shape) for shape in shapes],
+        ),
+        out_shape=[jax.ShapeDtypeStruct(shape, NARROW) for shape in shapes],
+        compiler_params=params(32),
+        cost_estimate=cost(3),
+        name="place_results",
+    )(place, *backs, *still)
+
+
+TABLE_LANES = 256
+
+
+def table_rows(shares, index_ref, out_ref, turned_ref, left_ref, right_ref, batch):
+    rows, lanes = index_ref.shape
+    groups = out_ref.shape[0] // 32
+    top = jnp.zeros((8, lanes), WIDE)
+    head = 0
+    for own_ref, other_ref in shares:
+        for number in range(own_ref.shape[0]):
+            value = own_ref[number].astype(WIDE) + other_ref[number].astype(WIDE)
+            turned_ref[:, head, :lanes] = value
+            size = jnp.abs(value)
+            for first in range(0, rows, 8):
+                top = jnp.maximum(top, size[first : first + 8])
+            head += 1
+    peak = jnp.maximum(jnp.max(top, keepdims=True), 1e-30)
+    scale = 256.0 / peak
+    back = peak * (1.0 / 256.0)
+    zero = jnp.zeros((), TERM)
+    one = jnp.ones((), TERM)
+    codes = (lax.broadcasted_iota(jnp.int32, (TABLE_LANES, LANES), 0) - 128).astype(jnp.int8)
+    columns = slice(0, batch * lanes)
+
+    def some_rows(part, carry):
+        for within in range(batch):
+            row = part * batch + within
+            index = index_ref[pl.ds(row, 1), :]
+            low = lax.bitwise_and(index, TABLE_LANES - 1) - 128
+            high = lax.shift_right_logical(index, 8)
+            for first in range(0, lanes, LANES):
+                here = slice(first, first + LANES)
+                there = slice(within * lanes + first, within * lanes + first + LANES)
+                chosen = jnp.broadcast_to(low[:, here], (TABLE_LANES, LANES)).astype(jnp.int8)
+                right_ref[:, there] = jnp.where(codes == chosen, one, zero)
+                value = turned_ref[row, :, here] * scale
+                upper = value.astype(TERM)
+                lower = ((value - upper.astype(WIDE)) * 16.0).astype(TERM)
+                both = jnp.concatenate([upper, lower], 0)
+                wide_high = jnp.broadcast_to(high[:, here], both.shape).astype(jnp.int8)
+                for group in range(groups):
+                    left_ref[group * 32 : group * 32 + 32, there] = jnp.where(
+                        wide_high == jnp.int8(group), both, zero
+                    )
+        left = left_ref[: groups * 32, columns]
+        term = lax.dot_general(left, right_ref[:, columns], NT, preferred_element_type=WIDE)
+        out_ref[...] += term * back
+        return carry
+
+    lax.fori_loop(0, rows // batch, some_rows, 0)
+
+
+def table_jobs(counts, batch, ins, outs, turned_ref, left_ref, right_ref):
+    step = pl.program_id(0)
+    start = 0
+    for job, count in enumerate(counts):
+        own_ref, other_ref, index_ref = ins[3 * job : 3 * job + 3]
+
+        @pl.when((step >= start) & (step < start + count))
+        def _():
+            table_rows([(own_ref, other_ref)], index_ref, outs[job], turned_ref, left_ref, right_ref, batch)
+
+        start += count
+
+
+def table_kernel(counts, batch, place_ref, *refs):
+    ins, outs, scratch = refs[: 3 * len(counts)], refs[3 * len(counts) : 4 * len(counts)], refs[4 * len(counts) :]
+
+    @pl.when(pl.program_id(0) == 0)
+    def _():
+        scratch[0][...] = jnp.zeros_like(scratch[0])
+        for out_ref in outs:
+            out_ref[...] = jnp.zeros_like(out_ref)
+
+    table_jobs(counts, batch, ins, outs, *scratch)
+
+
+def joined_terms(value):
+    value = value.reshape(-1, 2, 16, TABLE_LANES)
+    return (value[:, 0] + value[:, 1] * (1 / 16)).reshape(-1, TABLE_LANES)
+
+
+def table_last_kernel(counts, batch, place_ref, *refs):
+    own_ref, other_ref, index_ref, large_ref, small_ref, vector_ref, mine_ref, theirs_ref = refs[:8]
+    total_ref, scratch = refs[8], refs[9:]
+
+    @pl.when(pl.program_id(0) == 0)
+    def _():
+        scratch[0][...] = jnp.zeros_like(scratch[0])
+        total_ref[...] = large_ref[...]
+
+    table_jobs(counts, batch, (own_ref, other_ref, index_ref), [total_ref], *scratch)
+
+    @pl.when(pl.program_id(0) == pl.num_programs(0) - 1)
+    def _():
+        rows = [joined_terms(total_ref[...]), joined_terms(small_ref[...]), vector_ref[...]]
+        rows = jnp.concatenate(rows, 0).astype(NARROW).astype(WIDE)
+        half = rows.shape[0] // 2
+        is_first = place_ref[CORE] == 0
+        mine_ref[...] = jnp.where(is_first, rows[:half], rows[half:]).astype(NARROW)
+        theirs_ref[...] = jnp.where(is_first, rows[half:], rows[:half]).astype(NARROW)
+
+
+def table_gradient_sum(place, own, other, jobs, last=None):
+    step, batch = 16, 8
+    heads = own.shape[0]
+    in_specs, args = [], []
+    lanes = [index.shape[1] for index, *_ in jobs]
+    groups = [round_up(rows, TABLE_LANES) // TABLE_LANES for _, rows, *_ in jobs]
+    counts = [job[-1] for job in jobs]
+    start = 0
+    for (index, _, share_first, index_first, count), width in zip(jobs, lanes):
+        total = index.shape[0] // 2 // step
+
+        def local(i, start=start, count=count):
+            return jnp.clip(i - start, 0, count - 1)
+
+        for value in (own, other):
+            in_specs.append(
+                pl.BlockSpec(
+                    (heads, step, width),
+                    lambda i, place, local=local, first=share_first: (0, first + local(i), 0),
+                )
+            )
+        in_specs.append(
+            pl.BlockSpec(
+                (step, width),
+                lambda i, place, local=local, first=index_first, total=total: (
+                    first + local(i) + place[CORE] * total,
+                    0,
+                ),
+            )
+        )
+        args += [own, other, index]
+        start += count
+    scratch = [
+        pltpu.VMEM((step, 16, max(lanes)), WIDE),
+        pltpu.VMEM((max(groups) * 32, batch * max(lanes)), TERM),
+        pltpu.VMEM((TABLE_LANES, batch * max(lanes)), TERM),
+    ]
+    if last is None:
+        kernel = table_kernel
+        out_shape = [jax.ShapeDtypeStruct((group * 32, TABLE_LANES), WIDE) for group in groups]
+    else:
+        kernel = table_last_kernel
+        in_specs += [whole_of(value) for value in last]
+        args += last
+        rows = last[0].shape[0] // 2 + last[1].shape[0] // 2 + last[2].shape[0]
+        out_shape = [jax.ShapeDtypeStruct((rows // 2, TABLE_LANES), NARROW)] * 2
+        scratch.insert(0, pltpu.VMEM(last[0].shape, WIDE))
+    return pl.pallas_call(
+        functools.partial(kernel, counts, batch),
+        grid_spec=pltpu.PrefetchScalarGridSpec(
+            num_scalar_prefetch=1,
+            grid=(start,),
+            in_specs=in_specs,
+            out_specs=[whole_of(value) for value in out_shape],
+            scratch_shapes=scratch,
+        ),
+        out_shape=out_shape,
+        compiler_params=params(48),
+        cost_estimate=cost(start * step * max(lanes) * 1.6e-4),
+        name="table_gradient",
+    )(place, *args)
+
+
+def rotate(value, axis, size, shift):
+    return lax.ppermute(value, axis, [(i, (i + shift) % size) for i in range(size)])
+
+
+def swap_bit(value, size, bit):
+    return lax.ppermute(value, "img", [(i, i ^ (1 << bit)) for i in range(size)])
+
+
+def send_round(pieces, size):
+    return [rotate(piece, "blk", size, shift + 1) for shift, piece in enumerate(pieces)]
+
+
+def other_pieces(value, size):
+    me = lax.axis_index("blk")
+    return [lax.dynamic_index_in_dim(value, lax.rem(me + shift, size), 0, False) for shift in range(1, size)]
+
+
+def add_low(first, second):
+    return (first.astype(WIDE) + second.astype(WIDE)).astype(NARROW)
+
+
+def sum_group(value, axis, patterns, size):
+    terms = [value.astype(WIDE)]
+    for pattern in patterns:
+        got = lax.ppermute(value, axis, [(i, i ^ pattern) for i in range(size)])
+        terms.append(got.astype(WIDE))
+    while len(terms) > 1:
+        terms = [one + two for one, two in zip(terms[::2], terms[1::2])]
+    return terms[0].astype(NARROW)
+
+
+class Tree:
+    def __init__(self, terms, bits):
+        self.bits = list(bits)
+        cuts = (2,) * len(self.bits)
+        self.terms = [
+            term if term.shape[:-2] == cuts else term.reshape(cuts + (-1, term.shape[-1])) for term in terms
+        ]
+
+    def cut(self, axis, bit):
+        position = self.bits.index((axis, bit))
+        mine = lax.rem(lax.div(lax.axis_index(axis), 1 << bit), 2)
+        send = [lax.dynamic_index_in_dim(term, 1 - mine, position, False) for term in self.terms]
+        self.terms = [lax.dynamic_index_in_dim(term, mine, position, False) for term in self.terms]
+        self.bits.remove((axis, bit))
+        if len(send) == 1:
+            return send[0]
+        return sum([term.astype(WIDE) for term in send[1:]], send[0].astype(WIDE)).astype(NARROW)
+
+    def total(self):
+        return sum([term.astype(WIDE) for term in self.terms[1:]], self.terms[0].astype(WIDE))
+
+
+def swap(value, axis, bit, sizes):
+    return lax.ppermute(value, axis, [(i, i ^ (1 << bit)) for i in range(sizes[axis])])
+
+
+def together(*values):
+    return lax.optimization_barrier(values)
+
+
+def image_on_device(
+    img,
+    blk,
+    images_large,
+    images_small,
+    cotan_large,
+    cotan_small,
+    lengths_large,
+    lengths_small,
+    index_large,
+    index_small,
+    attn_gain,
+    attn_shift,
+    qkv_weight,
+    query_bias,
+    value_bias,
+    table_large,
+    table_small,
+    proj_weight,
+    proj_bias,
+    attn_scale,
+    mlp_gain,
+    mlp_shift,
+    inner_weight,
+    inner_bias,
+    outer_weight,
+    outer_bias,
+    mlp_scale,
+):
+    width = attn_gain.shape[0]
+    heads = table_large.shape[1]
+    hidden = inner_bias.shape[0]
+    rows = images_large.shape[1]
+    smalls, small_rows = images_small.shape[:2]
+    part = round_up(rows, 8)
+    while part * blk % 16:
+        part += 8
+    large = part * blk
+    small = round_up(small_rows, 16)
+    tokens = large + smalls * small
+    images = ((0, large),) + tuple((large + i * small, small) for i in range(smalls))
+    lanes_large = round_up(large, LANES)
+    lanes_small = round_up(small, LANES)
+    double = round_up(small, 32)
+    blk_me = lax.axis_index("blk")
+    core = lax.rem(lax.axis_index("img"), 2)
+    place = jnp.stack([blk_me, core])
+    shape = (part, large, small)
+
+    sends = other_pieces(images_large, blk)
+    gots = send_round(sends, blk)
+    spread_large = spread_index(index_large, blk, part, large, lanes_large)
+    spread_small = spread_index(index_small, 1, small, double, lanes_small)
+    small_bias = bias_lookup(place, table_small, spread_small, 1)
+    own_bias = bias_lookup(place, table_large, together(spread_large, small_bias)[0], 2)
+    gots, own_bias, images_small, cotan_large, cotan_small, lengths_large, lengths_small = together(
+        gots, own_bias, images_small, cotan_large, cotan_small, lengths_large, lengths_small
+    )
+    other_bias = swap_bit(own_bias, img, 0)
+
+    token = jnp.arange(large, dtype=jnp.int32)
+    own_length = lax.dynamic_index_in_dim(lengths_large, blk_me, 0, False)
+    inside = (token % part < rows) & (token // part * rows + token % part < own_length)
+    small_token = jnp.arange(small, dtype=jnp.int32)
+    small_inside = (small_token[None, :] < lengths_small[:, None]).reshape(-1)
+    mask = jnp.where(jnp.concatenate([inside, small_inside]), 0.0, NEGATIVE).astype(NARROW)
+    mask = jnp.broadcast_to(mask[:, None], (tokens, LANES))
+
+    def row(vector):
+        return vector.astype(WIDE)[None, :]
+
+    bias_row = row(jnp.concatenate([query_bias, jnp.zeros_like(query_bias), value_bias]))
+    x, h, p = qkv_forward(
+        place, images_large, gots, images_small, row(attn_gain), row(attn_shift), qkv_weight, bias_row, *shape
+    )
+    sends = other_pieces(cotan_large, blk)
+    x, h, p, other_bias, sends = together(x, h, p, other_bias, sends)
+    gots = send_round(sends, blk)
+    out, large_p, small_p = attention_forward(place, p, mask, own_bias, other_bias, small_bias, images)
+    out, large_p, small_p, gots = together(out, large_p, small_p, gots)
+    zeros = jnp.zeros_like(proj_bias)
+    vectors = jnp.stack(
+        [proj_bias, attn_scale, mlp_gain, mlp_shift, outer_bias, mlp_scale, zeros, zeros]
+    ).astype(WIDE)
+    devices = img * blk
+    share = width // devices
+    found = mlp_pass(
+        place,
+        cotan_large,
+        gots,
+        cotan_small,
+        out,
+        x,
+        proj_weight,
+        vectors,
+        inner_weight,
+        row(inner_bias),
+        outer_weight,
+        *shape,
+        devices,
+    )
+    results, found = list(found[:blk]), found[blk:]
+    result_small, dm, grad_out, feed, mlp_sums, dinner_bias = found
+    sizes = {"img": img, "blk": blk}
+    bits = [("img", bit) for bit in range(1, img.bit_length() - 1)]
+    blk_bits = [("blk", bit) for bit in range(blk.bit_length() - 1)]
+    dims = bits[::-1] + blk_bits[::-1]
+    orders = [bits + blk_bits, bits[::-1] + blk_bits]
+
+    def cut(trees, level):
+        return [tree.cut(*order[level]) for tree, order in zip(trees, orders)]
+
+    def move(level, sends):
+        return [swap(send, *order[level], sizes) for order, send in zip(orders, sends)]
+
+    def add(trees, gots):
+        for tree, got in zip(trees, gots):
+            tree.terms.append(got)
+
+    grad_out, feed = together(grad_out, feed)
+    feed_part = lax.psum_scatter(feed, "img", scatter_dimension=0, tiled=True)
+    share_rows = large // 2 + double // 2
+    dp, own_share, theirs = attention_backward(
+        place, p, grad_out, out, large_p, small_p, images, (share_rows, lanes_large), 0, heads // 2
+    )
+    other_share = swap_bit(theirs, img, 0)
+    found = qkv_backward(place, results, dp, h, x, dm, row(attn_gain), qkv_weight, part, large, devices)
+    qkv_mine, qkv_theirs, backs, grad_small, qkv_sums = found[0], found[1], list(found[2:-2]), found[-2], found[-1]
+    qkv_mine, qkv_theirs, backs, qkv_sums, other_share, spread_large, spread_small = together(
+        qkv_mine, qkv_theirs, backs, qkv_sums, other_share, spread_large, spread_small
+    )
+
+    qkv_got = swap_bit(qkv_theirs, img, 0)
+    backs[1:] = send_round(backs[1:], blk)
+    middle = 3 * width // 2
+    columns = (slice(0, middle), slice(middle, None))
+    last = [Tree([qkv_mine[:, part], qkv_got[:, part]], dims) for part in columns]
+    sums = jnp.concatenate([mlp_sums[:6], qkv_sums[:4], dinner_bias.reshape(-1, width)], 0).reshape(-1, TABLE_LANES)
+    table_sizes = [round_up(table.shape[0], TABLE_LANES) // TABLE_LANES * 16 for table in (table_large, table_small)]
+    sums = jnp.pad(sums, ((0, -(sums.shape[0] + sum(table_sizes)) % 32), (0, 0)))
+    steps = large // 32
+    mark = steps * 2 // 5
+
+    sends = cut(last, 0)
+    sends, sums, spread_large, spread_small = together(sends, sums, spread_large, spread_small)
+    gots = move(0, sends)
+    large_sum, small_sum = table_gradient_sum(
+        place,
+        own_share,
+        other_share,
+        [
+            (spread_large, table_large.shape[0], 0, 0, mark),
+            (spread_small, table_small.shape[0], steps, 0, double // 32),
+        ],
+    )
+    large_sum, small_sum, gots, spread_large, feed_part = together(large_sum, small_sum, gots, spread_large, feed_part)
+    add(last, gots)
+    sends = cut(last, 1)
+    feed_tree = Tree([feed_part], blk_bits[::-1])
+    feed_send = feed_tree.cut(*blk_bits[0])
+    sends, feed_send, spread_large = together(sends, feed_send, spread_large)
+    gots = move(1, sends)
+    feed_got = swap(feed_send, *blk_bits[0], sizes)
+    mine, theirs = table_gradient_sum(
+        place,
+        own_share,
+        other_share,
+        [(spread_large, table_large.shape[0], mark, mark, steps - mark)],
+        [large_sum, small_sum, sums],
+    )
+    mine, theirs, gots, feed_got, backs = together(mine, theirs, gots, feed_got, backs)
+    add(last, gots)
+    feed_tree.terms.append(feed_got)
+
+    joined = add_low(mine, swap_bit(theirs, img, 0))
+    joined = sum_group(joined, "img", [2 * m for m in range(1, img // 2)], img)
+    last = Tree([jnp.concatenate([tree.terms[number] for tree in last], -1) for number in range(4)], dims[2:])
+    tail = [last, feed_tree]
+    for axis, bit in blk_bits:
+        for tree in tail:
+            if (axis, bit) in tree.bits:
+                got = swap(tree.cut(axis, bit), axis, bit, sizes)
+                tree.terms.append(got)
+    joined = sum_group(joined, "blk", range(1, blk), blk)
+    other = swap_bit(joined, img, 0)
+    joined = jnp.where(core == 0, jnp.stack([joined, other]), jnp.stack([other, joined]))
+    joined = joined.reshape(-1, TABLE_LANES).astype(WIDE)
+    last_sum, feed_sum = last.total(), feed_tree.total()
+    result_large, result_small, grad_large, grad_small = place_results(
+        place, backs, [result_small, grad_small], rows, small, smalls, small_rows
+    )
+    outs = []
+    first = 0
+    for table, count in zip((table_large, table_small), table_sizes):
+        value = joined[first : first + count].reshape(-1, 16, TABLE_LANES)[:, :heads]
+        outs.append(jnp.transpose(value, (0, 2, 1)).reshape(-1, heads)[: table.shape[0]])
+        first += count
+    sums = joined[first:].reshape(-1)
+    me = lax.axis_index("img") * blk + blk_me
+
+    def own(place, length=1):
+        return lax.dynamic_slice_in_dim(sums, place * width + me * share * length, share * length, 0)
+
+    return (
+        result_large,
+        result_small,
+        grad_large,
+        grad_small,
+        own(8),
+        own(9),
+        last_sum,
+        own(6),
+        own(7),
+        outs[0],
+        outs[1],
+        feed_sum[:, hidden : hidden + width],
+        own(5),
+        own(4),
+        own(2),
+        own(3),
+        feed_sum[:, :hidden],
+        own(10, hidden // width),
+        jnp.transpose(feed_sum[:, hidden + width :].reshape(share, -1, width), (1, 0, 2)).reshape(-1, width),
+        own(1),
+        own(0),
+    )
+
+
 def solution(mesh):
+    img, blk = mesh.shape["img"], mesh.shape["blk"]
+
+    def by_device(*args):
+        if args[0].shape[0] == blk:
+            return image_on_device(img, blk, *args)
+        return on_device(*args)
+
     return jax.shard_map(
-        on_device,
+        by_device,
         mesh=mesh,
         in_specs=(
             P("img", "blk", None),

time: 2070 us -> 325 us (0.16)
  matrix products: 858 us -> 0 us
  waiting for transfers between devices: 844 us -> 20.5 us
  local copies, waits for them, and re-layouts: 271 us -> 31.3 us
  Pallas kernels: 0 us -> 203 us
  other arithmetic: 64 us -> 5.97 us
  starting transfers between devices: 0.84 us -> 45.7 us
    dot_general x112 -> x0, matrix products: 858 us -> none  [the longest x44 368 us: table_one_query(): jnp.dot(selector.T, grad_row, precision=HIGHEST, preferred_element_type=j...]
    reduce_scatter x4 -> x1, waiting for transfers between devices: 515 us -> 3.57 us  [image_on_device(): feed_part = lax.psum_scatter(feed, 'img', scatter_dimension=0, tiled=True)]
    unnamed x11 -> x1, waiting for transfers between devices: 214 us -> 0.02 us
    pallas_call x0 -> x12, Pallas kernels: none -> 203 us  [the longest x1 59.8 us: mlp_pass(): pl.pallas_call(functools.partial(mlp_kernel, part, large, small, share, l...]
    psum x1 -> x0, waiting for transfers between devices: 115 us -> none  [on_device(): lax.psum((large_table_grad, small_table_grad), ('img', 'blk'))]
    reshape x16 -> x3, local copies, waits for them, and re-layouts: 74.7 us -> 0.76 us  [the longest x1 0.73 us: image_on_device(): feed_sum[:, hidden + width:].reshape(share, -1, width)]
    eq x86 -> x0, local copies, waits for them, and re-layouts: 61.2 us -> none  [the longest x43 30.6 us: table_one_query(): selector = (index_row[:, None] == table_codes[None, :]).astype(jnp.float32)]
    ppermute x0 -> x28, starting transfers between devices: none -> 45.7 us  [the longest x9 27.1 us: rotate(): lax.ppermute(value, axis, [(i, (i + shift) % size) for i in range(size)])]
  transfers between devices with their start and end apart: 9 -> 29, of which waited for: 7 -> 8; matrix products, arithmetic and copies ran while one was open for 28% -> 7% of each run, Pallas kernels for 0% -> 44%
where the time goes in v2:
time: 325 us; the launch traced here: 322 us
  Pallas kernels  203 us (62%)
  starting transfers between devices  45.7 us (14%)
  local copies, waits for them, and re-layouts  31.3 us (10%)
  waiting for transfers between devices  20.5 us (6%)
  between operations  15.6 us (5%)
  other arithmetic  5.97 us (2%)
    pallas_call x1, Pallas kernels, mlp_pass(): pl.pallas_call(functools.partial(mlp_kernel, part, large, small, share, l...  59.8 us
    pallas_call x2, Pallas kernels, table_gradient_sum(): pl.pallas_call(functools.partial(kernel, counts, batch), grid_spec=pltpu....  40.1 us
    pallas_call x2, Pallas kernels, bias_lookup(): pl.pallas_call(functools.partial(bias_kernel, heads, groups), grid_spec=p...  28.2 us
    ppermute x9, starting transfers between devices, rotate(): lax.ppermute(value, axis, [(i, (i + shift) % size) for i in range(size)])  27.1 us
    pallas_call x1, Pallas kernels, attention_backward(): pl.pallas_call(functools.partial(attention_backward_kernel, images), grid...  24.1 us
    pallas_call x1, Pallas kernels, attention_forward(): pl.pallas_call(functools.partial(attention_forward_kernel, images), grid_...  21.1 us
    pallas_call x1, Pallas kernels, qkv_backward(): pl.pallas_call(functools.partial(qkv_backward_kernel, part, large, blk *...  17.5 us
    unnamed x122, local copies, waits for them, and re-layouts  16.1 us
  transfers between devices with their start and end apart: 29, of which 8 were waited for; matrix products, arithmetic and copies ran while one was open for 7% of the time, Pallas kernels for 44%

profile of v2, /device:TPU:0, one launch (start us, length us, event | category | flops | bytes accessed | tf_op | source)
XLA Modules:
  0.0 322.0 jit_solution(4917161146376173993)
XLA Ops:
  9.5 3.0 collective-permute-start
  12.5 2.6 collective-permute-start.1
  19.6 3.2 %bias_lookup.2.small_bias_ref = bf16[12,224,256]{2,1,0:T(8,128)(2,1)S(1)} custom-call(s32[2]{0:T(128)S(1)} %pad_add_fusion.place_ref, f32[72,8,128]{2,1,0:T(8,128)S(1)} %broadcast_in_dim.61.table_ref, s32[224,256]{1,0:T(8,128)S(1)} %copy-done.6), custom_call_target="tpu_custom_call" | custom-call | flops 2848849920 | bytes 7927234 | tf_op jit(solution)/shard_map/bias_lookup/pallas_call | solution.py:480
  24.0 1.4 copy-done.10
  25.4 25.0 %bias_lookup.3.own_bias_ref = bf16[12,304,640]{2,1,0:T(8,128)(2,1)} custom-call(s32[2]{0:T(128)S(1)} %pad_add_fusion.place_ref, f32[216,8,128]{2,1,0:T(8,128)S(1)} %broadcast_in_dim.58.table_ref, s32[608,640]{1,0:T(8,128)S(1)} %copy-done.10), custom_call_target="tpu_custom_call" | custom-call | flops 28997222400 | bytes 80687920 | tf_op jit(solution)/shard_map/bias_lookup/pallas_call | solution.py:480
  55.0 9.1 %qkv_forward.1 = (bf16[1024,768]{1,0:T(8,128)(2,1)S(1)}, bf16[1024,768]{1,0:T(8,128)(2,1)S(1)}, bf16[1024,2304]{1,0:T(8,128)(2,1)}) custom-call(s32[2]{0:T(128)S(1)} %pad_add_fusion.place_ref, bf16[4,146,768]{2,1,0:T(8,128)(2,1)S(1)} %copy.78.mine_ref, bf16[146,768]{1,0:T(8,128)(2,1)S(1)} %collective-permute-done.refs_0_, ...), custom_call_target="tpu_custom_call" | custom-call | flops 10418651136 | bytes 28991028 | tf_op jit(solution)/shard_map/qkv_forward/pallas_call | solution.py:526
  67.5 13.9 %collective-permute-start.6 = (bf16[146,768]{1,0:T(8,128)(2,1)S(1)}, bf16[146,768]{1,0:T(8,128)(2,1)S(1)}, u32[]{:S(2)}, u32[]{:S(2)}) collective-permute-start(bf16[146,768]{1,0:T(8,128)(2,1)S(1)} %get-tuple-element.134), channel_id=1, source_target_pairs={{0,3},{1,0},{2,1},{3,2},{4,7},{5,4},{6,5},{7,6},{8,11},{9,8},{10,9... | collective-permute-start | bytes 672776 | tf_op jit(solution)/shard_map/ppermute | solution.py:1244
  82.4 21.1 %attention_forward.1 = (bf16[1024,768]{1,0:T(8,128)(2,1)}, bf16[12,608,608]{2,1,0:T(8,128)(2,1)}, bf16[12,2,208,208]{3,2,1,0:T(8,128)(2,1)}) custom-call(s32[2]{0:T(128)} %copy-done.3, bf16[1024,2304]{1,0:T(8,128)(2,1)} %get-tuple-element.125.q_ref.k_ref.v_ref, bf16[1024,2304]{1,0:T(8,128)(2,1)} %get-tuple-element.125.q_ref.k_ref.v_ref, ...), custom_call_target="tpu_custom_call" | custom-call | flops 23922708480 | bytes 66567536 | tf_op jit(solution)/shard_map/attention_forward/pallas_call | solution.py:619
  104.3 59.8 %mlp_pass.1 = (bf16[152,768]{1,0:T(8,128)(2,1)}, bf16[152,768]{1,0:T(8,128)(2,1)}, bf16[152,768]{1,0:T(8,128)(2,1)}, bf16[152,768]{1,0:T(8,128)(2,1)}, bf16[416,...) custom-call(s32[2]{0:T(128)} %copy-done.3, ...), custom_call_target="tpu_custom_call" | custom-call | flops 66679365632 | bytes 185542592 | tf_op jit(solution)/shard_map/mlp_pass/pallas_call | solution.py:917
  164.2 24.1 %attention_backward.1 = (bf16[3,1024,768]{2,1,0:T(8,128)(2,1)}, bf16[12,416,640]{2,1,0:T(8,128)(2,1)}, bf16[12,416,640]{2,1,0:T(8,128)(2,1)}) custom-call(s32[2]{0:T(128)} %copy-done.3, bf16[1024,2304]{1,0:T(8,128)(2,1)} %get-tuple-element.125.q_ref.k_ref.v_ref, bf16[1024,2304]{1,0:T(8,128)(2,1)} %get-tuple-element.125.q_ref.k_ref.v_ref, ...), custom_call_target="tpu_custom_call" | custom-call | flops 26440888320 | bytes 73574648 | tf_op jit(solution)/shard_map/attention_backward/pallas_call | solution.py:733
  189.4 17.5 %qkv_backward.1 = (bf16[384,2304]{1,0:T(8,128)(2,1)}, bf16[384,2304]{1,0:T(8,128)(2,1)}, bf16[2,152,768]{2,1,0:T(8,128)(2,1)S(1)}, bf16[2,152,768]{2,1,0:T(8,128...) custom-call(s32[2]{0:T(128)S(1)} %copy-done.4, ...), custom_call_target="tpu_custom_call" | custom-call | flops 17364418560 | bytes 48318384 | tf_op jit(solution)/shard_map/qkv_backward/pallas_call | solution.py:1014
  210.9 1.6 collective-permute-start.15
  212.5 2.8 collective-permute-start.16
  215.4 1.6 fusion.30
  217.9 1.6 fusion.31
  219.8 1.5 collective-permute-start.10
  221.3 1.5 collective-permute-start.9
  222.8 20.5 %table_gradient.2 = (f32[288,256]{1,0:T(8,128)S(1)}, f32[96,256]{1,0:T(8,128)S(1)}) custom-call(s32[2]{0:T(128)S(1)} %copy-done.4, bf16[12,416,640]{2,1,0:T(8,128)(2,1)} %get-tuple-element.146.refs_0_.refs_3_, bf16[12,416,640]{2,1,0:T(8,128)(2,1)} %collective-permute-done.7.refs_1_.refs_4_, s32[608,640]{1,0:T(8,128)S(1)} %copy-done.11, ...), custom_call_target="tpu_custom_call" | custom-call | flops 26378240000 | bytes 73400320 | tf_op jit(solution)/shard_map/table_gradient/pallas_call | solution.py:1227
  244.9 3.6 %reduce-scatter.2.cloned.1.call-done = bf16[96,6912]{1,0:T(8,128)(2,1)} async-done(((bf16[768,6912]{1,0:T(8,128)(2,1)}), bf16[96,6912]{1,0:T(8,128)(2,1)}) %reduce-scatter.2.cloned.1.call-update) | async-done | bytes 1327120 | tf_op jit(solution)/shard_map/reduce_scatter | solution.py:1424
  249.8 1.6 fusion.4
  251.4 1.6 collective-permute-start.13
  252.9 1.4 collective-permute-start.11
  254.3 19.6 %table_gradient.3 = (bf16[128,256]{1,0:T(8,128)(2,1)S(1)}, bf16[128,256]{1,0:T(8,128)(2,1)S(1)}) custom-call(s32[2]{0:T(128)S(1)} %copy-done.4, bf16[12,416,640]{2,1,0:T(8,128)(2,1)} %get-tuple-element.146.refs_0_.refs_3_, bf16[12,416,640]{2,1,0:T(8,128)(2,1)} %collective-permute-done.7.refs_1_.refs_4_, s32[608,640]{1,0:T(8,128)S(1)} %copy-done.12, ...), custom_call_target="tpu_custom_call" | custom-call | flops 22609920000 | bytes 62914560 | tf_op jit(solution)/shard_map/table_gradient/pallas_call | solution.py:1227
  275.7 5.0 %collective-permute-done.12 = bf16[2,2,24,1152]{3,2,1,0:T(8,128)(2,1)S(1)} collective-permute-done((bf16[2,2,24,1152]{3,2,1,0:T(8,128)(2,1)S(1)}, bf16[2,2,24,1152]{3,2,1,0:T(8,128)(2,1)S(1)}, u32[]{:S(2)}, u32[]{:S(2)}) %collective-permute-start.12) | collective-permute-done | bytes 221216 | tf_op jit(solution)/shard_map/ppermute | solution.py:1297
  280.8 2.5 collective-permute-start.27
  285.4 1.4 collective-permute-start.19
  286.8 1.4 collective-permute-start.20
  289.6 2.3 collective-permute-done.20
  293.2 3.3 %collective-permute-start.23 = (bf16[128,256]{1,0:T(8,128)(2,1)S(1)}, bf16[128,256]{1,0:T(8,128)(2,1)S(1)}, u32[]{:S(2)}, u32[]{:S(2)}) collective-permute-start(bf16[128,256]{1,0:T(8,128)(2,1)S(1)} %add_convert_fusion.4), channel_id=1, source_target_pairs={{0,3},{1,2},{2,1},{3,0},{4,7},{5,6},{6,5},{7,4},{8,11},{9,10},{10,... | collective-permute-start | bytes 196616 | tf_op jit(solution)/shard_map/ppermute | solution.py:1267
  296.5 1.8 place_results.1
  300.8 5.2 %collective-permute-done.21 = bf16[128,256]{1,0:T(8,128)(2,1)S(1)} collective-permute-done((bf16[128,256]{1,0:T(8,128)(2,1)S(1)}, bf16[128,256]{1,0:T(8,128)(2,1)S(1)}, u32[]{:S(2)}, u32[]{:S(2)}) %collective-permute-start.21) | collective-permute-done | bytes 65568 | tf_op jit(solution)/shard_map/ppermute | solution.py:1267
  312.4 1.5 collective-permute-done.26
  (236 shorter events, 42.3 us)
Async XLA Ops:
  7.2 241.3 %reduce-scatter.2.cloned.1.call-start = ((), (), s32[]{:S(2)}) async-start(), calls=%async_computation.1 | async-start | bytes 11943936 | tf_op jit(solution)/shard_map/reduce_scatter | solution.py:1424
  9.5 41.0 %collective-permute-start = (bf16[146,768]{1,0:T(8,128)(2,1)}, bf16[146,768]{1,0:T(8,128)(2,1)S(1)}, u32[]{:S(2)}, u32[]{:S(2)}) collective-permute-start(bf16[146,768]{1,0:T(8,128)(2,1)} %get-tuple-element.281), channel_id=1, source_target_pairs={{0,1},{1,2},{2,3},{3,0},{4,5},{5,6},{6,7},{7,4},{8,9},{9,10},{10,1... | collective-permute-start | bytes 672776 | tf_op jit(solution)/shard_map/ppermute | solution.py:1244
  12.5 37.9 %collective-permute-start.1 = (bf16[146,768]{1,0:T(8,128)(2,1)}, bf16[146,768]{1,0:T(8,128)(2,1)S(1)}, u32[]{:S(2)}, u32[]{:S(2)}) collective-permute-start(bf16[146,768]{1,0:T(8,128)(2,1)} %get-tuple-element.280), channel_id=1, source_target_pairs={{0,2},{1,3},{2,0},{3,1},{4,6},{5,7},{6,4},{7,5},{8,10},{9,11},{10,... | collective-permute-start | bytes 672776 | tf_op jit(solution)/shard_map/ppermute | solution.py:1244
  15.1 35.4 %collective-permute-start.2 = (bf16[146,768]{1,0:T(8,128)(2,1)}, bf16[146,768]{1,0:T(8,128)(2,1)S(1)}, u32[]{:S(2)}, u32[]{:S(2)}) collective-permute-start(bf16[146,768]{1,0:T(8,128)(2,1)} %get-tuple-element.279), channel_id=1, source_target_pairs={{0,3},{1,0},{2,1},{3,2},{4,7},{5,4},{6,5},{7,6},{8,11},{9,8},{10,9... | collective-permute-start | bytes 672776 | tf_op jit(solution)/shard_map/ppermute | solution.py:1244
  19.6 35.4 %copy-start.3 = (s32[2]{0:T(128)}, s32[2]{0:T(128)S(1)}, u32[]{:S(2)}) copy-start(s32[2]{0:T(128)S(1)} %pad_add_fusion.place_ref) | copy-start | bytes 28
  25.4 26.0 %copy-start.40 = (bf16[3072]{0:T(1024)(128)(2,1)S(1)}, bf16[3072]{0:T(1024)(128)(2,1)}, u32[]{:S(2)}) copy-start(bf16[3072]{0:T(1024)(128)(2,1)} %param.46) | copy-start | bytes 18436
  50.5 16.0 %collective-permute-start.3 = (bf16[12,304,640]{2,1,0:T(8,128)(2,1)}, bf16[12,304,640]{2,1,0:T(8,128)(2,1)}, u32[]{:S(2)}, u32[]{:S(2)}) collective-permute-start(bf16[12,304,640]{2,1,0:T(8,128)(2,1)} %bias_lookup.3.own_bias_ref), channel_id=1, source_target_pairs={{0,4},{4,0},{8,12},{12,8},{16,20},{20,16},{24,28},{28,24},{1,5},{5... | collective-permute-start | bytes 14008328 | tf_op jit(solution)/shard_map/ppermute | solution.py:1248
  66.5 37.0 %collective-permute-start.4 = (bf16[146,768]{1,0:T(8,128)(2,1)S(1)}, bf16[146,768]{1,0:T(8,128)(2,1)S(1)}, u32[]{:S(2)}, u32[]{:S(2)}) collective-permute-start(bf16[146,768]{1,0:T(8,128)(2,1)S(1)} %get-tuple-element.132), channel_id=1, source_target_pairs={{0,1},{1,2},{2,3},{3,0},{4,5},{5,6},{6,7},{7,4},{8,9},{9,10},{10,1... | collective-permute-start | bytes 672776 | tf_op jit(solution)/shard_map/ppermute | solution.py:1244
  67.2 36.3 %collective-permute-start.5 = (bf16[146,768]{1,0:T(8,128)(2,1)S(1)}, bf16[146,768]{1,0:T(8,128)(2,1)S(1)}, u32[]{:S(2)}, u32[]{:S(2)}) collective-permute-start(bf16[146,768]{1,0:T(8,128)(2,1)S(1)} %get-tuple-element.133), channel_id=1, source_target_pairs={{0,2},{1,3},{2,0},{3,1},{4,6},{5,7},{6,4},{7,5},{8,10},{9,11},{10,... | collective-permute-start | bytes 672776 | tf_op jit(solution)/shard_map/ppermute | solution.py:1244
  67.5 36.0 %collective-permute-start.6 = (bf16[146,768]{1,0:T(8,128)(2,1)S(1)}, bf16[146,768]{1,0:T(8,128)(2,1)S(1)}, u32[]{:S(2)}, u32[]{:S(2)}) collective-permute-start(bf16[146,768]{1,0:T(8,128)(2,1)S(1)} %get-tuple-element.134), channel_id=1, source_target_pairs={{0,3},{1,0},{2,1},{3,2},{4,7},{5,4},{6,5},{7,6},{8,11},{9,8},{10,9... | collective-permute-start | bytes 672776 | tf_op jit(solution)/shard_map/ppermute | solution.py:1244
  188.3 20.2 %collective-permute-start.7 = (bf16[12,416,640]{2,1,0:T(8,128)(2,1)}, bf16[12,416,640]{2,1,0:T(8,128)(2,1)}, u32[]{:S(2)}, u32[]{:S(2)}) collective-permute-start(bf16[12,416,640]{2,1,0:T(8,128)(2,1)} %get-tuple-element.161), channel_id=1, source_target_pairs={{0,4},{4,0},{8,12},{12,8},{16,20},{20,16},{24,28},{28,24},{1,5},{5... | collective-permute-start | bytes 19169288 | tf_op jit(solution)/shard_map/ppermute | solution.py:1248
  208.5 9.3 %collective-permute-start.8 = (bf16[384,2304]{1,0:T(8,128)(2,1)}, bf16[384,2304]{1,0:T(8,128)(2,1)}, u32[]{:S(2)}, u32[]{:S(2)}) collective-permute-start(bf16[384,2304]{1,0:T(8,128)(2,1)} %get-tuple-element.164), channel_id=1, source_target_pairs={{0,4},{4,0},{8,12},{12,8},{16,20},{20,16},{24,28},{28,24},{1,5},{5... | collective-permute-start | bytes 5308424 | tf_op jit(solution)/shard_map/ppermute | solution.py:1248
  210.2 63.8 %collective-permute-start.14 = (bf16[2,152,768]{2,1,0:T(8,128)(2,1)S(1)}, bf16[2,152,768]{2,1,0:T(8,128)(2,1)S(1)}, u32[]{:S(2)}, u32[]{:S(2)}) collective-permute-start(bf16[2,152,768]{2,1,0:T(8,128)(2,1)S(1)} %get-tuple-element.191), channel_id=1, source_target_pairs={{0,1},{1,2},{2,3},{3,0},{4,5},{5,6},{6,7},{7,4},{8,9},{9,10},{10,1... | collective-permute-start | bytes 1400840 | tf_op jit(solution)/shard_map/ppermute | solution.py:1244
  210.9 64.7 %collective-permute-start.15 = (bf16[2,152,768]{2,1,0:T(8,128)(2,1)S(1)}, bf16[2,152,768]{2,1,0:T(8,128)(2,1)S(1)}, u32[]{:S(2)}, u32[]{:S(2)}) collective-permute-start(bf16[2,152,768]{2,1,0:T(8,128)(2,1)S(1)} %get-tuple-element.192), channel_id=1, source_target_pairs={{0,2},{1,3},{2,0},{3,1},{4,6},{5,7},{6,4},{7,5},{8,10},{9,11},{10,... | collective-permute-start | bytes 1400840 | tf_op jit(solution)/shard_map/ppermute | solution.py:1244
  212.5 63.1 %collective-permute-start.16 = (bf16[2,152,768]{2,1,0:T(8,128)(2,1)S(1)}, bf16[2,152,768]{2,1,0:T(8,128)(2,1)S(1)}, u32[]{:S(2)}, u32[]{:S(2)}) collective-permute-start(bf16[2,152,768]{2,1,0:T(8,128)(2,1)S(1)} %get-tuple-element.193), channel_id=1, source_target_pairs={{0,3},{1,0},{2,1},{3,2},{4,7},{5,4},{6,5},{7,6},{8,11},{9,8},{10,9... | collective-permute-start | bytes 1400840 | tf_op jit(solution)/shard_map/ppermute | solution.py:1244
  219.8 24.4 %collective-permute-start.10 = (bf16[2,2,2,24,1152]{4,3,2,1,0:T(8,128)(2,1)S(1)}, bf16[2,2,2,24,1152]{4,3,2,1,0:T(8,128)(2,1)S(1)}, u32[]{:S(2)}, u32[]{:S(2)}) collective-permute-start(bf16[2,2,2,24,1152]{4,3,2,1,0:T(8,128)(2,1)S(1)} %fusion.3), channel_id=1, source_target_pairs={{0,16},{4,20},{8,24},{12,28},{16,0},{20,4},{24,8},{28,12},{1,17},{... | collective-permute-start | bytes 1327112 | tf_op jit(solution)/shard_map/ppermute | solution.py:1297
  221.3 23.6 %collective-permute-start.9 = (bf16[2,2,2,24,1152]{4,3,2,1,0:T(8,128)(2,1)S(1)}, bf16[2,2,2,24,1152]{4,3,2,1,0:T(8,128)(2,1)}, u32[]{:S(2)}, u32[]{:S(2)}) collective-permute-start(bf16[2,2,2,24,1152]{4,3,2,1,0:T(8,128)(2,1)S(1)} %fusion.2), channel_id=1, source_target_pairs={{0,8},{4,12},{8,0},{12,4},{16,24},{20,28},{24,16},{28,20},{1,9},{5... | collective-permute-start | bytes 1327112 | tf_op jit(solution)/shard_map/ppermute | solution.py:1297
  251.4 29.3 %copy-start.33 = (bf16[96,6912]{1,0:T(8,128)(2,1)S(1)}, bf16[96,6912]{1,0:T(8,128)(2,1)}, u32[]{:S(2)}) copy-start(bf16[96,6912]{1,0:T(8,128)(2,1)} %reduce-scatter.2.cloned.1.call-done) | copy-start | bytes 3981316
  251.4 29.3 %collective-permute-start.13 = (bf16[2,24,6912]{2,1,0:T(8,128)(2,1)S(1)}, bf16[2,24,6912]{2,1,0:T(8,128)(2,1)S(1)}, u32[]{:S(2)}, u32[]{:S(2)}) collective-permute-start(bf16[2,24,6912]{2,1,0:T(8,128)(2,1)S(1)} %dynamic-slice_bitcast_fusion), channel_id=1, source_target_pairs={{0,1},{1,0},{2,3},{3,2},{4,5},{5,4},{6,7},{7,6},{8,9},{9,8},{10,11... | collective-permute-start | bytes 1990664 | tf_op jit(solution)/shard_map/ppermute | solution.py:1297
  252.9 22.8 %collective-permute-start.11 = (bf16[2,2,24,1152]{3,2,1,0:T(8,128)(2,1)S(1)}, bf16[2,2,24,1152]{3,2,1,0:T(8,128)(2,1)S(1)}, u32[]{:S(2)}, u32[]{:S(2)}) collective-permute-start(bf16[2,2,24,1152]{3,2,1,0:T(8,128)(2,1)S(1)} %get-tuple-element.187), channel_id=1, source_target_pairs={{0,16},{4,20},{8,24},{12,28},{16,0},{20,4},{24,8},{28,12},{1,17},{... | collective-permute-start | bytes 663560 | tf_op jit(solution)/shard_map/ppermute | solution.py:1297
  274.0 6.7 %collective-permute-start.12 = (bf16[2,2,24,1152]{3,2,1,0:T(8,128)(2,1)S(1)}, bf16[2,2,24,1152]{3,2,1,0:T(8,128)(2,1)S(1)}, u32[]{:S(2)}, u32[]{:S(2)}) collective-permute-start(bf16[2,2,24,1152]{3,2,1,0:T(8,128)(2,1)S(1)} %get-tuple-element.188), channel_id=1, source_target_pairs={{0,8},{4,12},{8,0},{12,4},{16,24},{20,28},{24,16},{28,20},{1,9},{5... | collective-permute-start | bytes 663560 | tf_op jit(solution)/shard_map/ppermute | solution.py:1297
  280.8 29.4 %collective-permute-start.27 = (bf16[24,6912]{1,0:T(8,128)(2,1)S(1)}, bf16[24,6912]{1,0:T(8,128)(2,1)S(1)}, u32[]{:S(2)}, u32[]{:S(2)}) collective-permute-start(bf16[24,6912]{1,0:T(8,128)(2,1)S(1)} %fusion), channel_id=1, source_target_pairs={{0,2},{1,3},{2,0},{3,1},{4,6},{5,7},{6,4},{7,5},{8,10},{9,11},{10,... | collective-permute-start | bytes 995336 | tf_op jit(solution)/shard_map/ppermute | solution.py:1297
  283.3 1.3 collective-permute-start.17
  284.7 4.3 %collective-permute-start.18 = (bf16[128,256]{1,0:T(8,128)(2,1)S(1)}, bf16[128,256]{1,0:T(8,128)(2,1)S(1)}, u32[]{:S(2)}, u32[]{:S(2)}) collective-permute-start(bf16[128,256]{1,0:T(8,128)(2,1)S(1)} %add_convert_fusion.5), channel_id=1, source_target_pairs={{0,8},{4,12},{8,0},{12,4},{16,24},{20,28},{24,16},{28,20},{1,9},{5... | collective-permute-start | bytes 196616 | tf_op jit(solution)/shard_map/ppermute | solution.py:1267
  285.4 4.3 %collective-permute-start.19 = (bf16[128,256]{1,0:T(8,128)(2,1)S(1)}, bf16[128,256]{1,0:T(8,128)(2,1)S(1)}, u32[]{:S(2)}, u32[]{:S(2)}) collective-permute-start(bf16[128,256]{1,0:T(8,128)(2,1)S(1)} %add_convert_fusion.5), channel_id=1, source_target_pairs={{0,16},{4,20},{8,24},{12,28},{16,0},{20,4},{24,8},{28,12},{1,17},{... | collective-permute-start | bytes 196616 | tf_op jit(solution)/shard_map/ppermute | solution.py:1267
  286.8 5.2 %collective-permute-start.20 = (bf16[128,256]{1,0:T(8,128)(2,1)S(1)}, bf16[128,256]{1,0:T(8,128)(2,1)S(1)}, u32[]{:S(2)}, u32[]{:S(2)}) collective-permute-start(bf16[128,256]{1,0:T(8,128)(2,1)S(1)} %add_convert_fusion.5), channel_id=1, source_target_pairs={{0,24},{4,28},{8,16},{12,20},{16,8},{20,12},{24,0},{28,4},{1,25},{... | collective-permute-start | bytes 196616 | tf_op jit(solution)/shard_map/ppermute | solution.py:1267
  288.4 17.7 %collective-permute-start.25 = (bf16[2,24,2304]{2,1,0:T(8,128)(2,1)S(1)}, bf16[2,24,2304]{2,1,0:T(8,128)(2,1)S(1)}, u32[]{:S(2)}, u32[]{:S(2)}) collective-permute-start(bf16[2,24,2304]{2,1,0:T(8,128)(2,1)S(1)} %fusion.6), channel_id=1, source_target_pairs={{0,1},{1,0},{2,3},{3,2},{4,5},{5,4},{6,7},{7,6},{8,9},{9,8},{10,11... | collective-permute-start | bytes 663560 | tf_op jit(solution)/shard_map/ppermute | solution.py:1297
  292.0 13.9 %collective-permute-start.21 = (bf16[128,256]{1,0:T(8,128)(2,1)S(1)}, bf16[128,256]{1,0:T(8,128)(2,1)S(1)}, u32[]{:S(2)}, u32[]{:S(2)}) collective-permute-start(bf16[128,256]{1,0:T(8,128)(2,1)S(1)} %add_convert_fusion.4), channel_id=1, source_target_pairs={{0,1},{1,0},{2,3},{3,2},{4,5},{5,4},{6,7},{7,6},{8,9},{9,8},{10,11... | collective-permute-start | bytes 196616 | tf_op jit(solution)/shard_map/ppermute | solution.py:1267
  292.6 13.3 %collective-permute-start.22 = (bf16[128,256]{1,0:T(8,128)(2,1)S(1)}, bf16[128,256]{1,0:T(8,128)(2,1)S(1)}, u32[]{:S(2)}, u32[]{:S(2)}) collective-permute-start(bf16[128,256]{1,0:T(8,128)(2,1)S(1)} %add_convert_fusion.4), channel_id=1, source_target_pairs={{0,2},{1,3},{2,0},{3,1},{4,6},{5,7},{6,4},{7,5},{8,10},{9,11},{10,... | collective-permute-start | bytes 196616 | tf_op jit(solution)/shard_map/ppermute | solution.py:1267
  293.2 12.8 %collective-permute-start.23 = (bf16[128,256]{1,0:T(8,128)(2,1)S(1)}, bf16[128,256]{1,0:T(8,128)(2,1)S(1)}, u32[]{:S(2)}, u32[]{:S(2)}) collective-permute-start(bf16[128,256]{1,0:T(8,128)(2,1)S(1)} %add_convert_fusion.4), channel_id=1, source_target_pairs={{0,3},{1,2},{2,1},{3,0},{4,7},{5,6},{6,5},{7,4},{8,11},{9,10},{10,... | collective-permute-start | bytes 196616 | tf_op jit(solution)/shard_map/ppermute | solution.py:1267
  306.0 1.3 collective-permute-start.24
  306.1 7.8 %collective-permute-start.26 = (bf16[24,2304]{1,0:T(8,128)(2,1)S(1)}, bf16[24,2304]{1,0:T(8,128)(2,1)S(1)}, u32[]{:S(2)}, u32[]{:S(2)}) collective-permute-start(bf16[24,2304]{1,0:T(8,128)(2,1)S(1)} %fusion.10), channel_id=1, source_target_pairs={{0,2},{1,3},{2,0},{3,1},{4,6},{5,7},{6,4},{7,5},{8,10},{9,11},{10,... | collective-permute-start | bytes 331784 | tf_op jit(solution)/shard_map/ppermute | solution.py:1297
  (53 other events, 658.8 us)
Sparse Core Ops, SparseCore 0:
  164.3 84.1 reduce-scatter.1

commit v3 on v2

--- a/solution.py
+++ b/solution.py
@@ -495,6 +495,15 @@
     )(place, table, index)
 
 
+def split_pairs(value, pairs_ref):
+    for pair in range(pairs_ref.shape[0]):
+        pairs_ref[pair] = value[:, pair * LANES : (pair + 1) * LANES]
+
+
+def join_pairs(pairs_ref):
+    return jnp.concatenate([pairs_ref[pair] for pair in range(pairs_ref.shape[0])], 1)
+
+
 def qkv_kernel(
     part,
     large,
@@ -516,7 +525,7 @@
         h_ref[...] = (normal * gain_ref[...] + shift_ref[...]).astype(NARROW)
 
     product = jnp.dot(h_ref[...], weight_ref[...], preferred_element_type=WIDE)
-    p_ref[...] = (product + bias_ref[...]).astype(NARROW)
+    split_pairs((product + bias_ref[...]).astype(NARROW), p_ref)
 
 
 def qkv_forward(place, pieces, gots, smalls, gain, shift, weight, bias, part, large, small):
@@ -540,14 +549,14 @@
             out_specs=[
                 whole(tokens, width),
                 whole(tokens, width),
-                pl.BlockSpec((tokens, width), lambda i, place: (0, i)),
+                pl.BlockSpec((width // LANES, tokens, LANES), lambda i, place: (i, 0, 0)),
             ],
             scratch_shapes=[pltpu.VMEM((tokens, width), WIDE)],
         ),
         out_shape=[
             jax.ShapeDtypeStruct((tokens, width), NARROW),
             jax.ShapeDtypeStruct((tokens, width), NARROW),
-            jax.ShapeDtypeStruct((tokens, total), NARROW),
+            jax.ShapeDtypeStruct((total // LANES, tokens, LANES), NARROW),
         ],
         compiler_params=params(48),
         cost_estimate=cost(tokens * width * total * 5e-9),
@@ -604,14 +613,14 @@
 
 
 def attention_forward(place, p, mask, own_bias, other_bias, small_bias, images):
-    tokens = p.shape[0]
+    tokens = p.shape[1]
     heads = small_bias.shape[0]
     pairs = heads // 2
     large, small, smalls = images[0][1], images[1][1], len(images) - 1
     area = large * large + smalls * small * small
 
     def column(offset):
-        return pl.BlockSpec((tokens, LANES), lambda i, place: (0, offset + i))
+        return pl.BlockSpec((None, tokens, LANES), lambda i, place: (offset + i, 0, 0))
 
     def by_pair(*shape):
         return pl.BlockSpec((2,) + shape, lambda i, place: (i,) + (0,) * len(shape))
@@ -637,7 +646,7 @@
             ],
         ),
         out_shape=[
-            jax.ShapeDtypeStruct((tokens, heads * HEAD), NARROW),
+            jax.ShapeDtypeStruct((pairs, tokens, LANES), NARROW),
             jax.ShapeDtypeStruct((heads, large, large), NARROW),
             jax.ShapeDtypeStruct((heads, smalls, small, small), NARROW),
         ],
@@ -718,13 +727,13 @@
 
 
 def attention_backward(place, p, grad_out, out, large_p, small_p, images, share, first, count):
-    tokens = p.shape[0]
+    tokens = p.shape[1]
     pairs = large_p.shape[0] // 2
     large, small, smalls = images[0][1], images[1][1], len(images) - 1
     area = large * large + smalls * small * small
 
     def column(offset):
-        return pl.BlockSpec((tokens, LANES), lambda i, place: (0, offset + first + i))
+        return pl.BlockSpec((None, tokens, LANES), lambda i, place: (offset + first + i, 0, 0))
 
     def by_pair(*shape):
         return pl.BlockSpec((2,) + shape, lambda i, place: (first + i,) + (0,) * len(shape))
@@ -744,9 +753,9 @@
                 by_pair(large, large),
                 by_pair(smalls, small, small),
             ],
-            out_specs=[pl.BlockSpec((3, tokens, LANES), lambda i, place: (0, 0, i)), share_spec, share_spec],
+            out_specs=[pl.BlockSpec((3, None, tokens, LANES), lambda i, place: (0, i, 0, 0)), share_spec, share_spec],
         ),
-        out_shape=[jax.ShapeDtypeStruct((3, tokens, count * LANES), NARROW)]
+        out_shape=[jax.ShapeDtypeStruct((3, count, tokens, LANES), NARROW)]
         + [jax.ShapeDtypeStruct((2 * count,) + share, NARROW)] * 2,
         compiler_params=params(60),
         cost_estimate=cost(2 * count * area * 4.2e-6),
@@ -804,7 +813,7 @@
 
     @pl.when(step == 0)
     def _():
-        r_ref[...] = jnp.dot(o_ref[...], proj_ref[...], preferred_element_type=WIDE) + proj_bias
+        r_ref[...] = jnp.dot(join_pairs(o_ref), proj_ref[...], preferred_element_type=WIDE) + proj_bias
         assemble(z_ref, me, part, mine_ref[...], got_refs, small_ref, large, small)
 
         @pl.loop(0, tokens // chunk)
@@ -885,12 +894,12 @@
                 dvector_ref[place : place + 1, :] += jnp.sum(term, 0, keepdims=True)
 
         dr = g_ref[...]
-        dproj = lax.dot_general(o_ref[...], dr, TN, preferred_element_type=WIDE).astype(NARROW)
+        dproj = lax.dot_general(join_pairs(o_ref), dr, TN, preferred_element_type=WIDE).astype(NARROW)
         wide_copy(steps - 1).wait()
         tall_copy(steps - 1).wait()
         wide_ref[...] = dproj
         wide_copy(steps).start()
-        do_ref[...] = lax.dot_general(dr, proj_ref[...], NT, preferred_element_type=WIDE).astype(NARROW)
+        split_pairs(lax.dot_general(dr, proj_ref[...], NT, preferred_element_type=WIDE).astype(NARROW), do_ref)
         dismantle(r_ref, me, part, back_refs, small_back_ref, large)
         wide_copy(steps).wait()
 
@@ -909,10 +918,10 @@
     shapes = [jax.ShapeDtypeStruct((part, width), NARROW)] * blk + [
         jax.ShapeDtypeStruct((tokens - large, width), NARROW),
         jax.ShapeDtypeStruct((tokens, width), WIDE),
-        jax.ShapeDtypeStruct((tokens, width), NARROW),
+        jax.ShapeDtypeStruct(out.shape, NARROW),
         jax.ShapeDtypeStruct((width, hidden + width + tall), NARROW),
         jax.ShapeDtypeStruct((8, width), WIDE),
-        jax.ShapeDtypeStruct((1, hidden), WIDE),
+        jax.ShapeDtypeStruct((steps, 1, width), WIDE),
     ]
     return pl.pallas_call(
         functools.partial(mlp_kernel, part, large, small, share, len(gots)),
@@ -929,7 +938,7 @@
             + [whole_of(got) for got in gots]
             + [
                 whole_of(smalls),
-                whole(tokens, width),
+                whole_of(out),
                 whole(tokens, width),
                 whole(width, width),
                 whole(8, width),
@@ -941,10 +950,10 @@
             + [
                 whole(tokens - large, width),
                 whole(tokens, width),
-                whole(tokens, width),
+                whole_of(out),
                 pl.BlockSpec(memory_space=pl.ANY),
                 whole(8, width),
-                pl.BlockSpec((1, width), lambda i, place: (0, feed(i))),
+                pl.BlockSpec((None, 1, width), lambda i, place: (feed(i), 0, 0)),
             ],
             scratch_shapes=[
                 pltpu.VMEM((tokens, width), WIDE),
@@ -971,7 +980,7 @@
     back_refs = refs[8 : 8 + pieces]
     small_back_ref, dvector_ref, dh_ref = refs[8 + pieces :]
     step = pl.program_id(0)
-    grad = dp_ref[0]
+    grad = join_pairs(dp_ref)
     dweight = lax.dot_general(h_ref[...], grad, TN, preferred_element_type=WIDE).astype(NARROW)
     deal_rows(dweight, half, place_ref[CORE] == 0, mine_ref, theirs_ref)
     term = lax.dot_general(grad, weight_ref[...], NT, preferred_element_type=WIDE)
@@ -1018,7 +1027,7 @@
             grid=(3,),
             in_specs=[whole_of(result) for result in results]
             + [
-                pl.BlockSpec((1, tokens, width), lambda i, place: (i, 0, 0)),
+                pl.BlockSpec((None,) + dp.shape[1:], lambda i, place: (i, 0, 0, 0)),
                 whole(tokens, width),
                 whole(tokens, width),
                 whole(tokens, width),
@@ -1077,25 +1086,31 @@
 TABLE_LANES = 256
 
 
-def table_rows(shares, index_ref, out_ref, turned_ref, left_ref, right_ref, batch):
+def table_shape(table_rows, heads):
+    groups = round_up(table_rows, TABLE_LANES) // TABLE_LANES
+    unit = 2 * round_up(heads, 4)
+    return groups, unit, round_up(groups * unit, 32)
+
+
+def table_rows(own_ref, other_ref, index_ref, out_ref, turned_ref, left_ref, right_ref, unit, batch):
     rows, lanes = index_ref.shape
-    groups = out_ref.shape[0] // 32
+    height = out_ref.shape[0]
+    half = unit // 2
     top = jnp.zeros((8, lanes), WIDE)
-    head = 0
-    for own_ref, other_ref in shares:
-        for number in range(own_ref.shape[0]):
-            value = own_ref[number].astype(WIDE) + other_ref[number].astype(WIDE)
-            turned_ref[:, head, :lanes] = value
-            size = jnp.abs(value)
-            for first in range(0, rows, 8):
-                top = jnp.maximum(top, size[first : first + 8])
-            head += 1
+    for head in range(own_ref.shape[0]):
+        value = own_ref[head].astype(WIDE) + other_ref[head].astype(WIDE)
+        turned_ref[:, head, :lanes] = value
+        size = jnp.abs(value)
+        for first in range(0, rows, 8):
+            top = jnp.maximum(top, size[first : first + 8])
     peak = jnp.maximum(jnp.max(top, keepdims=True), 1e-30)
     scale = 256.0 / peak
     back = peak * (1.0 / 256.0)
     zero = jnp.zeros((), TERM)
     one = jnp.ones((), TERM)
     codes = (lax.broadcasted_iota(jnp.int32, (TABLE_LANES, LANES), 0) - 128).astype(jnp.int8)
+    is_upper = lax.broadcasted_iota(jnp.int32, (unit, LANES), 0) < half
+    row_group = lax.broadcasted_iota(jnp.int32, (height, LANES), 0) // unit
     columns = slice(0, batch * lanes)
 
     def some_rows(part, carry):
@@ -1110,15 +1125,20 @@
                 chosen = jnp.broadcast_to(low[:, here], (TABLE_LANES, LANES)).astype(jnp.int8)
                 right_ref[:, there] = jnp.where(codes == chosen, one, zero)
                 value = turned_ref[row, :, here] * scale
-                upper = value.astype(TERM)
-                lower = ((value - upper.astype(WIDE)) * 16.0).astype(TERM)
-                both = jnp.concatenate([upper, lower], 0)
-                wide_high = jnp.broadcast_to(high[:, here], both.shape).astype(jnp.int8)
-                for group in range(groups):
-                    left_ref[group * 32 : group * 32 + 32, there] = jnp.where(
-                        wide_high == jnp.int8(group), both, zero
-                    )
-        left = left_ref[: groups * 32, columns]
+                value = jnp.concatenate([value[:half], value[:half]], 0)
+                upper = value.astype(TERM).astype(WIDE)
+                value = jnp.where(is_upper, upper, (value - upper) * 16.0)
+                eighths = [value[eight : eight + 8] for eight in range(0, unit, 8)]
+                wide_high = jnp.broadcast_to(high[:, here], (32, LANES)).astype(jnp.int8)
+                turns = {}
+                for tile in range(height // 32):
+                    turn = tile * 4 % len(eighths)
+                    if turn not in turns:
+                        picked = [eighths[(turn + place) % len(eighths)] for place in range(4)]
+                        turns[turn] = jnp.concatenate(picked, 0).astype(TERM)
+                    group = row_group[tile * 32 : tile * 32 + 32].astype(jnp.int8)
+                    left_ref[tile * 32 : tile * 32 + 32, there] = jnp.where(wide_high == group, turns[turn], zero)
+        left = left_ref[:height, columns]
         term = lax.dot_general(left, right_ref[:, columns], NT, preferred_element_type=WIDE)
         out_ref[...] += term * back
         return carry
@@ -1126,66 +1146,56 @@
     lax.fori_loop(0, rows // batch, some_rows, 0)
 
 
-def table_jobs(counts, batch, ins, outs, turned_ref, left_ref, right_ref):
+def table_kernel(slots, counts, shapes, heads, batch, last, place_ref, *refs):
+    ins, refs = refs[: 3 * len(counts)], refs[3 * len(counts) :]
+    if last:
+        before, (vector_ref, mine_ref, theirs_ref), refs = refs[: len(shapes)], refs[len(shapes) :][:3], refs[len(shapes) + 3 :]
+    totals, scratch = refs[: len(shapes)], refs[len(shapes) :]
     step = pl.program_id(0)
+
+    @pl.when(step == 0)
+    def _():
+        scratch[0][...] = jnp.zeros_like(scratch[0])
+        for number, total_ref in enumerate(totals):
+            total_ref[...] = before[number][...] if last else jnp.zeros_like(total_ref)
+
     start = 0
     for job, count in enumerate(counts):
-        own_ref, other_ref, index_ref = ins[3 * job : 3 * job + 3]
 
         @pl.when((step >= start) & (step < start + count))
         def _():
-            table_rows([(own_ref, other_ref)], index_ref, outs[job], turned_ref, left_ref, right_ref, batch)
+            slot = slots[job]
+            table_rows(*ins[3 * job : 3 * job + 3], totals[slot], *scratch, shapes[slot][1], batch)
 
         start += count
 
-
-def table_kernel(counts, batch, place_ref, *refs):
-    ins, outs, scratch = refs[: 3 * len(counts)], refs[3 * len(counts) : 4 * len(counts)], refs[4 * len(counts) :]
-
-    @pl.when(pl.program_id(0) == 0)
-    def _():
-        scratch[0][...] = jnp.zeros_like(scratch[0])
-        for out_ref in outs:
-            out_ref[...] = jnp.zeros_like(out_ref)
-
-    table_jobs(counts, batch, ins, outs, *scratch)
-
-
-def joined_terms(value):
-    value = value.reshape(-1, 2, 16, TABLE_LANES)
-    return (value[:, 0] + value[:, 1] * (1 / 16)).reshape(-1, TABLE_LANES)
-
-
-def table_last_kernel(counts, batch, place_ref, *refs):
-    own_ref, other_ref, index_ref, large_ref, small_ref, vector_ref, mine_ref, theirs_ref = refs[:8]
-    total_ref, scratch = refs[8], refs[9:]
-
-    @pl.when(pl.program_id(0) == 0)
-    def _():
-        scratch[0][...] = jnp.zeros_like(scratch[0])
-        total_ref[...] = large_ref[...]
-
-    table_jobs(counts, batch, (own_ref, other_ref, index_ref), [total_ref], *scratch)
-
-    @pl.when(pl.program_id(0) == pl.num_programs(0) - 1)
-    def _():
-        rows = [joined_terms(total_ref[...]), joined_terms(small_ref[...]), vector_ref[...]]
-        rows = jnp.concatenate(rows, 0).astype(NARROW).astype(WIDE)
-        half = rows.shape[0] // 2
-        is_first = place_ref[CORE] == 0
-        mine_ref[...] = jnp.where(is_first, rows[:half], rows[half:]).astype(NARROW)
-        theirs_ref[...] = jnp.where(is_first, rows[half:], rows[:half]).astype(NARROW)
-
-
-def table_gradient_sum(place, own, other, jobs, last=None):
+    if last:
+
+        @pl.when(step == start - 1)
+        def _():
+            rows = []
+            for total_ref, (groups, unit, _) in zip(totals, shapes):
+                for group in range(groups):
+                    first, second = group * unit, group * unit + unit // 2
+                    rows.append(total_ref[first : first + heads, :] + total_ref[second : second + heads, :] * (1 / 16))
+            rows = jnp.concatenate(rows + [vector_ref[...]], 0)
+            half = rows.shape[0] // 2
+            is_first = place_ref[CORE] == 0
+            mine_ref[...] = jnp.where(is_first, rows[:half], rows[half:]).astype(NARROW)
+            theirs_ref[...] = jnp.where(is_first, rows[half:], rows[:half]).astype(NARROW)
+
+
+def table_gradients(place, own, other, tables, jobs, before=None, vectors=None):
     step, batch = 16, 8
     heads = own.shape[0]
+    last = before is not None
     in_specs, args = [], []
-    lanes = [index.shape[1] for index, *_ in jobs]
-    groups = [round_up(rows, TABLE_LANES) // TABLE_LANES for _, rows, *_ in jobs]
+    shapes = [table_shape(rows, heads) for rows in tables]
+    slots = [job[0] for job in jobs]
+    lanes = [job[1].shape[1] for job in jobs]
     counts = [job[-1] for job in jobs]
     start = 0
-    for (index, _, share_first, index_first, count), width in zip(jobs, lanes):
+    for (_, index, share_first, index_first, count), width in zip(jobs, lanes):
         total = index.shape[0] // 2 // step
 
         def local(i, start=start, count=count):
@@ -1209,23 +1219,23 @@
         )
         args += [own, other, index]
         start += count
+    tall = max(height for *_, height in shapes)
+    sums = [jax.ShapeDtypeStruct((height, TABLE_LANES), WIDE) for *_, height in shapes]
     scratch = [
         pltpu.VMEM((step, 16, max(lanes)), WIDE),
-        pltpu.VMEM((max(groups) * 32, batch * max(lanes)), TERM),
+        pltpu.VMEM((tall, batch * max(lanes)), TERM),
         pltpu.VMEM((TABLE_LANES, batch * max(lanes)), TERM),
     ]
-    if last is None:
-        kernel = table_kernel
-        out_shape = [jax.ShapeDtypeStruct((group * 32, TABLE_LANES), WIDE) for group in groups]
+    if last:
+        args += before + [vectors]
+        in_specs += [whole_of(value) for value in before + [vectors]]
+        rows = sum(groups * heads for groups, *_ in shapes) + vectors.shape[0]
+        out_shape = [jax.ShapeDtypeStruct((rows // 2, TABLE_LANES), NARROW)] * 2
+        scratch = [pltpu.VMEM(value.shape, WIDE) for value in sums] + scratch
     else:
-        kernel = table_last_kernel
-        in_specs += [whole_of(value) for value in last]
-        args += last
-        rows = last[0].shape[0] // 2 + last[1].shape[0] // 2 + last[2].shape[0]
-        out_shape = [jax.ShapeDtypeStruct((rows // 2, TABLE_LANES), NARROW)] * 2
-        scratch.insert(0, pltpu.VMEM(last[0].shape, WIDE))
+        out_shape = sums
     return pl.pallas_call(
-        functools.partial(kernel, counts, batch),
+        functools.partial(table_kernel, slots, counts, shapes, heads, batch, last),
         grid_spec=pltpu.PrefetchScalarGridSpec(
             num_scalar_prefetch=1,
             grid=(start,),
@@ -1236,7 +1246,7 @@
         out_shape=out_shape,
         compiler_params=params(48),
         cost_estimate=cost(start * step * max(lanes) * 1.6e-4),
-        name="table_gradient",
+        name="table_gradients",
     )(place, *args)
 
 
@@ -1435,67 +1445,69 @@
 
     qkv_got = swap_bit(qkv_theirs, img, 0)
     backs[1:] = send_round(backs[1:], blk)
+    sums = jnp.concatenate([mlp_sums[:6], qkv_sums[:4], dinner_bias[:, 0]], 0).reshape(-1, TABLE_LANES)
+    table_sizes = [heads * table_shape(table.shape[0], heads)[0] for table in (table_large, table_small)]
+    sums = jnp.pad(sums, ((0, -(sums.shape[0] + sum(table_sizes)) % 32), (0, 0)))
     middle = 3 * width // 2
     columns = (slice(0, middle), slice(middle, None))
-    last = [Tree([qkv_mine[:, part], qkv_got[:, part]], dims) for part in columns]
-    sums = jnp.concatenate([mlp_sums[:6], qkv_sums[:4], dinner_bias.reshape(-1, width)], 0).reshape(-1, TABLE_LANES)
-    table_sizes = [round_up(table.shape[0], TABLE_LANES) // TABLE_LANES * 16 for table in (table_large, table_small)]
-    sums = jnp.pad(sums, ((0, -(sums.shape[0] + sum(table_sizes)) % 32), (0, 0)))
-    steps = large // 32
-    mark = steps * 2 // 5
-
-    sends = cut(last, 0)
+    trees = [Tree([qkv_mine[:, part], qkv_got[:, part]], dims) for part in columns]
+    sends = cut(trees, 0)
     sends, sums, spread_large, spread_small = together(sends, sums, spread_large, spread_small)
     gots = move(0, sends)
-    large_sum, small_sum = table_gradient_sum(
+    tables = [table_small.shape[0], table_large.shape[0]]
+    steps = large // 32
+    mark = steps * 4 // 7
+    small_total, large_total = table_gradients(
         place,
         own_share,
         other_share,
-        [
-            (spread_large, table_large.shape[0], 0, 0, mark),
-            (spread_small, table_small.shape[0], steps, 0, double // 32),
-        ],
-    )
-    large_sum, small_sum, gots, spread_large, feed_part = together(large_sum, small_sum, gots, spread_large, feed_part)
-    add(last, gots)
-    sends = cut(last, 1)
-    feed_tree = Tree([feed_part], blk_bits[::-1])
-    feed_send = feed_tree.cut(*blk_bits[0])
-    sends, feed_send, spread_large = together(sends, feed_send, spread_large)
+        tables,
+        [(0, spread_small, steps, 0, double // 32), (1, spread_large, 0, 0, mark)],
+    )
+    small_total, large_total, gots, spread_large, sums, feed_part = together(
+        small_total, large_total, gots, spread_large, sums, feed_part
+    )
+    add(trees, gots)
+    feed_sum = lax.psum_scatter(feed_part, "blk", scatter_dimension=0, tiled=True)
+    sends = cut(trees, 1)
+    sends, sums, spread_large = together(sends, sums, spread_large)
     gots = move(1, sends)
-    feed_got = swap(feed_send, *blk_bits[0], sizes)
-    mine, theirs = table_gradient_sum(
+    mine, theirs = table_gradients(
         place,
         own_share,
         other_share,
-        [(spread_large, table_large.shape[0], mark, mark, steps - mark)],
-        [large_sum, small_sum, sums],
-    )
-    mine, theirs, gots, feed_got, backs = together(mine, theirs, gots, feed_got, backs)
-    add(last, gots)
-    feed_tree.terms.append(feed_got)
-
-    joined = add_low(mine, swap_bit(theirs, img, 0))
-    joined = sum_group(joined, "img", [2 * m for m in range(1, img // 2)], img)
-    last = Tree([jnp.concatenate([tree.terms[number] for tree in last], -1) for number in range(4)], dims[2:])
-    tail = [last, feed_tree]
-    for axis, bit in blk_bits:
-        for tree in tail:
-            if (axis, bit) in tree.bits:
-                got = swap(tree.cut(axis, bit), axis, bit, sizes)
-                tree.terms.append(got)
+        tables,
+        [(1, spread_large, mark, mark, steps - mark)],
+        [small_total, large_total],
+        sums,
+    )
+    mine, theirs, gots, backs = together(mine, theirs, gots, backs)
+
+    core_got = swap_bit(theirs, img, 0)
+    add(trees, gots)
+    last = Tree([jnp.concatenate([tree.terms[number] for tree in trees], -1) for number in range(4)], dims[2:])
+    send = last.cut(*blk_bits[0])
+    send, core_got = together(send, core_got)
+    got = swap(send, *blk_bits[0], sizes)
+    joined = sum_group(add_low(mine, core_got), "img", [2 * m for m in range(1, img // 2)], img)
+    joined, got, feed_sum = together(joined, got, feed_sum)
+    last.terms.append(got)
+    send = last.cut(*blk_bits[1])
+    last.terms.append(swap(send, *blk_bits[1], sizes))
     joined = sum_group(joined, "blk", range(1, blk), blk)
     other = swap_bit(joined, img, 0)
+    last_sum, feed_sum = last.total(), feed_sum.astype(WIDE)
+    result_large, result_small, grad_large, grad_small = place_results(
+        place, backs, [result_small, grad_small], rows, small, smalls, small_rows
+    )
     joined = jnp.where(core == 0, jnp.stack([joined, other]), jnp.stack([other, joined]))
     joined = joined.reshape(-1, TABLE_LANES).astype(WIDE)
-    last_sum, feed_sum = last.total(), feed_tree.total()
-    result_large, result_small, grad_large, grad_small = place_results(
-        place, backs, [result_small, grad_small], rows, small, smalls, small_rows
-    )
+    outs = []
     outs = []
     first = 0
-    for table, count in zip((table_large, table_small), table_sizes):
-        value = joined[first : first + count].reshape(-1, 16, TABLE_LANES)[:, :heads]
+    table_sizes.reverse()
+    for table, count in zip((table_small, table_large), table_sizes):
+        value = joined[first : first + count].reshape(-1, heads, TABLE_LANES)
         outs.append(jnp.transpose(value, (0, 2, 1)).reshape(-1, heads)[: table.shape[0]])
         first += count
     sums = joined[first:].reshape(-1)
@@ -1514,8 +1526,8 @@
         last_sum,
         own(6),
         own(7),
+        outs[1],
         outs[0],
-        outs[1],
         feed_sum[:, hidden : hidden + width],
         own(5),
         own(4),

time: 325 us -> 319 us (0.982)
  waiting for transfers between devices: 20.5 us -> 16.5 us
  local copies, waits for them, and re-layouts: 31.3 us -> 35 us
    ppermute x6, waiting for transfers between devices: 8.12 us -> 2.79 us  [sum_group(): got = lax.ppermute(value, axis, [(i, i ^ pattern) for i in range(size)])]
    ppermute x8 -> x6, waiting for transfers between devices: 6.45 us -> 10.9 us  [swap(): lax.ppermute(value, axis, [(i, i ^ 1 << bit) for i in range(sizes[axis])])]
    ppermute x8 -> x6, starting transfers between devices: 9.9 us -> 6.67 us  [swap(): lax.ppermute(value, axis, [(i, i ^ 1 << bit) for i in range(sizes[axis])])]
    unnamed x122 -> x135, local copies, waits for them, and re-layouts: 16.1 us -> 18.4 us
  transfers between devices with their start and end apart: 29 -> 28, of which waited for: 8 -> 4; matrix products, arithmetic and copies ran while one was open for 7% -> 8% of each run, Pallas kernels for 44% -> 45%
where the time goes in v3:
time: 319 us; the launch traced here: 316 us
  Pallas kernels  201 us (63%)
  starting transfers between devices  42.5 us (13%)
  local copies, waits for them, and re-layouts  35 us (11%)
  waiting for transfers between devices  16.5 us (5%)
  between operations  15.7 us (5%)
  other arithmetic  5.81 us (2%)
    pallas_call x1, Pallas kernels, mlp_pass(): pl.pallas_call(functools.partial(mlp_kernel, part, large, small, share, l...  59.8 us
    pallas_call x2, Pallas kernels, table_gradients(): pl.pallas_call(functools.partial(table_kernel, slots, counts, shapes, hea...  38 us
    pallas_call x2, Pallas kernels, bias_lookup(): pl.pallas_call(functools.partial(bias_kernel, heads, groups), grid_spec=p...  28.2 us
    ppermute x9, starting transfers between devices, rotate(): lax.ppermute(value, axis, [(i, (i + shift) % size) for i in range(size)])  27.2 us
    pallas_call x1, Pallas kernels, attention_backward(): pl.pallas_call(functools.partial(attention_backward_kernel, images), grid...  24.4 us
    pallas_call x1, Pallas kernels, attention_forward(): pl.pallas_call(functools.partial(attention_forward_kernel, images), grid_...  21 us
    unnamed x135, local copies, waits for them, and re-layouts  18.4 us
    pallas_call x1, Pallas kernels, qkv_backward(): pl.pallas_call(functools.partial(qkv_backward_kernel, part, large, blk *...  17.1 us
  transfers between devices with their start and end apart: 28, of which 4 were waited for; matrix products, arithmetic and copies ran while one was open for 8% of the time, Pallas kernels for 45%

profile of v3, /device:TPU:0, one launch (start us, length us, event | category | flops | bytes accessed | tf_op | source)
XLA Modules:
  0.0 316.0 jit_solution(17677919816809654221)
XLA Ops:
  9.5 3.0 collective-permute-start
  12.5 2.6 collective-permute-start.1
  19.6 3.2 %bias_lookup.2.small_bias_ref = bf16[12,224,256]{2,1,0:T(8,128)(2,1)S(1)} custom-call(s32[2]{0:T(128)S(1)} %pad_add_fusion.place_ref, f32[72,8,128]{2,1,0:T(8,128)S(1)} %broadcast_in_dim.61.table_ref, s32[224,256]{1,0:T(8,128)S(1)} %copy-done.6), custom_call_target="tpu_custom_call" | custom-call | flops 2848849920 | bytes 7927234 | tf_op jit(solution)/shard_map/bias_lookup/pallas_call | solution.py:480
  24.0 1.4 copy-done.10
  25.5 25.0 %bias_lookup.3.own_bias_ref = bf16[12,304,640]{2,1,0:T(8,128)(2,1)} custom-call(s32[2]{0:T(128)S(1)} %pad_add_fusion.place_ref, f32[216,8,128]{2,1,0:T(8,128)S(1)} %broadcast_in_dim.58.table_ref, s32[608,640]{1,0:T(8,128)S(1)} %copy-done.10), custom_call_target="tpu_custom_call" | custom-call | flops 28997222400 | bytes 80687920 | tf_op jit(solution)/shard_map/bias_lookup/pallas_call | solution.py:480
  55.1 9.0 %qkv_forward.1 = (bf16[1024,768]{1,0:T(8,128)(2,1)S(1)}, bf16[1024,768]{1,0:T(8,128)(2,1)S(1)}, bf16[18,1024,128]{2,1,0:T(8,128)(2,1)}) custom-call(s32[2]{0:T(128)S(1)} %pad_add_fusion.place_ref, bf16[4,146,768]{2,1,0:T(8,128)(2,1)S(1)} %copy.78.mine_ref, bf16[146,768]{1,0:T(8,128)(2,1)S(1)} %collective-permute-done.refs_0_, ...), custom_call_target="tpu_custom_call" | custom-call | flops 10418651136 | bytes 28991028 | tf_op jit(solution)/shard_map/qkv_forward/pallas_call | solution.py:535
  67.4 13.9 %collective-permute-start.6 = (bf16[146,768]{1,0:T(8,128)(2,1)S(1)}, bf16[146,768]{1,0:T(8,128)(2,1)S(1)}, u32[]{:S(2)}, u32[]{:S(2)}) collective-permute-start(bf16[146,768]{1,0:T(8,128)(2,1)S(1)} %get-tuple-element.139), channel_id=1, source_target_pairs={{0,3},{1,0},{2,1},{3,2},{4,7},{5,4},{6,5},{7,6},{8,11},{9,8},{10,9... | collective-permute-start | bytes 672776 | tf_op jit(solution)/shard_map/ppermute | solution.py:1254
  82.3 21.0 %attention_forward.1 = (bf16[6,1024,128]{2,1,0:T(8,128)(2,1)}, bf16[12,608,608]{2,1,0:T(8,128)(2,1)}, bf16[12,2,208,208]{3,2,1,0:T(8,128)(2,1)}) custom-call(s32[2]{0:T(128)} %copy-done.3, bf16[18,1024,128]{2,1,0:T(8,128)(2,1)} %get-tuple-element.130.q_ref.k_ref.v_ref, bf16[18,1024,128]{2,1,0:T(8,128)(2,1)} %get-tuple-element.130.q_ref.k_ref.v_ref, ...), custom_call_target="tpu_custom_call" | custom-call | flops 23922708480 | bytes 66567536 | tf_op jit(solution)/shard_map/attention_forward/pallas_call | solution.py:628
  104.2 59.8 %mlp_pass.1 = (bf16[152,768]{1,0:T(8,128)(2,1)}, bf16[152,768]{1,0:T(8,128)(2,1)}, bf16[152,768]{1,0:T(8,128)(2,1)}, bf16[152,768]{1,0:T(8,128)(2,1)}, bf16[416,...) custom-call(s32[2]{0:T(128)} %copy-done.3, ...), custom_call_target="tpu_custom_call" | custom-call | flops 66679365632 | bytes 185542592 | tf_op jit(solution)/shard_map/mlp_pass/pallas_call | solution.py:926
  164.1 24.4 %attention_backward.1 = (bf16[3,6,1024,128]{3,2,1,0:T(8,128)(2,1)}, bf16[12,416,640]{2,1,0:T(8,128)(2,1)}, bf16[12,416,640]{2,1,0:T(8,128)(2,1)}) custom-call(s32[2]{0:T(128)} %copy-done.3, bf16[18,1024,128]{2,1,0:T(8,128)(2,1)} %get-tuple-element.130.q_ref.k_ref.v_ref, bf16[18,1024,128]{2,1,0:T(8,128)(2,1)} %get-tuple-element.130.q_ref.k_ref.v_ref, ...), custom_call_target="tpu_custom_call" | custom-call | flops 26440888320 | bytes 73574648 | tf_op jit(solution)/shard_map/attention_backward/pallas_call | solution.py:742
  189.6 17.1 %qkv_backward.1 = (bf16[384,2304]{1,0:T(8,128)(2,1)}, bf16[384,2304]{1,0:T(8,128)(2,1)}, bf16[2,152,768]{2,1,0:T(8,128)(2,1)S(1)}, bf16[2,152,768]{2,1,0:T(8,128...) custom-call(s32[2]{0:T(128)S(1)} %copy-done.4, ...), custom_call_target="tpu_custom_call" | custom-call | flops 17364418560 | bytes 48318384 | tf_op jit(solution)/shard_map/qkv_backward/pallas_call | solution.py:1023
  209.7 1.4 collective-permute-start.14
  211.1 2.8 collective-permute-start.15
  214.0 1.6 fusion.28
  216.4 1.7 fusion.29
  218.4 1.6 collective-permute-start.10
  220.0 1.6 collective-permute-start.9
  221.6 23.5 %table_gradients.2 = (f32[96,256]{1,0:T(8,128)S(1)}, f32[224,256]{1,0:T(8,128)S(1)}) custom-call(s32[2]{0:T(128)S(1)} %copy-done.4, bf16[12,416,640]{2,1,0:T(8,128)(2,1)} %get-tuple-element.151.refs_0_.refs_3_, bf16[12,416,640]{2,1,0:T(8,128)(2,1)} %collective-permute-done.7.refs_1_.refs_4_, s32[224,256]{1,0:T(8,128)S(1)} %copy-done.7, ...), custom_call_target="tpu_custom_call" | custom-call | flops 32030720000 | bytes 89128960 | tf_op jit(solution)/shard_map/table_gradients/pallas_call | solution.py:1237
  246.7 2.8 reduce-scatter.3.cloned.1.call-done
  249.5 2.3 fusion.2
  253.9 1.4 copy-done.12
  255.3 14.5 %table_gradients.3 = (bf16[96,256]{1,0:T(8,128)(2,1)S(1)}, bf16[96,256]{1,0:T(8,128)(2,1)S(1)}) custom-call(s32[2]{0:T(128)S(1)} %copy-done.4, bf16[12,416,640]{2,1,0:T(8,128)(2,1)} %get-tuple-element.151.refs_0_.refs_3_, bf16[12,416,640]{2,1,0:T(8,128)(2,1)} %collective-permute-done.7.refs_1_.refs_4_, s32[608,640]{1,0:T(8,128)S(1)} %copy-done.12, ...), custom_call_target="tpu_custom_call" | custom-call | flops 16957440000 | bytes 47185920 | tf_op jit(solution)/shard_map/table_gradients/pallas_call | solution.py:1237
  273.3 1.4 collective-permute-start.17
  275.3 1.5 collective-permute-start.19
  276.8 1.8 place_results.1
  281.2 1.5 collective-permute-start.20
  282.7 6.3 %collective-permute-done.20 = bf16[2,24,2304]{2,1,0:T(8,128)(2,1)S(1)} collective-permute-done((bf16[2,24,2304]{2,1,0:T(8,128)(2,1)S(1)}, bf16[2,24,2304]{2,1,0:T(8,128)(2,1)S(1)}, u32[]{:S(2)}, u32[]{:S(2)}) %collective-permute-start.20) | collective-permute-done | bytes 221216 | tf_op jit(solution)/shard_map/ppermute | solution.py:1307
  289.6 2.4 collective-permute-start.22
  293.4 1.7 fusion.30
  295.1 2.8 collective-permute-done.23
  298.2 1.4 slice.63
  303.4 4.5 %collective-permute-done.25 = bf16[24,2304]{1,0:T(8,128)(2,1)S(1)} collective-permute-done((bf16[24,2304]{1,0:T(8,128)(2,1)S(1)}, bf16[24,2304]{1,0:T(8,128)(2,1)S(1)}, u32[]{:S(2)}, u32[]{:S(2)}) %collective-permute-start.25) | collective-permute-done | bytes 110624 | tf_op jit(solution)/shard_map/ppermute | solution.py:1307
  (243 shorter events, 39.2 us)
Async XLA Ops:
  7.2 242.3 %reduce-scatter.3.cloned.1.call-start = ((), (), s32[]{:S(2)}) async-start(), calls=%async_computation.2 | async-start | bytes 11943936 | tf_op jit(solution)/shard_map/reduce_scatter | solution.py:1434
  9.5 41.0 %collective-permute-start = (bf16[146,768]{1,0:T(8,128)(2,1)}, bf16[146,768]{1,0:T(8,128)(2,1)S(1)}, u32[]{:S(2)}, u32[]{:S(2)}) collective-permute-start(bf16[146,768]{1,0:T(8,128)(2,1)} %get-tuple-element.291), channel_id=1, source_target_pairs={{0,1},{1,2},{2,3},{3,0},{4,5},{5,6},{6,7},{7,4},{8,9},{9,10},{10,1... | collective-permute-start | bytes 672776 | tf_op jit(solution)/shard_map/ppermute | solution.py:1254
  12.5 38.0 %collective-permute-start.1 = (bf16[146,768]{1,0:T(8,128)(2,1)}, bf16[146,768]{1,0:T(8,128)(2,1)S(1)}, u32[]{:S(2)}, u32[]{:S(2)}) collective-permute-start(bf16[146,768]{1,0:T(8,128)(2,1)} %get-tuple-element.290), channel_id=1, source_target_pairs={{0,2},{1,3},{2,0},{3,1},{4,6},{5,7},{6,4},{7,5},{8,10},{9,11},{10,... | collective-permute-start | bytes 672776 | tf_op jit(solution)/shard_map/ppermute | solution.py:1254
  15.1 35.4 %collective-permute-start.2 = (bf16[146,768]{1,0:T(8,128)(2,1)}, bf16[146,768]{1,0:T(8,128)(2,1)S(1)}, u32[]{:S(2)}, u32[]{:S(2)}) collective-permute-start(bf16[146,768]{1,0:T(8,128)(2,1)} %get-tuple-element.289), channel_id=1, source_target_pairs={{0,3},{1,0},{2,1},{3,2},{4,7},{5,4},{6,5},{7,6},{8,11},{9,8},{10,9... | collective-permute-start | bytes 672776 | tf_op jit(solution)/shard_map/ppermute | solution.py:1254
  19.6 35.5 %copy-start.3 = (s32[2]{0:T(128)}, s32[2]{0:T(128)S(1)}, u32[]{:S(2)}) copy-start(s32[2]{0:T(128)S(1)} %pad_add_fusion.place_ref) | copy-start | bytes 28
  25.5 27.9 %copy-start.60 = (s32[2]{0:T(128)S(1)}, s32[2]{0:T(128)}, u32[]{:S(2)}) copy-start(s32[2]{0:T(128)} %param.30) | copy-start | bytes 28
  25.5 28.1 %copy-start.61 = (s32[4]{0:T(128)S(1)}, s32[4]{0:T(128)}, u32[]{:S(2)}) copy-start(s32[4]{0:T(128)} %param.29) | copy-start | bytes 52
  50.5 15.9 %collective-permute-start.3 = (bf16[12,304,640]{2,1,0:T(8,128)(2,1)}, bf16[12,304,640]{2,1,0:T(8,128)(2,1)}, u32[]{:S(2)}, u32[]{:S(2)}) collective-permute-start(bf16[12,304,640]{2,1,0:T(8,128)(2,1)} %bias_lookup.3.own_bias_ref), channel_id=1, source_target_pairs={{0,4},{4,0},{8,12},{12,8},{16,20},{20,16},{24,28},{28,24},{1,5},{5... | collective-permute-start | bytes 14008328 | tf_op jit(solution)/shard_map/ppermute | solution.py:1258
  66.4 36.9 %collective-permute-start.4 = (bf16[146,768]{1,0:T(8,128)(2,1)S(1)}, bf16[146,768]{1,0:T(8,128)(2,1)S(1)}, u32[]{:S(2)}, u32[]{:S(2)}) collective-permute-start(bf16[146,768]{1,0:T(8,128)(2,1)S(1)} %get-tuple-element.137), channel_id=1, source_target_pairs={{0,1},{1,2},{2,3},{3,0},{4,5},{5,6},{6,7},{7,4},{8,9},{9,10},{10,1... | collective-permute-start | bytes 672776 | tf_op jit(solution)/shard_map/ppermute | solution.py:1254
  67.1 36.2 %collective-permute-start.5 = (bf16[146,768]{1,0:T(8,128)(2,1)S(1)}, bf16[146,768]{1,0:T(8,128)(2,1)S(1)}, u32[]{:S(2)}, u32[]{:S(2)}) collective-permute-start(bf16[146,768]{1,0:T(8,128)(2,1)S(1)} %get-tuple-element.138), channel_id=1, source_target_pairs={{0,2},{1,3},{2,0},{3,1},{4,6},{5,7},{6,4},{7,5},{8,10},{9,11},{10,... | collective-permute-start | bytes 672776 | tf_op jit(solution)/shard_map/ppermute | solution.py:1254
  67.4 35.9 %collective-permute-start.6 = (bf16[146,768]{1,0:T(8,128)(2,1)S(1)}, bf16[146,768]{1,0:T(8,128)(2,1)S(1)}, u32[]{:S(2)}, u32[]{:S(2)}) collective-permute-start(bf16[146,768]{1,0:T(8,128)(2,1)S(1)} %get-tuple-element.139), channel_id=1, source_target_pairs={{0,3},{1,0},{2,1},{3,2},{4,7},{5,4},{6,5},{7,6},{8,11},{9,8},{10,9... | collective-permute-start | bytes 672776 | tf_op jit(solution)/shard_map/ppermute | solution.py:1254
  164.1 125.0 %reduce-scatter.5.cloned.1.call-start = ((), (), s32[]{:S(2)}) async-start(), calls=%async_computation.3 | async-start | bytes 1658880 | tf_op jit(solution)/shard_map/reduce_scatter | solution.py:1471
  188.6 19.7 %collective-permute-start.7 = (bf16[12,416,640]{2,1,0:T(8,128)(2,1)}, bf16[12,416,640]{2,1,0:T(8,128)(2,1)}, u32[]{:S(2)}, u32[]{:S(2)}) collective-permute-start(bf16[12,416,640]{2,1,0:T(8,128)(2,1)} %get-tuple-element.166), channel_id=1, source_target_pairs={{0,4},{4,0},{8,12},{12,8},{16,20},{20,16},{24,28},{28,24},{1,5},{5... | collective-permute-start | bytes 19169288 | tf_op jit(solution)/shard_map/ppermute | solution.py:1258
  208.2 8.2 %collective-permute-start.8 = (bf16[384,2304]{1,0:T(8,128)(2,1)}, bf16[384,2304]{1,0:T(8,128)(2,1)}, u32[]{:S(2)}, u32[]{:S(2)}) collective-permute-start(bf16[384,2304]{1,0:T(8,128)(2,1)} %get-tuple-element.169), channel_id=1, source_target_pairs={{0,4},{4,0},{8,12},{12,8},{16,20},{20,16},{24,28},{28,24},{1,5},{5... | collective-permute-start | bytes 5308424 | tf_op jit(solution)/shard_map/ppermute | solution.py:1258
  208.7 62.3 %collective-permute-start.13 = (bf16[2,152,768]{2,1,0:T(8,128)(2,1)S(1)}, bf16[2,152,768]{2,1,0:T(8,128)(2,1)S(1)}, u32[]{:S(2)}, u32[]{:S(2)}) collective-permute-start(bf16[2,152,768]{2,1,0:T(8,128)(2,1)S(1)} %get-tuple-element.196), channel_id=1, source_target_pairs={{0,1},{1,2},{2,3},{3,0},{4,5},{5,6},{6,7},{7,4},{8,9},{9,10},{10,1... | collective-permute-start | bytes 1400840 | tf_op jit(solution)/shard_map/ppermute | solution.py:1254
  209.7 61.3 %collective-permute-start.14 = (bf16[2,152,768]{2,1,0:T(8,128)(2,1)S(1)}, bf16[2,152,768]{2,1,0:T(8,128)(2,1)S(1)}, u32[]{:S(2)}, u32[]{:S(2)}) collective-permute-start(bf16[2,152,768]{2,1,0:T(8,128)(2,1)S(1)} %get-tuple-element.197), channel_id=1, source_target_pairs={{0,2},{1,3},{2,0},{3,1},{4,6},{5,7},{6,4},{7,5},{8,10},{9,11},{10,... | collective-permute-start | bytes 1400840 | tf_op jit(solution)/shard_map/ppermute | solution.py:1254
  211.1 59.9 %collective-permute-start.15 = (bf16[2,152,768]{2,1,0:T(8,128)(2,1)S(1)}, bf16[2,152,768]{2,1,0:T(8,128)(2,1)S(1)}, u32[]{:S(2)}, u32[]{:S(2)}) collective-permute-start(bf16[2,152,768]{2,1,0:T(8,128)(2,1)S(1)} %get-tuple-element.198), channel_id=1, source_target_pairs={{0,3},{1,0},{2,1},{3,2},{4,7},{5,4},{6,5},{7,6},{8,11},{9,8},{10,9... | collective-permute-start | bytes 1400840 | tf_op jit(solution)/shard_map/ppermute | solution.py:1254
  218.1 27.0 %copy-start.27 = (bf16[384,1152]{1,0:T(8,128)(2,1)}, bf16[384,1152]{1,0:T(8,128)(2,1)S(1)}, u32[]{:S(2)}) copy-start(bf16[384,1152]{1,0:T(8,128)(2,1)S(1)} %get-tuple-element.284) | copy-start | bytes 2654212
  218.4 27.5 %collective-permute-start.10 = (bf16[2,2,2,24,1152]{4,3,2,1,0:T(8,128)(2,1)S(1)}, bf16[2,2,2,24,1152]{4,3,2,1,0:T(8,128)(2,1)S(1)}, u32[]{:S(2)}, u32[]{:S(2)}) collective-permute-start(bf16[2,2,2,24,1152]{4,3,2,1,0:T(8,128)(2,1)S(1)} %fusion.1), channel_id=1, source_target_pairs={{0,16},{4,20},{8,24},{12,28},{16,0},{20,4},{24,8},{28,12},{1,17},{... | collective-permute-start | bytes 1327112 | tf_op jit(solution)/shard_map/ppermute | solution.py:1307
  220.0 26.7 %collective-permute-start.9 = (bf16[2,2,2,24,1152]{4,3,2,1,0:T(8,128)(2,1)S(1)}, bf16[2,2,2,24,1152]{4,3,2,1,0:T(8,128)(2,1)}, u32[]{:S(2)}, u32[]{:S(2)}) collective-permute-start(bf16[2,2,2,24,1152]{4,3,2,1,0:T(8,128)(2,1)S(1)} %fusion), channel_id=1, source_target_pairs={{0,8},{4,12},{8,0},{12,4},{16,24},{20,28},{24,16},{28,20},{1,9},{5... | collective-permute-start | bytes 1327112 | tf_op jit(solution)/shard_map/ppermute | solution.py:1307
  251.8 19.2 %collective-permute-start.11 = (bf16[2,2,24,1152]{3,2,1,0:T(8,128)(2,1)}, bf16[2,2,24,1152]{3,2,1,0:T(8,128)(2,1)}, u32[]{:S(2)}, u32[]{:S(2)}) collective-permute-start(bf16[2,2,24,1152]{3,2,1,0:T(8,128)(2,1)} %get-tuple-element.193), channel_id=1, source_target_pairs={{0,16},{4,20},{8,24},{12,28},{16,0},{20,4},{24,8},{28,12},{1,17},{... | collective-permute-start | bytes 663560 | tf_op jit(solution)/shard_map/ppermute | solution.py:1307
  253.2 17.9 %collective-permute-start.12 = (bf16[2,2,24,1152]{3,2,1,0:T(8,128)(2,1)}, bf16[2,2,24,1152]{3,2,1,0:T(8,128)(2,1)}, u32[]{:S(2)}, u32[]{:S(2)}) collective-permute-start(bf16[2,2,24,1152]{3,2,1,0:T(8,128)(2,1)} %get-tuple-element.194), channel_id=1, source_target_pairs={{0,8},{4,12},{8,0},{12,4},{16,24},{20,28},{24,16},{28,20},{1,9},{5... | collective-permute-start | bytes 663560 | tf_op jit(solution)/shard_map/ppermute | solution.py:1307
  271.0 2.2 collective-permute-start.16
  273.3 9.4 %collective-permute-start.17 = (bf16[96,256]{1,0:T(8,128)(2,1)S(1)}, bf16[96,256]{1,0:T(8,128)(2,1)S(1)}, u32[]{:S(2)}, u32[]{:S(2)}) collective-permute-start(bf16[96,256]{1,0:T(8,128)(2,1)S(1)} %add_convert_fusion.5), channel_id=1, source_target_pairs={{0,8},{4,12},{8,0},{12,4},{16,24},{20,28},{24,16},{28,20},{1,9},{5... | collective-permute-start | bytes 147464 | tf_op jit(solution)/shard_map/ppermute | solution.py:1277
  274.7 8.0 %collective-permute-start.18 = (bf16[96,256]{1,0:T(8,128)(2,1)S(1)}, bf16[96,256]{1,0:T(8,128)(2,1)S(1)}, u32[]{:S(2)}, u32[]{:S(2)}) collective-permute-start(bf16[96,256]{1,0:T(8,128)(2,1)S(1)} %add_convert_fusion.5), channel_id=1, source_target_pairs={{0,16},{4,20},{8,24},{12,28},{16,0},{20,4},{24,8},{28,12},{1,17},{... | collective-permute-start | bytes 147464 | tf_op jit(solution)/shard_map/ppermute | solution.py:1277
  275.3 7.3 %collective-permute-start.19 = (bf16[96,256]{1,0:T(8,128)(2,1)S(1)}, bf16[96,256]{1,0:T(8,128)(2,1)S(1)}, u32[]{:S(2)}, u32[]{:S(2)}) collective-permute-start(bf16[96,256]{1,0:T(8,128)(2,1)S(1)} %add_convert_fusion.5), channel_id=1, source_target_pairs={{0,24},{4,28},{8,16},{12,20},{16,8},{20,12},{24,0},{28,4},{1,25},{... | collective-permute-start | bytes 147464 | tf_op jit(solution)/shard_map/ppermute | solution.py:1277
  281.2 7.9 %collective-permute-start.20 = (bf16[2,24,2304]{2,1,0:T(8,128)(2,1)S(1)}, bf16[2,24,2304]{2,1,0:T(8,128)(2,1)S(1)}, u32[]{:S(2)}, u32[]{:S(2)}) collective-permute-start(bf16[2,24,2304]{2,1,0:T(8,128)(2,1)S(1)} %fusion.4), channel_id=1, source_target_pairs={{0,1},{1,0},{2,3},{3,2},{4,5},{5,4},{6,7},{7,6},{8,9},{9,8},{10,11... | collective-permute-start | bytes 663560 | tf_op jit(solution)/shard_map/ppermute | solution.py:1307
  289.0 6.1 %collective-permute-start.21 = (bf16[96,256]{1,0:T(8,128)(2,1)S(1)}, bf16[96,256]{1,0:T(8,128)(2,1)S(1)}, u32[]{:S(2)}, u32[]{:S(2)}) collective-permute-start(bf16[96,256]{1,0:T(8,128)(2,1)S(1)} %add_convert_fusion.4), channel_id=1, source_target_pairs={{0,1},{1,0},{2,3},{3,2},{4,5},{5,4},{6,7},{7,6},{8,9},{9,8},{10,11... | collective-permute-start | bytes 147464 | tf_op jit(solution)/shard_map/ppermute | solution.py:1277
  289.6 5.5 %collective-permute-start.22 = (bf16[96,256]{1,0:T(8,128)(2,1)S(1)}, bf16[96,256]{1,0:T(8,128)(2,1)S(1)}, u32[]{:S(2)}, u32[]{:S(2)}) collective-permute-start(bf16[96,256]{1,0:T(8,128)(2,1)S(1)} %add_convert_fusion.4), channel_id=1, source_target_pairs={{0,2},{1,3},{2,0},{3,1},{4,6},{5,7},{6,4},{7,5},{8,10},{9,11},{10,... | collective-permute-start | bytes 147464 | tf_op jit(solution)/shard_map/ppermute | solution.py:1277
  292.0 5.9 %collective-permute-start.23 = (bf16[96,256]{1,0:T(8,128)(2,1)S(1)}, bf16[96,256]{1,0:T(8,128)(2,1)S(1)}, u32[]{:S(2)}, u32[]{:S(2)}) collective-permute-start(bf16[96,256]{1,0:T(8,128)(2,1)S(1)} %add_convert_fusion.4), channel_id=1, source_target_pairs={{0,3},{1,2},{2,1},{3,0},{4,7},{5,6},{6,5},{7,4},{8,11},{9,10},{10,... | collective-permute-start | bytes 147464 | tf_op jit(solution)/shard_map/ppermute | solution.py:1277
  297.9 2.6 collective-permute-start.24
  300.5 7.4 %collective-permute-start.25 = (bf16[24,2304]{1,0:T(8,128)(2,1)S(1)}, bf16[24,2304]{1,0:T(8,128)(2,1)S(1)}, u32[]{:S(2)}, u32[]{:S(2)}) collective-permute-start(bf16[24,2304]{1,0:T(8,128)(2,1)S(1)} %fusion.8), channel_id=1, source_target_pairs={{0,2},{1,3},{2,0},{3,1},{4,6},{5,7},{6,4},{7,5},{8,10},{9,11},{10,... | collective-permute-start | bytes 331784 | tf_op jit(solution)/shard_map/ppermute | solution.py:1307
  (58 other events, 744.3 us)
Sparse Core Ops, SparseCore 0:
  164.1 85.3 reduce-scatter.2
  254.0 31.6 reduce-scatter.4
